TPU v7x, 512 devices: a whole 4x4x16 slice. The times are simulated.
512 devices in a mesh: prow: 32 (over z, core), pcol: 16 (over x, y).
Axes of the slice: x: 4, y: 4, z: 16, core: 2. Of those that a mesh axis runs over, the one named last changes fastest.
Arguments:
- eigen_in: float32 [1536, 155648], P('pcol', 'prow'), may hold values from -6 to 6
- house_vecs: float32 [4, 128, 155648], P(None, 'pcol', 'prow'), may hold values from -6 to 6
- wy_factor: float32 [4, 128, 128], P(None, 'pcol'), as said below
Outputs:
- eigen_out: float32 [1536, 155648], P('pcol', 'prow')
Inputs may be any that keep to these rules, and one draw needn't show every extreme that they name: `wy_factor`: each block's matrix is upper triangular.
All inputs are finite; a program needn't handle non-finite values.
Results may differ from a plain program's by a relative error of at most 0.00014.
Values sent between devices are 32-bit elements; how exact they have to be, the bound alone decides.
No kernel may reach another device: no remote copies, remote signals or barrier semaphores. Data moves between devices by JAX's collectives and lax.ppermute only.
A program may use at most 64 MiB of HBM per device.

v0:
```python
import jax
import jax.numpy as jnp
from jax import lax
from jax.sharding import PartitionSpec as P


def inner_rows(left, right):
    return lax.dot_general(
        left,
        right,
        (((1,), (1,)), ((), ())),
        precision=lax.Precision.HIGHEST,
        preferred_element_type=jnp.float32,
    )


def plain_product(left, right):
    return jnp.dot(left, right, precision=lax.Precision.HIGHEST, preferred_element_type=jnp.float32)


def scale_blocks(summed, factors):
    first = inner_rows(summed[0], factors[0])
    return first[None]


def reduce_scale(partial_sums, factors):
    summed = lax.psum(partial_sums, "prow")
    return scale_blocks(summed, factors)


def per_device(eigen_in, house_vecs, wy_factor):
    current = eigen_in
    nblk = house_vecs.shape[0]
    for block in range(nblk):
        vectors, factor = (
            lax.all_gather(house_vecs[block], "pcol", axis=0, tiled=True),
            lax.all_gather(wy_factor[block], "pcol", axis=0, tiled=True),
        )
        partial_sums = inner_rows(current, vectors)[None]
        scaled = reduce_scale(partial_sums, (factor,))
        current = current - plain_product(scaled[0], vectors)
    return current


def solution(mesh):
    placed = (P("pcol", "prow"), P(None, "pcol", "prow"), P(None, "pcol", None))
    return jax.shard_map(
        per_device, mesh=mesh, in_specs=placed, out_specs=P("pcol", "prow"), check_vma=False
    )
```

profile of v0, /device:TPU:1, one launch (start us, length us, event | category | flops | bytes accessed | tf_op | source)
XLA Modules:
  0.0 512.0 jit_solution(17086369404785405600)
XLA Ops:
  6.5 0.0 copy-start.3
  6.5 0.0 copy-start.2
  6.5 0.0 all-gather.13.cloned.1.call-start
  6.5 2.1 fusion.20
  8.7 0.0 all-gather.13.cloned.1.call-update
  8.7 0.0 all-gather.15.cloned.1.call-start
  8.7 0.7 all-gather.15.cloned.1.call-update
  9.4 0.0 all-gather.17.cloned.1.call-start
  9.5 0.7 all-gather.17.cloned.1.call-update
  10.2 0.0 all-gather.19.cloned.1.call-start
  10.2 0.5 all-gather.19.cloned.1.call-update
  10.7 0.0 copy-done.3
  10.8 19.3 %all-gather.1 = f32[1,128,128]{2,1,0:T(8,128)S(1)} all-gather(f32[1,8,128]{2,1,0:T(8,128)S(1)} %get-tuple-element.11), channel_id=3, replica_groups=mesh['prow'=32,'pcol'=16] {'pcol'}, dimensions={1}, use_global_device_ids=true | all-gather | bytes 69632 | tf_op jit(solution)/shard_map/all_gather | solution.py:37
  30.0 18.1 %all-gather.3 = f32[1,128,128]{2,1,0:T(8,128)S(1)} all-gather(f32[1,8,128]{2,1,0:T(8,128)S(1)} %get-tuple-element.10), channel_id=5, replica_groups=mesh['prow'=32,'pcol'=16] {'pcol'}, dimensions={1}, use_global_device_ids=true | all-gather | bytes 69632 | tf_op jit(solution)/shard_map/all_gather | solution.py:37
  48.1 15.8 %all-gather.5 = f32[1,128,128]{2,1,0:T(8,128)S(1)} all-gather(f32[1,8,128]{2,1,0:T(8,128)S(1)} %get-tuple-element.12), channel_id=7, replica_groups=mesh['prow'=32,'pcol'=16] {'pcol'}, dimensions={1}, use_global_device_ids=true | all-gather | bytes 69632 | tf_op jit(solution)/shard_map/all_gather | solution.py:37
  63.9 19.1 %all-gather.7 = f32[1,128,128]{2,1,0:T(8,128)S(1)} all-gather(f32[1,8,128]{2,1,0:T(8,128)S(1)} %get-tuple-element.9), channel_id=9, replica_groups=mesh['prow'=32,'pcol'=16] {'pcol'}, dimensions={1}, use_global_device_ids=true | all-gather | bytes 69632 | tf_op jit(solution)/shard_map/all_gather | solution.py:37
  83.0 0.0 all-gather.13.cloned.1.call-done
  83.0 0.0 copy-done.2
  83.0 4.1 fusion.10
  87.2 115.3 %psum.28 = f32[96,128]{1,0:T(8,128)S(1)} all-reduce(f32[96,128]{1,0:T(8,128)S(1)} %fusion.10), channel_id=1, replica_groups=mesh['prow'=32,'pcol'=16] {'prow'}, use_global_device_ids=true, to_apply=%region_0.0 | all-reduce | flops 12288 | bytes 98304 | tf_op jit(solution)/shard_map/psum | solution.py:27
  202.5 0.2 fusion.18
  202.7 3.9 convolution_subtract_fusion.3
  206.6 0.0 copy-start.1
  206.7 0.0 all-gather.15.cloned.1.call-done
  206.7 4.8 fusion.7
  211.5 0.0 copy-done.1
  211.5 91.0 %psum.29 = f32[96,128]{1,0:T(8,128)S(1)} all-reduce(f32[96,128]{1,0:T(8,128)S(1)} %fusion.7), channel_id=1, replica_groups=mesh['prow'=32,'pcol'=16] {'prow'}, use_global_device_ids=true, to_apply=%region_1.0 | all-reduce | flops 12288 | bytes 98304 | tf_op jit(solution)/shard_map/psum | solution.py:27
  302.5 0.2 fusion.16
  302.8 3.9 convolution_subtract_fusion.2
  306.7 0.0 all-gather.17.cloned.1.call-done
  306.7 4.1 fusion.4
  310.9 90.0 %psum.30 = f32[96,128]{1,0:T(8,128)S(1)} all-reduce(f32[96,128]{1,0:T(8,128)S(1)} %fusion.4), channel_id=1, replica_groups=mesh['prow'=32,'pcol'=16] {'prow'}, use_global_device_ids=true, to_apply=%region_2.0 | all-reduce | flops 12288 | bytes 98304 | tf_op jit(solution)/shard_map/psum | solution.py:27
  400.9 0.2 fusion.14
  401.2 4.6 convolution_subtract_fusion.1
  405.8 0.0 copy-start
  405.8 0.0 all-gather.19.cloned.1.call-done
  405.8 4.8 fusion.1
  410.6 90.0 %psum.31 = f32[96,128]{1,0:T(8,128)S(1)} all-reduce(f32[96,128]{1,0:T(8,128)S(1)} %fusion.1), channel_id=1, replica_groups=mesh['prow'=32,'pcol'=16] {'prow'}, use_global_device_ids=true, to_apply=%region_3.0 | all-reduce | flops 12288 | bytes 98304 | tf_op jit(solution)/shard_map/psum | solution.py:27
  500.6 0.2 fusion.12
  500.9 0.0 copy-done
  500.9 4.6 convolution_subtract_fusion
  (1 shorter events, 0.0 us)
Async XLA Ops:
  6.5 4.2 copy-start.3
  6.5 76.5 %copy-start.2 = (f32[96,4864]{1,0:T(8,128)S(1)}, f32[96,4864]{1,0:T(8,128)}, u32[]{:S(2)}) copy-start(f32[96,4864]{1,0:T(8,128)} %param.3) | copy-start | bytes 5603332
  6.5 76.5 %all-gather.13.cloned.1.call-start = ((), (), s32[]{:S(2)}) async-start(), calls=%async_computation | async-start | bytes 2646016 | tf_op jit(solution)/shard_map/all_gather | solution.py:36
  8.7 198.0 %all-gather.15.cloned.1.call-start = ((), (), s32[]{:S(2)}) async-start(), calls=%async_computation.1 | async-start | bytes 2646016 | tf_op jit(solution)/shard_map/all_gather | solution.py:36
  9.4 297.3 %all-gather.17.cloned.1.call-start = ((), (), s32[]{:S(2)}) async-start(), calls=%async_computation.2 | async-start | bytes 2646016 | tf_op jit(solution)/shard_map/all_gather | solution.py:36
  10.2 395.6 %all-gather.19.cloned.1.call-start = ((), (), s32[]{:S(2)}) async-start(), calls=%async_computation.3 | async-start | bytes 2646016 | tf_op jit(solution)/shard_map/all_gather | solution.py:36
  206.6 4.8 copy-start.1
  405.8 95.1 %copy-start = (f32[96,4864]{1,0:T(8,128)S(1)}, f32[96,4864]{1,0:T(8,128)}, u32[]{:S(2)}) copy-start(f32[96,4864]{1,0:T(8,128)} %convolution_subtract_fusion.1) | copy-start | bytes 5603332
Sparse Core Ops, SparseCore 0:
  10.4 66.0 all-gather.12
  79.5 60.8 all-gather.14
  143.5 60.7 all-gather.16
  207.1 60.7 all-gather.18
where the time goes:
time: 513 us; the launch traced here: 512 us
  blocking collectives  459 us (89%)
  matrix products  35.9 us (7%)
  between operations  13.2 us (3%)
    psum x4, blocking collectives, reduce_scale(): summed = lax.psum(partial_sums, 'prow')  386 us
    all_gather x4, blocking collectives, per_device(): lax.all_gather(wy_factor[block], 'pcol', axis=0, tiled=True)  72.2 us
    dot_general x8, matrix products, inner_rows(): lax.dot_general(left, right, (((1,), (1,)), ((), ())), precision=lax.Prec...  18.9 us
    dot_general x4, matrix products, plain_product(): jnp.dot(left, right, precision=lax.Precision.HIGHEST, preferred_element_t...  17 us
  transfers between devices with their start and end apart: 4, of which 0 were waited for; matrix products, arithmetic and copies ran while one was open for 5% of the time, Pallas kernels for 0%

commit v1 on v0

v1 whole, which is shorter than its diff:
```python
import jax
import jax.numpy as jnp
from jax import lax
from jax.experimental import pallas as pl
from jax.experimental.pallas import tpu as pltpu
from jax.sharding import PartitionSpec as P

F32 = jnp.float32
BF16 = jnp.bfloat16
NT = (((1,), (1,)), ((), ()))
NN = (((1,), (0,)), ((), ()))


def split(x):
    high = x.astype(BF16)
    low = (x - high.astype(F32)).astype(BF16)
    return high, low


def product(left, right, dims):
    rows = left[0].shape[0]
    both = lax.dot_general(
        jnp.concatenate(left, axis=0), right[0], dims, preferred_element_type=F32
    )
    cross = lax.dot_general(left[0], right[1], dims, preferred_element_type=F32)
    return both[:rows] + (both[rows:] + cross)


def exact(left, right, dims):
    return lax.dot_general(
        left, right, dims, precision=lax.Precision.HIGHEST, preferred_element_type=F32
    )


def pair_list(nblk):
    return [(b, c) for b in range(nblk) for c in range(b + 1, nblk)]


def inner_kernel(half, core_ref, eig_ref, vec_ref, keep_ref, give_ref, high, low, total):
    rows = eig_ref.shape[0]
    owners, nblk, share, width = vec_ref.shape
    kb = owners * share
    step = pl.program_id(0)

    @pl.when(step == 0)
    def _():
        total[...] = jnp.zeros_like(total)

    high[:rows], low[:rows] = split(eig_ref[...])
    for b in range(nblk):
        at = rows + b * kb
        high[at : at + kb], low[at : at + kb] = split(vec_ref[:, b].reshape(kb, width))

    first_pair = nblk * rows
    pairs = pair_list(nblk)
    for c0 in range(0, nblk, 2):
        c1 = min(c0 + 2, nblk)
        top = rows + (c1 - 1) * kb
        cols = slice(rows + c0 * kb, rows + c1 * kb)
        out = product((high[:top], low[:top]), (high[cols], low[cols]), NT)
        for c in range(c0, c1):
            lane = slice((c - c0) * kb, (c - c0 + 1) * kb)
            total[c * rows : (c + 1) * rows] += out[:rows, lane]
            for b in range(c):
                at = first_pair + pairs.index((b, c)) * kb
                total[at : at + kb] += out[rows + b * kb : rows + (b + 1) * kb, lane]

    @pl.when(step == pl.num_programs(0) - 1)
    def _():
        core = core_ref[0]
        keep_ref[...] = total[pl.ds(pl.multiple_of(core * half, 8), half)]
        give_ref[...] = total[pl.ds(pl.multiple_of((1 - core) * half, 8), half)]


def inner_sums(core, eig, vecs, half):
    rows, cols = eig.shape
    owners, nblk, share, _ = vecs.shape
    kb = owners * share
    width = cols // 2
    depth = rows + nblk * kb
    return pl.pallas_call(
        lambda *refs: inner_kernel(half, *refs),
        out_shape=[jax.ShapeDtypeStruct((half, kb), F32)] * 2,
        grid_spec=pltpu.PrefetchScalarGridSpec(
            num_scalar_prefetch=1,
            grid=(2,),
            in_specs=[
                pl.BlockSpec((rows, width), lambda t, _: (0, t)),
                pl.BlockSpec((owners, nblk, share, width), lambda t, _: (0, 0, 0, t)),
            ],
            out_specs=[pl.BlockSpec((half, kb), lambda t, _: (0, 0))] * 2,
            scratch_shapes=[
                pltpu.VMEM((depth, width), BF16),
                pltpu.VMEM((depth, width), BF16),
                pltpu.VMEM((2 * half, kb), F32),
            ],
        ),
        compiler_params=pltpu.CompilerParams(vmem_limit_bytes=48 * 2**20),
        name="inner_sums",
    )(core, eig, vecs)


def update_kernel(sum_ref, fac_ref, eig_ref, vec_ref, out_ref, high, low):
    rows, width = eig_ref.shape
    owners, nblk, share, _ = vec_ref.shape
    kb = owners * share
    first_pair = nblk * rows
    pairs = pair_list(nblk)

    @pl.when(pl.program_id(0) == 0)
    def _():
        scaled = []
        for c in range(nblk):
            proj = sum_ref[c * rows : (c + 1) * rows]
            for b in range(c):
                at = first_pair + pairs.index((b, c)) * kb
                proj = proj - exact(scaled[b], sum_ref[at : at + kb], NN)
            scaled.append(exact(proj, fac_ref[:, c].reshape(kb, kb), NT))
            lane = slice(c * kb, (c + 1) * kb)
            high[:, lane], low[:, lane] = split(scaled[c])

    left = (high[...], low[...])
    for at in range(0, width, 256):
        lane = slice(at, min(at + 256, width))
        vecs = jnp.concatenate(
            [vec_ref[:, b, :, lane].reshape(kb, lane.stop - at) for b in range(nblk)], axis=0
        )
        out_ref[:, lane] = eig_ref[:, lane] - product(left, split(vecs), NN)


def update(sums, factors, eig, vecs):
    rows, cols = eig.shape
    owners, nblk, share, _ = vecs.shape
    kb = owners * share
    width = cols // 2
    return pl.pallas_call(
        update_kernel,
        out_shape=jax.ShapeDtypeStruct(eig.shape, F32),
        grid=(2,),
        in_specs=[
            pl.BlockSpec(sums.shape, lambda t: (0, 0)),
            pl.BlockSpec(factors.shape, lambda t: (0, 0, 0, 0)),
            pl.BlockSpec((rows, width), lambda t: (0, t)),
            pl.BlockSpec((owners, nblk, share, width), lambda t: (0, 0, 0, t)),
        ],
        out_specs=pl.BlockSpec((rows, width), lambda t: (0, t)),
        scratch_shapes=[pltpu.VMEM((rows, nblk * kb), BF16)] * 2,
        compiler_params=pltpu.CompilerParams(vmem_limit_bytes=48 * 2**20),
        name="update",
    )(sums, factors, eig, vecs)


def sum_over_rows(keep, give, nprow):
    half, kb = keep.shape
    nz = nprow // 2
    along_z = [list(range(core, nprow, 2)) for core in range(2)]
    in_chip = [[2 * z, 2 * z + 1] for z in range(nz)]
    mine = keep + lax.ppermute(give, "prow", [(i, i ^ 1) for i in range(nprow)])
    parts = lax.all_to_all(
        mine.reshape(nz, half // nz, kb), "prow", 0, 0, axis_index_groups=along_z
    )
    part = jnp.sum(parts, axis=0)
    whole = lax.all_to_all(
        jnp.broadcast_to(part, (nz,) + part.shape), "prow", 0, 0, axis_index_groups=along_z
    )
    return lax.all_gather(
        whole.reshape(half, kb), "prow", axis=0, tiled=True, axis_index_groups=in_chip
    )


def solution(mesh):
    placed = (P("pcol", "prow"), P(None, "pcol", "prow"), P(None, "pcol", None))
    nprow = mesh.shape["prow"]

    def per_device(eig, house_vecs, wy_factor):
        nblk, _, kb = wy_factor.shape
        vecs = lax.all_gather(house_vecs, "pcol", axis=0)
        factors = lax.all_gather(wy_factor, "pcol", axis=0)
        filled = nblk * eig.shape[0] + len(pair_list(nblk)) * kb
        half = -(-filled // (8 * nprow)) * 8 * nprow // 2
        core = lax.rem(lax.axis_index("prow"), 2).astype(jnp.int32).reshape(1)
        keep, give = inner_sums(core, eig, vecs, half)
        sums = sum_over_rows(keep, give, nprow)
        return update(sums, factors, eig, vecs)

    return jax.shard_map(
        per_device, mesh=mesh, in_specs=placed, out_specs=P("pcol", "prow"), check_vma=False
    )
```

time: 513 us -> 204 us (0.40)
  blocking collectives: 459 us -> 53.6 us
  waiting for transfers between devices: 1.96 us -> 104 us
  matrix products: 35.9 us -> 0 us
  Pallas kernels: 0 us -> 16.2 us
  starting transfers between devices: 0.12 us -> 14.2 us
    psum x4 -> x0, blocking collectives: 386 us -> none  [reduce_scale(): summed = lax.psum(partial_sums, 'prow')]
    all_gather x4 -> x1, waiting for transfers between devices: 0.05 us -> 102 us  [per_device(): vecs = lax.all_gather(house_vecs, 'pcol', axis=0)]
    all_gather x4 -> x2, blocking collectives: 72.2 us -> 26.2 us  [the longest x1 19 us: per_device(): factors = lax.all_gather(wy_factor, 'pcol', axis=0)]
    dot_general x12 -> x0, matrix products: 35.9 us -> none  [the longest x8 18.9 us: inner_rows(): lax.dot_general(left, right, (((1,), (1,)), ((), ())), precision=lax.Prec...]
    all_to_all x0 -> x1, blocking collectives: none -> 27.4 us  [sum_over_rows(): lax.all_to_all(mine.reshape(nz, half // nz, kb), 'prow', 0, 0, axis_index...]
    pallas_call x0 -> x2, Pallas kernels: none -> 16.2 us  [the longest x1 8.79 us: inner_sums(): pl.pallas_call(lambda *refs: inner_kernel(half, *refs), out_shape=[jax.Sh...]
    all_to_all x0 -> x1, starting transfers between devices: none -> 11.6 us  [sum_over_rows(): lax.all_to_all(jnp.broadcast_to(part, (nz,) + part.shape), 'prow', 0, 0,...]
  transfers between devices with their start and end apart: 4 -> 3, of which waited for: 0 -> 2; matrix products, arithmetic and copies ran while one was open for 5% -> 0% of each run, Pallas kernels for 0% -> 0%
where the time goes in v1:
time: 204 us; the launch traced here: 203 us
  waiting for transfers between devices  104 us (51%)
  blocking collectives  53.6 us (26%)
  Pallas kernels  16.2 us (8%)
  starting transfers between devices  14.2 us (7%)
  between operations  13.5 us (7%)
  local copies, waits for them, and re-layouts  2.27 us (1%)
    all_gather x1, waiting for transfers between devices, per_device(): vecs = lax.all_gather(house_vecs, 'pcol', axis=0)  102 us
    all_to_all x1, blocking collectives, sum_over_rows(): lax.all_to_all(mine.reshape(nz, half // nz, kb), 'prow', 0, 0, axis_index...  27.4 us
    all_gather x1, blocking collectives, per_device(): factors = lax.all_gather(wy_factor, 'pcol', axis=0)  19 us
    all_to_all x1, starting transfers between devices, sum_over_rows(): lax.all_to_all(jnp.broadcast_to(part, (nz,) + part.shape), 'prow', 0, 0,...  11.6 us
    pallas_call x1, Pallas kernels, inner_sums(): pl.pallas_call(lambda *refs: inner_kernel(half, *refs), out_shape=[jax.Sh...  8.79 us
    pallas_call x1, Pallas kernels, update(): pl.pallas_call(update_kernel, out_shape=jax.ShapeDtypeStruct(eig.shape, F...  7.38 us
    all_gather x1, blocking collectives, sum_over_rows(): lax.all_gather(whole.reshape(half, kb), 'prow', axis=0, tiled=True, axis_...  7.17 us
  transfers between devices with their start and end apart: 3, of which 2 were waited for; matrix products, arithmetic and copies ran while one was open for 0% of the time, Pallas kernels for 0%

profile of v1, /device:TPU:1, one launch (start us, length us, event | category | flops | bytes accessed | tf_op | source)
XLA Modules:
  0.0 203.4 jit_solution(3706453483518823978)
XLA Ops:
  6.5 0.0 all-gather.4.cloned.1.call-start
  6.5 0.7 all-gather.4.cloned.1.call-update
  7.3 101.8 %all-gather.4.cloned.1.call-done = f32[64,8,4864]{2,1,0:T(8,128)} async-done(((f32[4,8,4864]{2,1,0:T(8,128)}), f32[64,8,4864]{2,1,0:T(8,128)}) %all-gather.4.cloned.1.call-update) | async-done | bytes 9961488 | tf_op jit(solution)/shard_map/all_gather | solution.py:177
  109.1 0.0 copy-start
  109.1 1.5 copy-done
  110.6 8.8 %inner_sums.1 = (f32[640,128]{1,0:T(8,128)S(1)}, f32[640,128]{1,0:T(8,128)S(1)}) custom-call(s32[1]{0:T(128)} %bitcast.refs_0_, f32[96,4864]{1,0:T(8,128)S(1)} %copy-done, f32[16,4,8,4864]{3,2,1,0:T(8,128)} %bitcast.6), custom_call_target="tpu_custom_call" | custom-call | tf_op jit(solution)/shard_map/inner_sums/pallas_call | solution.py:81
  119.4 0.0 copy-start.2
  119.4 2.6 %collective-permute-start = (f32[640,128]{1,0:T(8,128)S(1)}, f32[640,128]{1,0:T(8,128)S(1)}, u32[]{:S(2)}, u32[]{:S(2)}) collective-permute-start(f32[640,128]{1,0:T(8,128)S(1)} %get-tuple-element.8), channel_id=1, source_target_pairs={{0,16},{16,0},{32,48},{48,32},{64,80},{80,64},{96,112},{112,96},{1... | collective-permute-start | bytes 983048 | tf_op jit(solution)/shard_map/ppermute | solution.py:158
  122.0 1.2 collective-permute-done
  123.3 0.0 copy-start.1
  123.3 27.4 %all_to_all.10 = f32[16,40,128]{2,1,0:T(8,128)S(1)} all-to-all(f32[16,40,128]{2,1,0:T(8,128)S(1)} %bitcast.9), channel_id=1, replica_groups={{0,32,64,96,128,160,192,224,256,288,320,352,384,416,448,480},{16,48,80,..., dimensions={0} | all-to-all | bytes 655360 | tf_op jit(solution)/shard_map/all_to_all | solution.py:159
  150.7 0.7 broadcast_in_dim.3
  151.4 11.6 %all-to-all-start.1 = ((f32[16,40,128]{2,1,0:T(8,128)}), f32[16,40,128]{2,1,0:T(8,128)S(1)}, u32[]{:S(2)}, u32[]{:S(2)}) async-start(f32[16,40,128]{2,1,0:T(8,128)} %broadcast_in_dim.3), calls=%async_computation.1 | async-start | bytes 655360 | tf_op jit(solution)/shard_map/all_to_all | solution.py:163
  163.0 0.0 copy-done.2
  163.0 19.0 %all-gather.1 = f32[64,8,128]{2,1,0:T(8,128)S(1)} all-gather(f32[4,8,128]{2,1,0:T(8,128)S(1)} %copy-done.2), channel_id=3, replica_groups=mesh['prow'=32,'pcol'=16] {'pcol'}, dimensions={0}, use_global_device_ids=true | all-gather | bytes 278528 | tf_op jit(solution)/shard_map/all_gather | solution.py:178
  182.0 0.0 all-to-all-done.1
  182.0 7.2 %all_gather.17.sum_ref = f32[1280,128]{1,0:T(8,128)S(1)} all-gather(f32[640,128]{1,0:T(8,128)S(1)} %bitcast.8), channel_id=1, replica_groups={{0,16},{32,48},{64,80},{96,112},{128,144},{160,176},{192,208},{224,240}..., dimensions={0}, use_global_device_ids=true | all-gather | bytes 983040 | tf_op jit(solution)/shard_map/all_gather | solution.py:166
  189.2 0.0 copy-done.1
  189.2 7.4 %update.1 = f32[96,4864]{1,0:T(8,128)} custom-call(f32[1280,128]{1,0:T(8,128)S(1)} %all_gather.17.sum_ref, f32[16,4,8,128]{3,2,1,0:T(8,128)S(1)} %bitcast.5, f32[96,4864]{1,0:T(8,128)S(1)} %copy-done.1, f32[16,4,8,4864]{3,2,1,0:T(8,128)} %bitcast.7), custom_call_target="tpu_custom_call" | custom-call | tf_op jit(solution)/shard_map/update/pallas_call | solution.py:136
  (2 shorter events, 0.1 us)
Async XLA Ops:
  6.5 102.5 %all-gather.4.cloned.1.call-start = ((), (), s32[]{:S(2)}) async-start(), calls=%async_computation.2 | async-start | bytes 10584064 | tf_op jit(solution)/shard_map/all_gather | solution.py:177
  109.1 1.5 copy-start
  119.4 43.6 %copy-start.2 = (f32[4,8,128]{2,1,0:T(8,128)S(1)}, f32[4,8,128]{2,1,0:T(8,128)}, u32[]{:S(2)}) copy-start(f32[4,8,128]{2,1,0:T(8,128)} %param.5) | copy-start | bytes 49156
  119.4 3.8 %collective-permute-start = (f32[640,128]{1,0:T(8,128)S(1)}, f32[640,128]{1,0:T(8,128)S(1)}, u32[]{:S(2)}, u32[]{:S(2)}) collective-permute-start(f32[640,128]{1,0:T(8,128)S(1)} %get-tuple-element.8), channel_id=1, source_target_pairs={{0,16},{16,0},{32,48},{48,32},{64,80},{80,64},{96,112},{112,96},{1... | collective-permute-start | bytes 983048 | tf_op jit(solution)/shard_map/ppermute | solution.py:158
  123.3 65.9 %copy-start.1 = (f32[96,4864]{1,0:T(8,128)S(1)}, f32[96,4864]{1,0:T(8,128)}, u32[]{:S(2)}) copy-start(f32[96,4864]{1,0:T(8,128)} %eig_ref.1) | copy-start | bytes 5603332
  151.4 30.6 %all-to-all-start.1 = ((f32[16,40,128]{2,1,0:T(8,128)}), f32[16,40,128]{2,1,0:T(8,128)S(1)}, u32[]{:S(2)}, u32[]{:S(2)}) async-start(f32[16,40,128]{2,1,0:T(8,128)} %broadcast_in_dim.3), calls=%async_computation.1 | async-start | bytes 655360 | tf_op jit(solution)/shard_map/all_to_all | solution.py:163
Sparse Core Ops, SparseCore 0:
  10.4 98.6 all-gather.3

commit v2 on v1

v2 whole, which is shorter than its diff:
```python
import jax
import jax.numpy as jnp
import numpy as np
from jax import lax
from jax.experimental import pallas as pl
from jax.experimental.pallas import tpu as pltpu
from jax.sharding import PartitionSpec as P

F32 = jnp.float32
BF16 = jnp.bfloat16
NT = (((1,), (1,)), ((), ()))
NN = (((1,), (0,)), ((), ()))
VMEM_LIMIT = 52 * 2**20
X_NEAR, X_WRAP, Y_NEAR, Y_WRAP = 4, 12, 1, 3
ROUTES = (
    ((X_NEAR, X_WRAP, Y_NEAR, Y_WRAP), (Y_NEAR, Y_WRAP, X_NEAR, X_WRAP)),
    ((X_WRAP, X_NEAR, Y_WRAP, Y_NEAR), (Y_WRAP, Y_NEAR, X_WRAP, X_NEAR)),
)


def split(x):
    high = x.astype(BF16)
    low = (x - high.astype(F32)).astype(BF16)
    return high, low


def product(left, right, dims):
    rows = left[0].shape[0]
    both = lax.dot_general(
        jnp.concatenate(left, axis=0), right[0], dims, preferred_element_type=F32
    )
    cross = lax.dot_general(left[0], right[1], dims, preferred_element_type=F32)
    return both[:rows] + (both[rows:] + cross)


def exact(left, right, dims):
    return lax.dot_general(
        left, right, dims, precision=lax.Precision.HIGHEST, preferred_element_type=F32
    )


def pair_list(nblk):
    return [(b, c) for b in range(nblk) for c in range(b + 1, nblk)]


def chunks_of(width):
    first = -(-width // 512) * 256
    return [(0, first), (first, width - first)]


def arrival_order(route):
    order = [0]
    for mask in route:
        order = order + [mask ^ at for at in order]
    return order


def gather_copies(order_ref, part, bufs, into, lane, sems):
    copies = []
    for k, buf in enumerate(bufs):
        for i in range(buf.shape[0]):
            slot = k * buf.shape[0] + i
            owner = order_ref[part, slot]
            copies.append(
                pltpu.make_async_copy(
                    buf.at[i, :, :, lane], into.at[owner, :, :, lane], sems.at[slot]
                )
            )
    return copies


def inner_kernel(part, half, order_ref, core_ref, *refs):
    last = part == 1
    eig_ref, bufs, refs = refs[0], refs[1:5], refs[5:]
    if last:
        before_ref, refs = refs[0], refs[1:]
    outs, refs = refs[: 1 + last], refs[1 + last :]
    vecs, eig, high, low, total, sems, eig_sems = refs
    rows = eig.shape[0]
    owners, nblk, share, _ = vecs.shape
    kb = owners * share
    width = eig.shape[1]
    start = eig_ref.shape[1] - width if last else 0
    pieces = chunks_of(width)

    copies = []
    for n, (at, size) in enumerate(pieces):
        lane = pl.ds(at, size)
        copies.append(
            gather_copies(order_ref, part, bufs, vecs, lane, sems.at[n])
            + [
                pltpu.make_async_copy(
                    eig_ref.at[:, pl.ds(start + at, size)], eig.at[:, lane], eig_sems.at[n]
                )
            ]
        )
        for copy in copies[n]:
            copy.start()
    total[...] = before_ref[...] if last else jnp.zeros_like(total)

    first_pair = nblk * rows
    pairs = pair_list(nblk)
    for n, (at, size) in enumerate(pieces):
        for copy in copies[n]:
            copy.wait()
        lane = slice(at, at + size)
        high[:rows, lane], low[:rows, lane] = split(eig[:, lane])
        for b in range(nblk):
            here = slice(rows + b * kb, rows + (b + 1) * kb)
            high[here, lane], low[here, lane] = split(vecs[:, b, :, lane].reshape(kb, size))
        for c0 in range(0, nblk, 2):
            c1 = min(c0 + 2, nblk)
            top = rows + (c1 - 1) * kb
            cols = slice(rows + c0 * kb, rows + c1 * kb)
            out = product(
                (high[:top, lane], low[:top, lane]), (high[cols, lane], low[cols, lane]), NT
            )
            for c in range(c0, c1):
                here = slice((c - c0) * kb, (c - c0 + 1) * kb)
                total[c * rows : (c + 1) * rows] += out[:rows, here]
                for b in range(c):
                    to = first_pair + pairs.index((b, c)) * kb
                    total[to : to + kb] += out[rows + b * kb : rows + (b + 1) * kb, here]

    if last:
        core = core_ref[0]
        outs[0][...] = total[pl.ds(pl.multiple_of(core * half, 8), half)]
        outs[1][...] = total[pl.ds(pl.multiple_of((1 - core) * half, 8), half)]
    else:
        outs[0][...] = total[...]


def inner_sums(part, half, order, core, eig, bufs, width, before=None):
    rows, cols = eig.shape
    _, nblk, share, buf_width = bufs[0].shape
    owners = sum(buf.shape[0] for buf in bufs)
    kb = owners * share
    depth = rows + nblk * kb
    last = part == 1
    vmem = pl.BlockSpec(memory_space=pltpu.VMEM)
    smem = pl.BlockSpec(memory_space=pltpu.SMEM)
    hbm = pl.BlockSpec(memory_space=pl.ANY)
    if last:
        outs = [jax.ShapeDtypeStruct((half, kb), F32)] * 2
    else:
        outs = [jax.ShapeDtypeStruct((2 * half, kb), F32)]
    products = width * kb * (nblk * rows + len(pair_list(nblk)) * kb)
    return pl.pallas_call(
        lambda *refs: inner_kernel(part, half, *refs),
        out_shape=outs,
        in_specs=[smem, smem] + [hbm] * 5 + [vmem] * last,
        out_specs=[vmem] * len(outs),
        scratch_shapes=[
            pltpu.VMEM((owners, nblk, share, width), F32),
            pltpu.VMEM((rows, width), F32),
            pltpu.VMEM((depth, width), BF16),
            pltpu.VMEM((depth, width), BF16),
            pltpu.VMEM((2 * half, kb), F32),
            pltpu.SemaphoreType.DMA((2, owners)),
            pltpu.SemaphoreType.DMA((2,)),
        ],
        compiler_params=pltpu.CompilerParams(vmem_limit_bytes=VMEM_LIMIT),
        cost_estimate=pl.CostEstimate(
            flops=6 * products, bytes_accessed=4 * width * depth, transcendentals=0
        ),
        name="inner_sums",
    )(order, core, eig, *bufs, *([before] if last else []))


def update_kernel(order_ref, sum_ref, eig_ref, *refs):
    bufs = (refs[0:4], refs[4:8])
    out_ref, vecs, eig, out, high, low = refs[8], refs[9:11], *refs[11:15]
    sems, eig_sems, out_sems = refs[15:]
    rows, cols = eig.shape
    owners, nblk, share, _ = vecs[0].shape
    kb = owners * share
    first_pair = nblk * rows
    pairs = pair_list(nblk)
    width_b = vecs[1].shape[3]
    width_a = cols - width_b

    eig_copies = []
    copies = []
    for part, (at, width) in enumerate(((0, width_a), (width_a, width_b))):
        whole = pl.ds(0, vecs[part].shape[3])
        copies.append(
            gather_copies(order_ref, part, bufs[part], vecs[part], whole, sems.at[part])
        )
        lane = pl.ds(at, width)
        eig_copies.append(
            pltpu.make_async_copy(eig_ref.at[:, lane], eig.at[:, lane], eig_sems.at[part])
        )
        for copy in copies[part]:
            copy.start()
        eig_copies[part].start()

    for copy in copies[0]:
        copy.wait()
    scaled = []
    for c in range(nblk):
        proj = sum_ref[c * rows : (c + 1) * rows]
        for b in range(c):
            at = first_pair + pairs.index((b, c)) * kb
            proj = proj - exact(scaled[b], sum_ref[at : at + kb], NN)
        factor = vecs[0][:, c, :, width_a : width_a + kb].reshape(kb, kb)
        scaled.append(exact(proj, factor, NT))
        lane = slice(c * kb, (c + 1) * kb)
        high[:, lane], low[:, lane] = split(scaled[c])

    left = (high[...], low[...])
    out_copies = []
    for part, (start, width) in enumerate(((0, width_a), (width_a, width_b))):
        if part > 0:
            for copy in copies[part]:
                copy.wait()
        eig_copies[part].wait()
        for at in range(0, width, 256):
            size = min(256, width - at)
            here = slice(start + at, start + at + size)
            right = jnp.concatenate(
                [vecs[part][:, b, :, at : at + size].reshape(kb, size) for b in range(nblk)],
                axis=0,
            )
            out[:, here] = eig[:, here] - product(left, split(right), NN)
        lane = pl.ds(start, width)
        out_copies.append(
            pltpu.make_async_copy(out.at[:, lane], out_ref.at[:, lane], out_sems.at[part])
        )
        out_copies[part].start()
    for copy in out_copies:
        copy.wait()


def update(order, sums, eig, parts):
    rows, cols = eig.shape
    _, nblk, share, _ = parts[0][0].shape
    owners = sum(buf.shape[0] for buf in parts[0])
    kb = owners * share
    vmem = pl.BlockSpec(memory_space=pltpu.VMEM)
    smem = pl.BlockSpec(memory_space=pltpu.SMEM)
    hbm = pl.BlockSpec(memory_space=pl.ANY)
    return pl.pallas_call(
        update_kernel,
        out_shape=jax.ShapeDtypeStruct(eig.shape, F32),
        in_specs=[smem, vmem] + [hbm] * 9,
        out_specs=hbm,
        scratch_shapes=[
            pltpu.VMEM((owners, nblk, share, parts[0][0].shape[3]), F32),
            pltpu.VMEM((owners, nblk, share, parts[1][0].shape[3]), F32),
            pltpu.VMEM((rows, cols), F32),
            pltpu.VMEM((rows, cols), F32),
            pltpu.VMEM((rows, nblk * kb), BF16),
            pltpu.VMEM((rows, nblk * kb), BF16),
            pltpu.SemaphoreType.DMA((2, owners)),
            pltpu.SemaphoreType.DMA((2,)),
            pltpu.SemaphoreType.DMA((2,)),
        ],
        compiler_params=pltpu.CompilerParams(vmem_limit_bytes=VMEM_LIMIT),
        cost_estimate=pl.CostEstimate(
            flops=6 * rows * nblk * kb * cols,
            bytes_accessed=4 * cols * (2 * rows + nblk * kb),
            transcendentals=0,
        ),
        name="update",
    )(order, sums, eig, *parts[0], *parts[1])


def gather_in_plane(own, part, nprow, npcol):
    def send(x, step):
        pairs = []
        for row in range(nprow):
            mask = ROUTES[part][row % 2][step]
            pairs += [(row * npcol + at, row * npcol + (at ^ mask)) for at in range(npcol)]
        return lax.ppermute(x, ("prow", "pcol"), pairs)

    held = own[None]
    held = jnp.concatenate([held, send(held, 0)], axis=0)
    held = jnp.concatenate([held, send(held, 1)], axis=0)
    third = send(held, 2)
    return held, third, send(held, 3), send(third, 3)


def sum_over_rows(keep, give, nprow):
    half, kb = keep.shape
    nz = nprow // 2
    along_z = [list(range(core, nprow, 2)) for core in range(2)]
    in_chip = [[2 * z, 2 * z + 1] for z in range(nz)]
    mine = keep + lax.ppermute(give, "prow", [(i, i ^ 1) for i in range(nprow)])
    parts = lax.all_to_all(
        mine.reshape(nz, half // nz, kb), "prow", 0, 0, axis_index_groups=along_z
    )
    part = jnp.sum(parts, axis=0)
    whole = lax.all_to_all(
        jnp.broadcast_to(part, (nz,) + part.shape), "prow", 0, 0, axis_index_groups=along_z
    )
    return lax.all_gather(
        whole.reshape(half, kb), "prow", axis=0, tiled=True, axis_index_groups=in_chip
    )


def solution(mesh):
    placed = (P("pcol", "prow"), P(None, "pcol", "prow"), P(None, "pcol", None))
    nprow, npcol = mesh.shape["prow"], mesh.shape["pcol"]
    orders = np.array([[arrival_order(route) for route in routes] for routes in ROUTES], np.int32)

    def per_device(eig, house_vecs, wy_factor):
        nblk, _, kb = wy_factor.shape
        rows, cols = eig.shape
        width_a = (cols // 128 - 1) // 2 * 128
        core = lax.rem(lax.axis_index("prow"), 2).astype(jnp.int32)
        order = jnp.bitwise_xor(
            lax.axis_index("pcol").astype(jnp.int32),
            jnp.where(core == 0, orders[:, 0], orders[:, 1]),
        )
        own_a = jnp.concatenate([house_vecs[:, :, :width_a], wy_factor], axis=2)
        own_b = house_vecs[:, :, width_a:]
        part_a = gather_in_plane(own_a, 0, nprow, npcol)
        part_b = gather_in_plane(own_b, 1, nprow, npcol)
        filled = nblk * rows + len(pair_list(nblk)) * kb
        half = -(-filled // (8 * nprow)) * 8 * nprow // 2
        core = core.reshape(1)
        (before,) = inner_sums(0, half, order, core, eig, part_a, width_a)
        keep, give = inner_sums(1, half, order, core, eig, part_b, cols - width_a, before)
        sums = sum_over_rows(keep, give, nprow)
        return update(order, sums, eig, (part_a, part_b))

    return jax.shard_map(
        per_device, mesh=mesh, in_specs=placed, out_specs=P("pcol", "prow"), check_vma=False
    )
```

time: 204 us -> 170 us (0.83)
  waiting for transfers between devices: 104 us -> 41.8 us
  starting transfers between devices: 14.2 us -> 45.3 us
  between operations: 13.5 us -> 0.25 us
  Pallas kernels: 16.2 us -> 22.4 us
  blocking collectives: 53.6 us -> 57.1 us
    all_gather x1 -> x0, waiting for transfers between devices: 102 us -> none  [per_device(): vecs = lax.all_gather(house_vecs, 'pcol', axis=0)]
    ppermute x0 -> x10, waiting for transfers between devices: none -> 40.6 us  [send(): return lax.ppermute(x, ('prow', 'pcol'), pairs)]
    ppermute x0 -> x10, starting transfers between devices: none -> 33.2 us  [send(): return lax.ppermute(x, ('prow', 'pcol'), pairs)]
    all_to_all x0 -> x1, blocking collectives: none -> 26.6 us  [sum_over_rows(): lax.all_to_all(jnp.broadcast_to(part, (nz,) + part.shape), 'prow', 0, 0,...]
    all_gather x1 -> x0, blocking collectives: 19 us -> none  [per_device(): factors = lax.all_gather(wy_factor, 'pcol', axis=0)]
    all_to_all x1 -> x0, starting transfers between devices: 11.6 us -> none  [sum_over_rows(): lax.all_to_all(jnp.broadcast_to(part, (nz,) + part.shape), 'prow', 0, 0,...]
    ppermute x1, starting transfers between devices: 2.58 us -> 12.1 us  [sum_over_rows(): mine = keep + lax.ppermute(give, 'prow', [(i, i ^ 1) for i in range(nprow)])]
    pallas_call x1 -> x2, Pallas kernels: 8.79 us -> 14.3 us  [inner_sums(): pl.pallas_call(lambda *refs: inner_kernel(part, half, *refs), out_shape=o...]
  transfers between devices with their start and end apart: 3 -> 11, of which waited for: 2 -> 8; matrix products, arithmetic and copies ran while one was open for 0% -> 0% of each run, Pallas kernels for 0% -> 4%
where the time goes in v2:
time: 170 us; the launch traced here: 169 us
  blocking collectives  57.1 us (34%)
  starting transfers between devices  45.3 us (27%)
  waiting for transfers between devices  41.8 us (25%)
  Pallas kernels  22.4 us (13%)
    ppermute x10, waiting for transfers between devices, send(): return lax.ppermute(x, ('prow', 'pcol'), pairs)  40.6 us
    ppermute x10, starting transfers between devices, send(): return lax.ppermute(x, ('prow', 'pcol'), pairs)  33.2 us
    all_to_all x1, blocking collectives, sum_over_rows(): lax.all_to_all(jnp.broadcast_to(part, (nz,) + part.shape), 'prow', 0, 0,...  26.6 us
    all_to_all x1, blocking collectives, sum_over_rows(): lax.all_to_all(mine.reshape(nz, half // nz, kb), 'prow', 0, 0, axis_index...  22.1 us
    pallas_call x2, Pallas kernels, inner_sums(): pl.pallas_call(lambda *refs: inner_kernel(part, half, *refs), out_shape=o...  14.3 us
    ppermute x1, starting transfers between devices, sum_over_rows(): mine = keep + lax.ppermute(give, 'prow', [(i, i ^ 1) for i in range(nprow)])  12.1 us
    all_gather x1, blocking collectives, sum_over_rows(): lax.all_gather(whole.reshape(half, kb), 'prow', axis=0, tiled=True, axis_...  8.44 us
    pallas_call x1, Pallas kernels, update(): pl.pallas_call(update_kernel, out_shape=jax.ShapeDtypeStruct(eig.shape, F...  8.17 us
  transfers between devices with their start and end apart: 11, of which 8 were waited for; matrix products, arithmetic and copies ran while one was open for 0% of the time, Pallas kernels for 4%

profile of v2, /device:TPU:1, one launch (start us, length us, event | category | flops | bytes accessed | tf_op | source)
XLA Modules:
  0.0 169.1 jit_solution(7136368650412604042)
XLA Ops:
  0.0 0.0 copy-start.1
  0.0 1.1 slice.7
  1.1 0.7 maximum_bitcast_fusion
  1.8 4.0 %collective-permute-start.5 = (f32[1,4,8,2432]{3,2,1,0:T(8,128)S(1)}, f32[1,4,8,2432]{3,2,1,0:T(8,128)S(1)}, u32[]{:S(2)}, u32[]{:S(2)}) collective-permute-start(f32[1,4,8,2432]{3,2,1,0:T(8,128)S(1)} %maximum_bitcast_fusion), channel_id=1, source_target_pairs={{0,4},{1,5},{2,6},{3,7},{4,0},{5,1},{6,2},{7,3},{8,12},{9,13},{10,... | collective-permute-start | bytes 933896 | tf_op jit(solution)/shard_map/ppermute | solution.py:274
  5.8 0.0 copy-done.1
  5.9 3.8 %collective-permute-start = (f32[1,4,8,2560]{3,2,1,0:T(8,128)S(1)}, f32[1,4,8,2560]{3,2,1,0:T(8,128)S(1)}, u32[]{:S(2)}, u32[]{:S(2)}) collective-permute-start(f32[1,4,8,2560]{3,2,1,0:T(8,128)S(1)} %slice_bitcast_fusion), channel_id=1, source_target_pairs={{0,12},{1,13},{2,14},{3,15},{4,8},{5,9},{6,10},{7,11},{8,4},{9,5},... | collective-permute-start | bytes 983048 | tf_op jit(solution)/shard_map/ppermute | solution.py:274
  9.7 0.4 collective-permute-done.5
  10.2 5.1 %collective-permute-start.6 = (f32[2,4,8,2432]{3,2,1,0:T(8,128)S(1)}, f32[2,4,8,2432]{3,2,1,0:T(8,128)S(1)}, u32[]{:S(2)}, u32[]{:S(2)}) collective-permute-start(f32[2,4,8,2432]{3,2,1,0:T(8,128)S(1)} %pad_maximum_fusion.3), channel_id=1, source_target_pairs={{0,12},{1,13},{2,14},{3,15},{4,8},{5,9},{6,10},{7,11},{8,4},{9,5},... | collective-permute-start | bytes 1867784 | tf_op jit(solution)/shard_map/ppermute | solution.py:274
  15.3 0.0 collective-permute-done
  15.3 1.9 %collective-permute-start.1 = (f32[2,4,8,2560]{3,2,1,0:T(8,128)S(1)}, f32[2,4,8,2560]{3,2,1,0:T(8,128)S(1)}, u32[]{:S(2)}, u32[]{:S(2)}) collective-permute-start(f32[2,4,8,2560]{3,2,1,0:T(8,128)S(1)} %pad_maximum_fusion.2), channel_id=1, source_target_pairs={{0,4},{1,5},{2,6},{3,7},{4,0},{5,1},{6,2},{7,3},{8,12},{9,13},{10,... | collective-permute-start | bytes 1966088 | tf_op jit(solution)/shard_map/ppermute | solution.py:274
  17.3 5.6 %collective-permute-done.6 = f32[2,4,8,2432]{3,2,1,0:T(8,128)S(1)} collective-permute-done((f32[2,4,8,2432]{3,2,1,0:T(8,128)S(1)}, f32[2,4,8,2432]{3,2,1,0:T(8,128)S(1)}, u32[]{:S(2)}, u32[]{:S(2)}) %collective-permute-start.6) | collective-permute-done | bytes 622624 | tf_op jit(solution)/shard_map/ppermute | solution.py:274
  22.9 0.1 pad_maximum_fusion.1.refs_3_.refs_0_
  23.0 0.0 copy-start.2
  23.0 0.0 copy-start.3
  23.0 3.1 %collective-permute-start.7 = (f32[4,4,8,2432]{3,2,1,0:T(8,128)S(1)}, f32[4,4,8,2432]{3,2,1,0:T(8,128)}, u32[]{:S(2)}, u32[]{:S(2)}) collective-permute-start(f32[4,4,8,2432]{3,2,1,0:T(8,128)S(1)} %pad_maximum_fusion.1.refs_3_.refs_0_), channel_id=1, source_target_pairs={{0,1},{1,0},{2,3},{3,2},{4,5},{5,4},{6,7},{7,6},{8,9},{9,8},{10,11... | collective-permute-start | bytes 3735560 | tf_op jit(solution)/shard_map/ppermute | solution.py:274
  26.1 0.8 collective-permute-done.1
  27.0 0.1 pad_maximum_fusion.refs_3_.refs_4_
  27.0 0.0 copy-start
  27.1 4.4 %collective-permute-start.2 = (f32[4,4,8,2560]{3,2,1,0:T(8,128)S(1)}, f32[4,4,8,2560]{3,2,1,0:T(8,128)}, u32[]{:S(2)}, u32[]{:S(2)}) collective-permute-start(f32[4,4,8,2560]{3,2,1,0:T(8,128)S(1)} %pad_maximum_fusion.refs_3_.refs_4_), channel_id=1, source_target_pairs={{0,3},{1,2},{2,1},{3,0},{4,7},{5,6},{6,5},{7,4},{8,11},{9,10},{10,... | collective-permute-start | bytes 3932168 | tf_op jit(solution)/shard_map/ppermute | solution.py:274
  31.5 2.1 %collective-permute-start.8 = (f32[4,4,8,2432]{3,2,1,0:T(8,128)S(1)}, f32[4,4,8,2432]{3,2,1,0:T(8,128)}, u32[]{:S(2)}, u32[]{:S(2)}) collective-permute-start(f32[4,4,8,2432]{3,2,1,0:T(8,128)S(1)} %pad_maximum_fusion.1.refs_3_.refs_0_), channel_id=1, source_target_pairs={{0,3},{1,2},{2,1},{3,0},{4,7},{5,6},{6,5},{7,4},{8,11},{9,10},{10,... | collective-permute-start | bytes 3735560 | tf_op jit(solution)/shard_map/ppermute | solution.py:274
  33.6 12.8 %collective-permute-done.7.refs_4_.refs_1_ = f32[4,4,8,2432]{3,2,1,0:T(8,128)} collective-permute-done((f32[4,4,8,2432]{3,2,1,0:T(8,128)S(1)}, f32[4,4,8,2432]{3,2,1,0:T(8,128)}, u32[]{:S(2)}, u32[]{:S(2)}) %collective-permute-start.7) | collective-permute-done | bytes 1245216 | tf_op jit(solution)/shard_map/ppermute | solution.py:274
  46.4 3.5 %collective-permute-start.9 = (f32[4,4,8,2432]{3,2,1,0:T(8,128)}, f32[4,4,8,2432]{3,2,1,0:T(8,128)}, u32[]{:S(2)}, u32[]{:S(2)}) collective-permute-start(f32[4,4,8,2432]{3,2,1,0:T(8,128)} %collective-permute-done.7.refs_4_.refs_1_), channel_id=1, source_target_pairs={{0,3},{1,2},{2,1},{3,0},{4,7},{5,6},{6,5},{7,4},{8,11},{9,10},{10,... | collective-permute-start | bytes 3735560 | tf_op jit(solution)/shard_map/ppermute | solution.py:274
  49.9 1.9 %collective-permute-start.3 = (f32[4,4,8,2560]{3,2,1,0:T(8,128)S(1)}, f32[4,4,8,2560]{3,2,1,0:T(8,128)}, u32[]{:S(2)}, u32[]{:S(2)}) collective-permute-start(f32[4,4,8,2560]{3,2,1,0:T(8,128)S(1)} %pad_maximum_fusion.refs_3_.refs_4_), channel_id=1, source_target_pairs={{0,1},{1,0},{2,3},{3,2},{4,5},{5,4},{6,7},{7,6},{8,9},{9,8},{10,11... | collective-permute-start | bytes 3932168 | tf_op jit(solution)/shard_map/ppermute | solution.py:274
  51.8 0.0 collective-permute-done.2.refs_4_.refs_5_
  51.8 3.4 %collective-permute-start.4 = (f32[4,4,8,2560]{3,2,1,0:T(8,128)}, f32[4,4,8,2560]{3,2,1,0:T(8,128)}, u32[]{:S(2)}, u32[]{:S(2)}) collective-permute-start(f32[4,4,8,2560]{3,2,1,0:T(8,128)} %collective-permute-done.2.refs_4_.refs_5_), channel_id=1, source_target_pairs={{0,1},{1,0},{2,3},{3,2},{4,5},{5,4},{6,7},{7,6},{8,9},{9,8},{10,11... | collective-permute-start | bytes 3932168 | tf_op jit(solution)/shard_map/ppermute | solution.py:274
  55.2 0.0 copy-done.2
  55.2 0.0 copy-done.3
  55.2 5.1 %collective-permute-done.8.refs_5_.refs_2_ = f32[4,4,8,2432]{3,2,1,0:T(8,128)} collective-permute-done((f32[4,4,8,2432]{3,2,1,0:T(8,128)S(1)}, f32[4,4,8,2432]{3,2,1,0:T(8,128)}, u32[]{:S(2)}, u32[]{:S(2)}) %collective-permute-start.8) | collective-permute-done | bytes 1245216 | tf_op jit(solution)/shard_map/ppermute | solution.py:274
  60.4 13.3 %collective-permute-done.9.refs_6_.refs_3_ = f32[4,4,8,2432]{3,2,1,0:T(8,128)} collective-permute-done((f32[4,4,8,2432]{3,2,1,0:T(8,128)}, f32[4,4,8,2432]{3,2,1,0:T(8,128)}, u32[]{:S(2)}, u32[]{:S(2)}) %collective-permute-start.9) | collective-permute-done | bytes 1245216 | tf_op jit(solution)/shard_map/ppermute | solution.py:274
  73.7 6.6 %inner_sums.2.refs_7_ = f32[1280,128]{1,0:T(8,128)S(1)} custom-call(s32[2,16]{1,0:T(2,128)S(1)} %select_xor_fusion.refs_0_.order_ref, s32[1]{0:T(128)} %bitcast.refs_1_, f32[96,4864]{1,0:T(8,128)} %eig_ref.1, f32[4,4,8,2432]{3,2,1,0:T(8,128)S(1)} %pad_maximum_fusion.1.refs_3_.refs_0_, f32[4,4,8,2432]{3,2,1,0:T(8,128)} %collective-permute-done.7.refs_4_.refs_1_, ...), custom_call_target="tpu_custom_call" | custom-call | flops 2038431744 | bytes 5603328 | tf_op jit(solution)/shard_map/inner_sums/pallas_call | solution.py:148
  80.3 0.0 copy-done
  80.3 0.0 collective-permute-done.3.refs_5_.refs_6_
  80.3 2.4 %collective-permute-done.4.refs_6_.refs_7_ = f32[4,4,8,2560]{3,2,1,0:T(8,128)} collective-permute-done((f32[4,4,8,2560]{3,2,1,0:T(8,128)}, f32[4,4,8,2560]{3,2,1,0:T(8,128)}, u32[]{:S(2)}, u32[]{:S(2)}) %collective-permute-start.4) | collective-permute-done | bytes 1310752 | tf_op jit(solution)/shard_map/ppermute | solution.py:274
  82.7 7.7 %inner_sums.3 = (f32[640,128]{1,0:T(8,128)S(1)}, f32[640,128]{1,0:T(8,128)S(1)}) custom-call(s32[2,16]{1,0:T(2,128)S(1)} %select_xor_fusion.refs_0_.order_ref, s32[1]{0:T(128)} %bitcast.refs_1_, f32[96,4864]{1,0:T(8,128)} %eig_ref.1, f32[4,4,8,2560]{3,2,1,0:T(8,128)} %copy-done, f32[4,4,8,2560]{3,2,1,0:T(8,128)} %collective-permute-done.2.refs_4_.refs_5_, ...), custom_call_target="tpu_custom_call" | custom-call | flops 2264924160 | bytes 6225920 | tf_op jit(solution)/shard_map/inner_sums/pallas_call | solution.py:148
  90.4 12.1 %collective-permute-start.10 = (f32[640,128]{1,0:T(8,128)S(1)}, f32[640,128]{1,0:T(8,128)S(1)}, u32[]{:S(2)}, u32[]{:S(2)}) collective-permute-start(f32[640,128]{1,0:T(8,128)S(1)} %get-tuple-element.8), channel_id=1, source_target_pairs={{0,16},{16,0},{32,48},{48,32},{64,80},{80,64},{96,112},{112,96},{1... | collective-permute-start | bytes 983048 | tf_op jit(solution)/shard_map/ppermute | solution.py:288
  102.5 1.2 collective-permute-done.10
  103.8 22.1 %all_to_all.10 = f32[16,40,128]{2,1,0:T(8,128)S(1)} all-to-all(f32[16,40,128]{2,1,0:T(8,128)S(1)} %bitcast.7), channel_id=1, replica_groups={{0,32,64,96,128,160,192,224,256,288,320,352,384,416,448,480},{16,48,80,..., dimensions={0} | all-to-all | bytes 655360 | tf_op jit(solution)/shard_map/all_to_all | solution.py:289
  125.9 26.6 %all_to_all.11 = f32[16,40,128]{2,1,0:T(8,128)S(1)} all-to-all(f32[16,40,128]{2,1,0:T(8,128)S(1)} %broadcast_in_dim.11), channel_id=1, replica_groups={{0,32,64,96,128,160,192,224,256,288,320,352,384,416,448,480},{16,48,80,..., dimensions={0} | all-to-all | bytes 655360 | tf_op jit(solution)/shard_map/all_to_all | solution.py:293
  152.5 8.4 %all_gather.3.sum_ref = f32[1280,128]{1,0:T(8,128)S(1)} all-gather(f32[640,128]{1,0:T(8,128)S(1)} %bitcast.8), channel_id=1, replica_groups={{0,16},{32,48},{64,80},{96,112},{128,144},{160,176},{192,208},{224,240}..., dimensions={0}, use_global_device_ids=true | all-gather | bytes 983040 | tf_op jit(solution)/shard_map/all_gather | solution.py:296
  160.9 8.2 %update.1 = f32[96,4864]{1,0:T(8,128)} custom-call(s32[2,16]{1,0:T(2,128)S(1)} %select_xor_fusion.refs_0_.order_ref, f32[1280,128]{1,0:T(8,128)S(1)} %all_gather.3.sum_ref, f32[96,4864]{1,0:T(8,128)} %eig_ref.1, f32[4,4,8,2432]{3,2,1,0:T(8,128)S(1)} %pad_maximum_fusion.1.refs_3_.refs_0_, f32[4,4,8,2432]{3,2,1,0:T(8,128)} %collective-permute-done.7.refs_4_.refs_1_, ...), custom_call_target="tpu_custom_call" | custom-call | flops 1434451968 | bytes 13697024 | tf_op jit(solution)/shard_map/update/pallas_call | solution.py:242
  (7 shorter events, 0.2 us)
Async XLA Ops:
  0.0 5.8 %copy-start.1 = (f32[4,8,4864]{2,1,0:T(8,128)S(1)}, f32[4,8,4864]{2,1,0:T(8,128)}, u32[]{:S(2)}) copy-start(f32[4,8,4864]{2,1,0:T(8,128)} %param.6) | copy-start | bytes 1867780
  1.8 8.3 %collective-permute-start.5 = (f32[1,4,8,2432]{3,2,1,0:T(8,128)S(1)}, f32[1,4,8,2432]{3,2,1,0:T(8,128)S(1)}, u32[]{:S(2)}, u32[]{:S(2)}) collective-permute-start(f32[1,4,8,2432]{3,2,1,0:T(8,128)S(1)} %maximum_bitcast_fusion), channel_id=1, source_target_pairs={{0,4},{1,5},{2,6},{3,7},{4,0},{5,1},{6,2},{7,3},{8,12},{9,13},{10,... | collective-permute-start | bytes 933896 | tf_op jit(solution)/shard_map/ppermute | solution.py:274
  5.9 9.4 %collective-permute-start = (f32[1,4,8,2560]{3,2,1,0:T(8,128)S(1)}, f32[1,4,8,2560]{3,2,1,0:T(8,128)S(1)}, u32[]{:S(2)}, u32[]{:S(2)}) collective-permute-start(f32[1,4,8,2560]{3,2,1,0:T(8,128)S(1)} %slice_bitcast_fusion), channel_id=1, source_target_pairs={{0,12},{1,13},{2,14},{3,15},{4,8},{5,9},{6,10},{7,11},{8,4},{9,5},... | collective-permute-start | bytes 983048 | tf_op jit(solution)/shard_map/ppermute | solution.py:274
  10.2 12.7 %collective-permute-start.6 = (f32[2,4,8,2432]{3,2,1,0:T(8,128)S(1)}, f32[2,4,8,2432]{3,2,1,0:T(8,128)S(1)}, u32[]{:S(2)}, u32[]{:S(2)}) collective-permute-start(f32[2,4,8,2432]{3,2,1,0:T(8,128)S(1)} %pad_maximum_fusion.3), channel_id=1, source_target_pairs={{0,12},{1,13},{2,14},{3,15},{4,8},{5,9},{6,10},{7,11},{8,4},{9,5},... | collective-permute-start | bytes 1867784 | tf_op jit(solution)/shard_map/ppermute | solution.py:274
  15.3 11.6 %collective-permute-start.1 = (f32[2,4,8,2560]{3,2,1,0:T(8,128)S(1)}, f32[2,4,8,2560]{3,2,1,0:T(8,128)S(1)}, u32[]{:S(2)}, u32[]{:S(2)}) collective-permute-start(f32[2,4,8,2560]{3,2,1,0:T(8,128)S(1)} %pad_maximum_fusion.2), channel_id=1, source_target_pairs={{0,4},{1,5},{2,6},{3,7},{4,0},{5,1},{6,2},{7,3},{8,12},{9,13},{10,... | collective-permute-start | bytes 1966088 | tf_op jit(solution)/shard_map/ppermute | solution.py:274
  23.0 32.2 %copy-start.2 = (s32[2,16]{1,0:T(2,128)S(1)}, s32[2,16]{1,0:T(2,128)}, u32[]{:S(2)}) copy-start(s32[2,16]{1,0:T(2,128)} %constant.22.clone) | copy-start | bytes 388
  23.0 32.2 %copy-start.3 = (s32[2,16]{1,0:T(2,128)S(1)}, s32[2,16]{1,0:T(2,128)}, u32[]{:S(2)}) copy-start(s32[2,16]{1,0:T(2,128)} %constant.21.clone) | copy-start | bytes 388
  23.0 23.4 %collective-permute-start.7 = (f32[4,4,8,2432]{3,2,1,0:T(8,128)S(1)}, f32[4,4,8,2432]{3,2,1,0:T(8,128)}, u32[]{:S(2)}, u32[]{:S(2)}) collective-permute-start(f32[4,4,8,2432]{3,2,1,0:T(8,128)S(1)} %pad_maximum_fusion.1.refs_3_.refs_0_), channel_id=1, source_target_pairs={{0,1},{1,0},{2,3},{3,2},{4,5},{5,4},{6,7},{7,6},{8,9},{9,8},{10,11... | collective-permute-start | bytes 3735560 | tf_op jit(solution)/shard_map/ppermute | solution.py:274
  27.0 53.2 %copy-start = (f32[4,4,8,2560]{3,2,1,0:T(8,128)}, f32[4,4,8,2560]{3,2,1,0:T(8,128)S(1)}, u32[]{:S(2)}) copy-start(f32[4,4,8,2560]{3,2,1,0:T(8,128)S(1)} %pad_maximum_fusion.refs_3_.refs_4_) | copy-start | bytes 3932164
  27.1 24.8 %collective-permute-start.2 = (f32[4,4,8,2560]{3,2,1,0:T(8,128)S(1)}, f32[4,4,8,2560]{3,2,1,0:T(8,128)}, u32[]{:S(2)}, u32[]{:S(2)}) collective-permute-start(f32[4,4,8,2560]{3,2,1,0:T(8,128)S(1)} %pad_maximum_fusion.refs_3_.refs_4_), channel_id=1, source_target_pairs={{0,3},{1,2},{2,1},{3,0},{4,7},{5,6},{6,5},{7,4},{8,11},{9,10},{10,... | collective-permute-start | bytes 3932168 | tf_op jit(solution)/shard_map/ppermute | solution.py:274
  31.5 28.9 %collective-permute-start.8 = (f32[4,4,8,2432]{3,2,1,0:T(8,128)S(1)}, f32[4,4,8,2432]{3,2,1,0:T(8,128)}, u32[]{:S(2)}, u32[]{:S(2)}) collective-permute-start(f32[4,4,8,2432]{3,2,1,0:T(8,128)S(1)} %pad_maximum_fusion.1.refs_3_.refs_0_), channel_id=1, source_target_pairs={{0,3},{1,2},{2,1},{3,0},{4,7},{5,6},{6,5},{7,4},{8,11},{9,10},{10,... | collective-permute-start | bytes 3735560 | tf_op jit(solution)/shard_map/ppermute | solution.py:274
  46.4 27.3 %collective-permute-start.9 = (f32[4,4,8,2432]{3,2,1,0:T(8,128)}, f32[4,4,8,2432]{3,2,1,0:T(8,128)}, u32[]{:S(2)}, u32[]{:S(2)}) collective-permute-start(f32[4,4,8,2432]{3,2,1,0:T(8,128)} %collective-permute-done.7.refs_4_.refs_1_), channel_id=1, source_target_pairs={{0,3},{1,2},{2,1},{3,0},{4,7},{5,6},{6,5},{7,4},{8,11},{9,10},{10,... | collective-permute-start | bytes 3735560 | tf_op jit(solution)/shard_map/ppermute | solution.py:274
  49.9 30.4 %collective-permute-start.3 = (f32[4,4,8,2560]{3,2,1,0:T(8,128)S(1)}, f32[4,4,8,2560]{3,2,1,0:T(8,128)}, u32[]{:S(2)}, u32[]{:S(2)}) collective-permute-start(f32[4,4,8,2560]{3,2,1,0:T(8,128)S(1)} %pad_maximum_fusion.refs_3_.refs_4_), channel_id=1, source_target_pairs={{0,1},{1,0},{2,3},{3,2},{4,5},{5,4},{6,7},{7,6},{8,9},{9,8},{10,11... | collective-permute-start | bytes 3932168 | tf_op jit(solution)/shard_map/ppermute | solution.py:274
  51.8 30.9 %collective-permute-start.4 = (f32[4,4,8,2560]{3,2,1,0:T(8,128)}, f32[4,4,8,2560]{3,2,1,0:T(8,128)}, u32[]{:S(2)}, u32[]{:S(2)}) collective-permute-start(f32[4,4,8,2560]{3,2,1,0:T(8,128)} %collective-permute-done.2.refs_4_.refs_5_), channel_id=1, source_target_pairs={{0,1},{1,0},{2,3},{3,2},{4,5},{5,4},{6,7},{7,6},{8,9},{9,8},{10,11... | collective-permute-start | bytes 3932168 | tf_op jit(solution)/shard_map/ppermute | solution.py:274
  90.4 13.3 %collective-permute-start.10 = (f32[640,128]{1,0:T(8,128)S(1)}, f32[640,128]{1,0:T(8,128)S(1)}, u32[]{:S(2)}, u32[]{:S(2)}) collective-permute-start(f32[640,128]{1,0:T(8,128)S(1)} %get-tuple-element.8), channel_id=1, source_target_pairs={{0,16},{16,0},{32,48},{48,32},{64,80},{80,64},{96,112},{112,96},{1... | collective-permute-start | bytes 983048 | tf_op jit(solution)/shard_map/ppermute | solution.py:288

commit v3 on v0

v3 whole, which is shorter than its diff:
```python
import jax
import jax.numpy as jnp
import numpy as np
from jax import lax
from jax.experimental import pallas as pl
from jax.experimental.pallas import tpu as pltpu
from jax.sharding import PartitionSpec as P

F32 = jnp.float32
BF16 = jnp.bfloat16
NT = (((1,), (1,)), ((), ()))
NN = (((1,), (0,)), ((), ()))
VMEM_LIMIT = 52 * 2**20
X_NEAR, X_WRAP, Y_NEAR, Y_WRAP = 4, 12, 1, 3
PARTNER = (Y_WRAP, X_WRAP)
ROUTES = (
    ((Y_NEAR, X_NEAR, X_WRAP), (X_NEAR, Y_NEAR, Y_WRAP)),
    ((X_WRAP, Y_NEAR, X_NEAR), (Y_WRAP, X_NEAR, Y_NEAR)),
)
LATE_ROUTE = ((Y_NEAR, X_WRAP, X_NEAR), (X_NEAR, Y_WRAP, Y_NEAR))


def split(x):
    high = x.astype(BF16)
    low = (x - high.astype(F32)).astype(BF16)
    return high, low


def product(left, right, dims):
    def dot(x, y):
        return lax.dot_general(x, y, dims, preferred_element_type=F32)

    return dot(left[0], right[0]) + (dot(left[1], right[0]) + dot(left[0], right[1]))


def exact(left, right, dims):
    return lax.dot_general(
        left, right, dims, precision=lax.Precision.HIGHEST, preferred_element_type=F32
    )


def pair_list(nblk):
    return [(b, c) for b in range(nblk) for c in range(b + 1, nblk)]


def arrival_order(part, core):
    near, second, third = ROUTES[part][core]
    first = [0, near, PARTNER[core], PARTNER[core] ^ near]
    return [at ^ mask for mask in (0, second, third, second ^ third) for at in first]


def late_orders(core):
    near, second, third = LATE_ROUTE[core]
    group = [at ^ mask for mask in (0, second, third, second ^ third) for at in (0, near)]
    rows = [group]
    for part in range(2):
        near, second, third = ROUTES[part][core]
        rows.append(
            [
                PARTNER[core] ^ at ^ mask
                for mask in (0, second, third, second ^ third)
                for at in (0, near)
            ]
        )
    return rows


def owner_copies(order_ref, part, bufs, into, start, sems):
    copies = []
    slot = 0
    for buf in bufs:
        for i in range(buf.shape[0]):
            lane = pl.ds(start, buf.shape[3])
            copies.append(
                pltpu.make_async_copy(
                    buf.at[i], into.at[order_ref[part, slot], :, :, lane], sems.at[part, slot]
                )
            )
            slot += 1
    return copies


def inner_kernel(order_ref, info_ref, eig_ref, mate_ref, *refs):
    bufs = (refs[0:4], refs[4:8])
    keep_ref, give_ref, fac_ref = refs[8:11]
    vecs, eig, mate, high, low, gram, sems, eig_sems, mate_sems = refs[11:]
    rows, half = eig.shape
    owners, nblk, share, _ = vecs.shape
    kb = owners * share
    side, parity = info_ref[0], info_ref[1]
    width_a = bufs[0][0].shape[3]
    data_a = half - bufs[1][0].shape[3]
    pieces = ((0, 0, data_a), (width_a, data_a, half - data_a))

    copies = []
    for part, (start, at, size) in enumerate(pieces):
        lane = pl.ds(at, size)
        off = pl.multiple_of(side * half + at, 128)
        copies.append(
            owner_copies(order_ref, part, bufs[part], vecs, start, sems)
            + [
                pltpu.make_async_copy(
                    eig_ref.at[:, pl.ds(off, size)], eig.at[:, lane], eig_sems.at[part]
                ),
                pltpu.make_async_copy(
                    mate_ref.at[:, lane], mate.at[:, lane], mate_sems.at[part]
                ),
            ]
        )
        for copy in copies[part]:
            copy.start()

    pairs = pair_list(nblk)
    first = 2 * rows
    for part, (start, at, size) in enumerate(pieces):
        for copy in copies[part]:
            copy.wait()
        lane = slice(at, at + size)
        high[:rows, lane], low[:rows, lane] = split(eig[:, lane])
        high[rows:first, lane], low[rows:first, lane] = split(mate[:, lane])
        for b in range(nblk):
            here = slice(first + b * kb, first + (b + 1) * kb)
            high[here, lane], low[here, lane] = split(
                vecs[:, b, :, start : start + size].reshape(kb, size)
            )
        for c0 in range(0, nblk, 2):
            c1 = min(c0 + 2, nblk)
            top = first + (c1 - 1) * kb
            cols = slice(first + c0 * kb, first + c1 * kb)
            out = product(
                (high[:top, lane], low[:top, lane]), (high[cols, lane], low[cols, lane]), NT
            )
            for c in range(c0, c1):
                here = slice((c - c0) * kb, (c - c0 + 1) * kb)
                to = slice(c * rows, (c + 1) * rows)
                terms = [(keep_ref, to, out[:rows, here]), (give_ref, to, out[rows:first, here])]
                for b in range(c):
                    at_pair = pairs.index((b, c)) * kb
                    from_row = first + b * kb
                    terms.append(
                        (gram, slice(at_pair, at_pair + kb), out[from_row : from_row + kb, here])
                    )
                for ref, to, term in terms:
                    ref[to] = term if part == 0 else ref[to] + term

    for b in range(nblk):
        fac_ref[b] = vecs[:, b, :, data_a:width_a].reshape(kb, kb)
    below = nblk * rows
    count = gram.shape[0] // 2
    keep_ref[below:] = gram[pl.ds(pl.multiple_of(parity * count, 8), count)]
    give_ref[below:] = gram[pl.ds(pl.multiple_of((1 - parity) * count, 8), count)]


def inner_sums(order, info, eig, mate, parts):
    rows, half = mate.shape
    _, nblk, share, _ = parts[0][0].shape
    owners = order.shape[1]
    kb = owners * share
    width = parts[0][0].shape[3] + parts[1][0].shape[3]
    depth = 2 * rows + nblk * kb
    npair = len(pair_list(nblk))
    vmem = pl.BlockSpec(memory_space=pltpu.VMEM)
    smem = pl.BlockSpec(memory_space=pltpu.SMEM)
    hbm = pl.BlockSpec(memory_space=pl.ANY)
    out = jax.ShapeDtypeStruct((nblk * rows + npair // 2 * kb, kb), F32)
    return pl.pallas_call(
        inner_kernel,
        out_shape=[out, out, jax.ShapeDtypeStruct((nblk, kb, kb), F32)],
        in_specs=[smem, smem] + [hbm] * 10,
        out_specs=[vmem] * 3,
        scratch_shapes=[
            pltpu.VMEM((owners, nblk, share, width), F32),
            pltpu.VMEM((rows, half), F32),
            pltpu.VMEM((rows, half), F32),
            pltpu.VMEM((depth, half), BF16),
            pltpu.VMEM((depth, half), BF16),
            pltpu.VMEM((npair * kb, kb), F32),
            pltpu.SemaphoreType.DMA((2, owners)),
            pltpu.SemaphoreType.DMA((2,)),
            pltpu.SemaphoreType.DMA((2,)),
        ],
        compiler_params=pltpu.CompilerParams(vmem_limit_bytes=VMEM_LIMIT),
        cost_estimate=pl.CostEstimate(
            flops=6 * half * kb * (2 * nblk * rows + npair * kb),
            bytes_accessed=4 * half * depth,
            transcendentals=0,
        ),
        name="inner_sums",
    )(order, info, eig, mate, *parts[0], *parts[1])


def update_kernel(order_ref, late_ref, info_ref, sum_ref, rest_ref, fac_ref, eig_ref, *refs):
    near, group, far, refs = (refs[0:4], refs[4:8]), refs[8:12], (refs[12:14], refs[14:16]), refs[16:]
    out_ref, vecs, eig, out, gram, high, low = refs[0], refs[1:3], *refs[3:8]
    near_sems, late_sems, eig_sems, out_sems = refs[8:]
    rows, cols = eig.shape
    owners, nblk, share, _ = vecs[0].shape
    kb = owners * share
    half = cols // 2
    width_a = near[0][0].shape[3]
    data_a = half - near[1][0].shape[3]
    side, parity = info_ref[0], info_ref[1]
    offsets = [pl.multiple_of(side * half, 128), pl.multiple_of((1 - side) * half, 128)]
    lanes = [pl.ds(0, half), pl.ds(half, half)]

    copies = [[], owner_copies(late_ref, 0, group, vecs[1], 0, late_sems)]
    for part, start in enumerate((0, width_a)):
        copies[0] += owner_copies(order_ref, part, near[part], vecs[0], start, near_sems)
        copies[1] += owner_copies(late_ref, 1 + part, far[part], vecs[1], start, late_sems)
    eig_copies, out_copies = [], []
    for n in range(2):
        theirs = pl.ds(offsets[n], half)
        eig_copies.append(
            pltpu.make_async_copy(eig_ref.at[:, theirs], eig.at[:, lanes[n]], eig_sems.at[n])
        )
        out_copies.append(
            pltpu.make_async_copy(out.at[:, lanes[n]], out_ref.at[:, theirs], out_sems.at[n])
        )
        for copy in copies[n]:
            copy.start()
        eig_copies[n].start()

    below = nblk * rows
    count = gram.shape[0] // 2
    gram[pl.ds(pl.multiple_of(parity * count, 8), count)] = sum_ref[below:]
    gram[pl.ds(pl.multiple_of((1 - parity) * count, 8), count)] = rest_ref[...]
    pairs = pair_list(nblk)
    scaled = []
    for c in range(nblk):
        proj = sum_ref[c * rows : (c + 1) * rows]
        for b in range(c):
            at = pairs.index((b, c)) * kb
            proj = proj - exact(scaled[b], gram[at : at + kb], NN)
        scaled.append(exact(proj, fac_ref[c], NT))
        lane = slice(c * kb, (c + 1) * kb)
        high[:, lane], low[:, lane] = split(scaled[c])

    left = (high[...], low[...])
    for n in range(2):
        for copy in copies[n]:
            copy.wait()
        eig_copies[n].wait()
        for start, at, stop in ((0, 0, data_a), (width_a, data_a, half)):
            for one in range(at, stop, 256):
                size = min(256, stop - one)
                here = slice(n * half + one, n * half + one + size)
                there = slice(start + one - at, start + one - at + size)
                right = jnp.concatenate(
                    [vecs[n][:, b, :, there].reshape(kb, size) for b in range(nblk)], axis=0
                )
                out[:, here] = eig[:, here] - product(left, split(right), NN)
        out_copies[n].start()
    for copy in out_copies:
        copy.wait()


def update(order, late, info, sums, rest, factors, eig, near, group, far):
    rows, cols = eig.shape
    _, nblk, share, _ = near[0][0].shape
    owners = order.shape[1]
    kb = owners * share
    width = near[0][0].shape[3] + near[1][0].shape[3]
    vmem = pl.BlockSpec(memory_space=pltpu.VMEM)
    smem = pl.BlockSpec(memory_space=pltpu.SMEM)
    hbm = pl.BlockSpec(memory_space=pl.ANY)
    return pl.pallas_call(
        update_kernel,
        out_shape=jax.ShapeDtypeStruct(eig.shape, F32),
        in_specs=[smem] * 3 + [vmem] * 3 + [hbm] * 17,
        out_specs=hbm,
        scratch_shapes=[
            pltpu.VMEM((owners, nblk, share, width), F32),
            pltpu.VMEM((owners, nblk, share, width), F32),
            pltpu.VMEM((rows, cols), F32),
            pltpu.VMEM((rows, cols), F32),
            pltpu.VMEM((2 * rest.shape[0], kb), F32),
            pltpu.VMEM((rows, nblk * kb), BF16),
            pltpu.VMEM((rows, nblk * kb), BF16),
            pltpu.SemaphoreType.DMA((2, owners)),
            pltpu.SemaphoreType.DMA((3, owners // 2)),
            pltpu.SemaphoreType.DMA((2,)),
            pltpu.SemaphoreType.DMA((2,)),
        ],
        compiler_params=pltpu.CompilerParams(vmem_limit_bytes=VMEM_LIMIT),
        cost_estimate=pl.CostEstimate(
            flops=6 * rows * nblk * kb * cols,
            bytes_accessed=4 * cols * (2 * rows + nblk * kb),
            transcendentals=0,
        ),
        name="update",
    )(order, late, info, sums, rest, factors, eig, *near[0], *near[1], *group, *far[0], *far[1])


def solution(mesh):
    placed = (P("pcol", "prow"), P(None, "pcol", "prow"), P(None, "pcol", None))
    nprow, npcol = mesh.shape["prow"], mesh.shape["pcol"]
    orders = np.array(
        [[arrival_order(part, core) for core in range(2)] for part in range(2)], np.int32
    )
    lates = np.zeros((2, 3, npcol), np.int32)
    lates[:, :, : npcol // 2] = [late_orders(core) for core in range(2)]
    in_chip = [[2 * z, 2 * z + 1] for z in range(nprow // 2)]

    def send(x, masks):
        pairs = []
        for row in range(nprow):
            mask = masks[row % 2]
            pairs += [(row * npcol + at, row * npcol + (at ^ mask)) for at in range(npcol)]
        return lax.ppermute(x, ("prow", "pcol"), pairs)

    def after(x, *others):
        return lax.optimization_barrier((x,) + others)[0]

    def doubling(own, mates, part):
        steps = [(ROUTES[part][0][n], ROUTES[part][1][n]) for n in range(3)]
        first = jnp.stack([own, send(own, steps[0]), mates, send(mates, steps[0])])
        second = send(first, steps[1])
        return first, second, send(first, steps[2]), steps[2]

    def along_z(x):
        nz = nprow // 2
        groups = [list(range(core, nprow, 2)) for core in range(2)]
        return lax.all_to_all(x, "prow", 0, 0, axis_index_groups=groups)

    def per_device(eig, house_vecs, wy_factor):
        nblk, _, kb = wy_factor.shape
        rows, cols = eig.shape
        half = cols // 2
        data_a = (half // 128 - 1) // 2 * 128
        width_a = data_a + kb
        at = lax.axis_index("pcol").astype(jnp.int32)
        core = lax.rem(lax.axis_index("prow"), 2).astype(jnp.int32)
        side = jnp.bitwise_and(jnp.where(core == 0, at >> 1, at >> 3), 1)
        parity = jnp.bitwise_and(jnp.bitwise_xor(at >> 1, at >> 3), 1)
        info = jnp.stack([side, parity])
        order = jnp.bitwise_xor(at, jnp.where(core == 0, orders[:, 0], orders[:, 1]))
        late = jnp.bitwise_xor(at, jnp.where(core == 0, lates[0], lates[1]))

        def columns(x, which):
            return lax.dynamic_slice_in_dim(x, which * half, half, axis=x.ndim - 1)

        vec_other = columns(house_vecs, 1 - side)
        vec_other = jnp.concatenate(
            [vec_other[:, :, :data_a], wy_factor, vec_other[:, :, data_a:]], axis=2
        )
        mates = send(vec_other, PARTNER)
        vec_mine = columns(house_vecs, side)
        own_a = jnp.concatenate([vec_mine[:, :, :data_a], wy_factor], axis=2)
        own_b = vec_mine[:, :, data_a:]
        near_a = doubling(own_a, mates[:, :, :width_a], 0)
        near_b = doubling(own_b, mates[:, :, width_a:], 1)
        eig_other = after(columns(eig, 1 - side), mates)
        mate_eig = send(eig_other, PARTNER)
        near = tuple(
            (first, second, third, send(after(second, mate_eig), step))
            for first, second, third, step in (near_a, near_b)
        )
        keep, give, factors = inner_sums(order, info, eig, mate_eig, near)

        late_steps = [(LATE_ROUTE[0][n], LATE_ROUTE[1][n]) for n in range(3)]
        own = after(vec_other, keep)[None]
        one = send(own, late_steps[0])
        sums = keep + send(give, PARTNER)
        pair = jnp.concatenate([own, one])
        pair = after(pair, sums)
        two = send(pair, late_steps[1])
        three = send(pair, late_steps[2])
        early = [
            send(after(jnp.concatenate([part[0][:2], part[1][:2]]), sums), PARTNER) for part in near
        ]
        count = sums.shape[0] // 2
        mine = lax.dynamic_slice_in_dim(sums, core * count, count)
        theirs = lax.dynamic_slice_in_dim(sums, (1 - core) * count, count)
        mine = mine + lax.ppermute(theirs, "prow", [(i, i ^ 1) for i in range(nprow)])
        nz = nprow // 2
        part = jnp.sum(along_z(mine.reshape(nz, count // nz, kb)), axis=0)
        part = after(part, two, *early)
        four = send(after(two, part), late_steps[2])
        last = [
            send(after(jnp.concatenate([part_[2][:2], part_[3][:2]]), part), PARTNER)
            for part_ in near
        ]
        whole = along_z(jnp.broadcast_to(part, (nz,) + part.shape)).reshape(count, kb)
        whole = after(whole, four, three, *last)
        sums = lax.all_gather(whole, "prow", axis=0, tiled=True, axis_index_groups=in_chip)
        rest = send(sums[nblk * rows :], PARTNER)
        far = tuple(zip(early, last))
        group = (pair, two, three, four)
        return update(order, late, info, sums, rest, factors, eig, near, group, far)

    return jax.shard_map(
        per_device, mesh=mesh, in_specs=placed, out_specs=P("pcol", "prow"), check_vma=False
    )
```

time: 513 us -> 189 us (0.37)
  blocking collectives: 459 us -> 2.48 us
  starting transfers between devices: 0.12 us -> 99.8 us
  waiting for transfers between devices: 1.96 us -> 49.4 us
  matrix products: 35.9 us -> 0 us
  Pallas kernels: 0 us -> 19.3 us
  between operations: 13.2 us -> 0.63 us
  local copies, waits for them, and re-layouts: 2.13 us -> 9.94 us
  other arithmetic: 0 us -> 6.54 us
    psum x4 -> x0, blocking collectives: 386 us -> none  [reduce_scale(): summed = lax.psum(partial_sums, 'prow')]
    ppermute x0 -> x23, starting transfers between devices: none -> 78.7 us  [the longest x22 69 us: send(): return lax.ppermute(x, ('prow', 'pcol'), pairs)]
    all_gather x4 -> x1, blocking collectives: 72.2 us -> 2.48 us  [per_device(): lax.all_gather(whole, 'prow', axis=0, tiled=True, axis_index_groups=in_chip)]
    ppermute x0 -> x23, waiting for transfers between devices: none -> 49.4 us  [the longest x22 49.2 us: send(): return lax.ppermute(x, ('prow', 'pcol'), pairs)]
    dot_general x12 -> x0, matrix products: 35.9 us -> none  [the longest x8 18.9 us: inner_rows(): lax.dot_general(left, right, (((1,), (1,)), ((), ())), precision=lax.Prec...]
    all_to_all x0 -> x2, starting transfers between devices: none -> 21.1 us  [along_z(): return lax.all_to_all(x, 'prow', 0, 0, axis_index_groups=groups)]
    pallas_call x0 -> x2, Pallas kernels: none -> 19.3 us  [the longest x1 10.6 us: update(): pl.pallas_call(update_kernel, out_shape=jax.ShapeDtypeStruct(eig.shape, F...]
    concatenate x0 -> x6, other arithmetic: none -> 5.57 us  [the longest x2 2.85 us: per_device(): jnp.concatenate([part[0][:2], part[1][:2]])]
  transfers between devices with their start and end apart: 4 -> 25, of which waited for: 0 -> 13; matrix products, arithmetic and copies ran while one was open for 5% -> 6% of each run, Pallas kernels for 0% -> 0%
where the time goes in v3:
time: 189 us; the launch traced here: 188 us
  starting transfers between devices  99.8 us (53%)
  waiting for transfers between devices  49.4 us (26%)
  Pallas kernels  19.3 us (10%)
  local copies, waits for them, and re-layouts  9.94 us (5%)
  other arithmetic  6.54 us (3%)
  blocking collectives  2.48 us (1%)
    ppermute x22, starting transfers between devices, send(): return lax.ppermute(x, ('prow', 'pcol'), pairs)  69 us
    ppermute x22, waiting for transfers between devices, send(): return lax.ppermute(x, ('prow', 'pcol'), pairs)  49.2 us
    all_to_all x2, starting transfers between devices, along_z(): return lax.all_to_all(x, 'prow', 0, 0, axis_index_groups=groups)  21.1 us
    pallas_call x1, Pallas kernels, update(): pl.pallas_call(update_kernel, out_shape=jax.ShapeDtypeStruct(eig.shape, F...  10.6 us
    ppermute x1, starting transfers between devices, per_device(): lax.ppermute(theirs, 'prow', [(i, i ^ 1) for i in range(nprow)])  9.77 us
    pallas_call x1, Pallas kernels, inner_sums(): pl.pallas_call(inner_kernel, out_shape=[out, out, jax.ShapeDtypeStruct((n...  8.73 us
  transfers between devices with their start and end apart: 25, of which 13 were waited for; matrix products, arithmetic and copies ran while one was open for 6% of the time, Pallas kernels for 0%

profile of v3, /device:TPU:1, one launch (start us, length us, event | category | flops | bytes accessed | tf_op | source)
XLA Modules:
  0.0 188.1 jit_solution(5121896534119264228)
XLA Ops:
  0.0 1.1 constant_dynamic-slice_fusion
  1.1 1.0 constant_dynamic-slice_fusion.3
  3.0 5.2 %collective-permute-start = (f32[4,8,2560]{2,1,0:T(8,128)S(1)}, f32[4,8,2560]{2,1,0:T(8,128)S(1)}, u32[]{:S(2)}, u32[]{:S(2)}) collective-permute-start(f32[4,8,2560]{2,1,0:T(8,128)S(1)} %pad_maximum_fusion.7), channel_id=1, source_target_pairs={{0,3},{1,2},{2,1},{3,0},{4,7},{5,6},{6,5},{7,4},{8,11},{9,10},{10,... | collective-permute-start | bytes 983048 | tf_op jit(solution)/shard_map/ppermute | solution.py:309
  8.2 1.9 %collective-permute-start.2 = (f32[4,8,1280]{2,1,0:T(8,128)S(1)}, f32[4,8,1280]{2,1,0:T(8,128)S(1)}, u32[]{:S(2)}, u32[]{:S(2)}) collective-permute-start(f32[4,8,1280]{2,1,0:T(8,128)S(1)} %get-tuple-element.44), channel_id=1, source_target_pairs={{0,1},{1,0},{2,3},{3,2},{4,5},{5,4},{6,7},{7,6},{8,9},{9,8},{10,11... | collective-permute-start | bytes 491528 | tf_op jit(solution)/shard_map/ppermute | solution.py:309
  10.2 4.6 %collective-permute-start.7 = (f32[4,8,1280]{2,1,0:T(8,128)S(1)}, f32[4,8,1280]{2,1,0:T(8,128)S(1)}, u32[]{:S(2)}, u32[]{:S(2)}) collective-permute-start(f32[4,8,1280]{2,1,0:T(8,128)S(1)} %get-tuple-element.35), channel_id=1, source_target_pairs={{0,12},{1,13},{2,14},{3,15},{4,8},{5,9},{6,10},{7,11},{8,4},{9,5},... | collective-permute-start | bytes 491528 | tf_op jit(solution)/shard_map/ppermute | solution.py:309
  14.9 2.9 %collective-permute-start.8 = (f32[4,8,1280]{2,1,0:T(8,128)S(1)}, f32[4,8,1280]{2,1,0:T(8,128)S(1)}, u32[]{:S(2)}, u32[]{:S(2)}) collective-permute-start(f32[4,8,1280]{2,1,0:T(8,128)S(1)} %get-tuple-element.41), channel_id=1, source_target_pairs={{0,12},{1,13},{2,14},{3,15},{4,8},{5,9},{6,10},{7,11},{8,4},{9,5},... | collective-permute-start | bytes 491528 | tf_op jit(solution)/shard_map/ppermute | solution.py:309
  17.9 2.4 %collective-permute-start.3 = (f32[4,8,1280]{2,1,0:T(8,128)S(1)}, f32[4,8,1280]{2,1,0:T(8,128)S(1)}, u32[]{:S(2)}, u32[]{:S(2)}) collective-permute-start(f32[4,8,1280]{2,1,0:T(8,128)S(1)} %get-tuple-element.42), channel_id=1, source_target_pairs={{0,1},{1,0},{2,3},{3,2},{4,5},{5,4},{6,7},{7,6},{8,9},{9,8},{10,11... | collective-permute-start | bytes 491528 | tf_op jit(solution)/shard_map/ppermute | solution.py:309
  20.3 4.0 %collective-permute-start.1 = (f32[96,2432]{1,0:T(8,128)S(1)}, f32[96,2432]{1,0:T(8,128)S(1)}, u32[]{:S(2)}, u32[]{:S(2)}) collective-permute-start(f32[96,2432]{1,0:T(8,128)S(1)} %constant_dynamic-slice_fusion.5), channel_id=1, source_target_pairs={{0,3},{1,2},{2,1},{3,0},{4,7},{5,6},{6,5},{7,4},{8,11},{9,10},{10,... | collective-permute-start | bytes 2801672 | tf_op jit(solution)/shard_map/ppermute | solution.py:309
  24.4 2.8 %collective-permute-start.9 = (f32[4,4,8,1280]{3,2,1,0:T(8,128)S(1)}, f32[4,4,8,1280]{3,2,1,0:T(8,128)S(1)}, u32[]{:S(2)}, u32[]{:S(2)}) collective-permute-start(f32[4,4,8,1280]{3,2,1,0:T(8,128)S(1)} %pad_maximum_fusion.2.refs_4_), channel_id=1, source_target_pairs={{0,1},{1,0},{2,3},{3,2},{4,5},{5,4},{6,7},{7,6},{8,9},{9,8},{10,11... | collective-permute-start | bytes 1966088 | tf_op jit(solution)/shard_map/ppermute | solution.py:309
  27.2 1.9 %collective-permute-start.4 = (f32[4,4,8,1280]{3,2,1,0:T(8,128)S(1)}, f32[4,4,8,1280]{3,2,1,0:T(8,128)S(1)}, u32[]{:S(2)}, u32[]{:S(2)}) collective-permute-start(f32[4,4,8,1280]{3,2,1,0:T(8,128)S(1)} %pad_maximum_fusion.refs_0_), channel_id=1, source_target_pairs={{0,4},{1,5},{2,6},{3,7},{4,0},{5,1},{6,2},{7,3},{8,12},{9,13},{10,... | collective-permute-start | bytes 1966088 | tf_op jit(solution)/shard_map/ppermute | solution.py:309
  29.2 3.4 %collective-permute-start.10 = (f32[4,4,8,1280]{3,2,1,0:T(8,128)S(1)}, f32[4,4,8,1280]{3,2,1,0:T(8,128)S(1)}, u32[]{:S(2)}, u32[]{:S(2)}) collective-permute-start(f32[4,4,8,1280]{3,2,1,0:T(8,128)S(1)} %pad_maximum_fusion.2.refs_4_), channel_id=1, source_target_pairs={{0,4},{1,5},{2,6},{3,7},{4,0},{5,1},{6,2},{7,3},{8,12},{9,13},{10,... | collective-permute-start | bytes 1966088 | tf_op jit(solution)/shard_map/ppermute | solution.py:309
  32.5 1.9 %collective-permute-start.5 = (f32[4,4,8,1280]{3,2,1,0:T(8,128)S(1)}, f32[4,4,8,1280]{3,2,1,0:T(8,128)}, u32[]{:S(2)}, u32[]{:S(2)}) collective-permute-start(f32[4,4,8,1280]{3,2,1,0:T(8,128)S(1)} %pad_maximum_fusion.refs_0_), channel_id=1, source_target_pairs={{0,12},{1,13},{2,14},{3,15},{4,8},{5,9},{6,10},{7,11},{8,4},{9,5},... | collective-permute-start | bytes 1966088 | tf_op jit(solution)/shard_map/ppermute | solution.py:309
  34.5 1.5 collective-permute-done.9.refs_5_
  36.0 1.9 collective-permute-done.1.mate_ref
  37.9 2.1 %collective-permute-done.4.refs_1_ = f32[4,4,8,1280]{3,2,1,0:T(8,128)S(1)} collective-permute-done((f32[4,4,8,1280]{3,2,1,0:T(8,128)S(1)}, f32[4,4,8,1280]{3,2,1,0:T(8,128)S(1)}, u32[]{:S(2)}, u32[]{:S(2)}) %collective-permute-start.4) | collective-permute-done | bytes 655392 | tf_op jit(solution)/shard_map/ppermute | solution.py:309
  40.0 3.3 %collective-permute-start.6 = (f32[4,4,8,1280]{3,2,1,0:T(8,128)S(1)}, f32[4,4,8,1280]{3,2,1,0:T(8,128)}, u32[]{:S(2)}, u32[]{:S(2)}) collective-permute-start(f32[4,4,8,1280]{3,2,1,0:T(8,128)S(1)} %collective-permute-done.4.refs_1_), channel_id=1, source_target_pairs={{0,12},{1,13},{2,14},{3,15},{4,8},{5,9},{6,10},{7,11},{8,4},{9,5},... | collective-permute-start | bytes 1966088 | tf_op jit(solution)/shard_map/ppermute | solution.py:309
  43.3 1.9 %collective-permute-start.11 = (f32[4,4,8,1280]{3,2,1,0:T(8,128)S(1)}, f32[4,4,8,1280]{3,2,1,0:T(8,128)}, u32[]{:S(2)}, u32[]{:S(2)}) collective-permute-start(f32[4,4,8,1280]{3,2,1,0:T(8,128)S(1)} %collective-permute-done.9.refs_5_), channel_id=1, source_target_pairs={{0,4},{1,5},{2,6},{3,7},{4,0},{5,1},{6,2},{7,3},{8,12},{9,13},{10,... | collective-permute-start | bytes 1966088 | tf_op jit(solution)/shard_map/ppermute | solution.py:309
  45.3 7.7 %collective-permute-done.10.refs_6_ = f32[4,4,8,1280]{3,2,1,0:T(8,128)S(1)} collective-permute-done((f32[4,4,8,1280]{3,2,1,0:T(8,128)S(1)}, f32[4,4,8,1280]{3,2,1,0:T(8,128)S(1)}, u32[]{:S(2)}, u32[]{:S(2)}) %collective-permute-start.10) | collective-permute-done | bytes 655392 | tf_op jit(solution)/shard_map/ppermute | solution.py:309
  53.0 3.4 %collective-permute-done.6.refs_3_ = f32[4,4,8,1280]{3,2,1,0:T(8,128)} collective-permute-done((f32[4,4,8,1280]{3,2,1,0:T(8,128)S(1)}, f32[4,4,8,1280]{3,2,1,0:T(8,128)}, u32[]{:S(2)}, u32[]{:S(2)}) %collective-permute-start.6) | collective-permute-done | bytes 655392 | tf_op jit(solution)/shard_map/ppermute | solution.py:309
  56.4 3.6 %collective-permute-done.11.refs_7_ = f32[4,4,8,1280]{3,2,1,0:T(8,128)} collective-permute-done((f32[4,4,8,1280]{3,2,1,0:T(8,128)S(1)}, f32[4,4,8,1280]{3,2,1,0:T(8,128)}, u32[]{:S(2)}, u32[]{:S(2)}) %collective-permute-start.11) | collective-permute-done | bytes 655392 | tf_op jit(solution)/shard_map/ppermute | solution.py:309
  60.0 8.7 %inner_sums.1 = (f32[768,128]{1,0:T(8,128)S(1)}, f32[768,128]{1,0:T(8,128)S(1)}, f32[4,128,128]{2,1,0:T(8,128)S(1)}) custom-call(s32[2,16]{1,0:T(2,128)S(1)} %select_xor_fusion.1.order_ref, s32[2]{0:T(128)S(1)} %pad_add_fusion.info_ref, f32[96,4864]{1,0:T(8,128)} %eig_ref.3, f32[96,2432]{1,0:T(8,128)} %copy-done.23, ...), custom_call_target="tpu_custom_call" | custom-call | flops 2868903936 | bytes 6848512 | tf_op jit(solution)/shard_map/inner_sums/pallas_call | solution.py:166
  68.8 4.3 %collective-permute-start.12 = (f32[768,128]{1,0:T(8,128)S(1)}, f32[768,128]{1,0:T(8,128)S(1)}, u32[]{:S(2)}, u32[]{:S(2)}) collective-permute-start(f32[768,128]{1,0:T(8,128)S(1)} %get-tuple-element.24), channel_id=1, source_target_pairs={{0,3},{1,2},{2,1},{3,0},{4,7},{5,6},{6,5},{7,4},{8,11},{9,10},{10,... | collective-permute-start | bytes 1179656 | tf_op jit(solution)/shard_map/ppermute | solution.py:309
  73.1 1.0 slice.59
  74.1 1.0 slice.58
  75.2 2.0 %fusion.1 = f32[4,4,8,1280]{3,2,1,0:T(8,128)} fusion(f32[1,4,8,1280]{3,2,1,0:T(8,128)} %bitcast.24, f32[1,4,8,1280]{3,2,1,0:T(8,128)} %bitcast.17, f32[2,4,8,1280]{3,2,1,0:T(8,128)S(1)} %slice.59), kind=kLoop, calls=%fused_computation.5 | loop fusion | flops 327680 | bytes 1310720 | tf_op jit(solution)/shard_map/concatenate | solution.py:369
  77.1 1.9 %collective-permute-start.14 = (f32[1,4,8,2560]{3,2,1,0:T(8,128)S(1)}, f32[1,4,8,2560]{3,2,1,0:T(8,128)}, u32[]{:S(2)}, u32[]{:S(2)}) collective-permute-start(f32[1,4,8,2560]{3,2,1,0:T(8,128)S(1)} %bitcast.18), channel_id=1, source_target_pairs={{0,1},{1,0},{2,3},{3,2},{4,5},{5,4},{6,7},{7,6},{8,9},{9,8},{10,11... | collective-permute-start | bytes 983048 | tf_op jit(solution)/shard_map/ppermute | solution.py:309
  79.1 9.8 %collective-permute-start.13 = (f32[384,128]{1,0:T(8,128)S(1)}, f32[384,128]{1,0:T(8,128)S(1)}, u32[]{:S(2)}, u32[]{:S(2)}) collective-permute-start(f32[384,128]{1,0:T(8,128)S(1)} %constant_dynamic-slice_fusion.2), channel_id=1, source_target_pairs={{0,16},{16,0},{32,48},{48,32},{64,80},{80,64},{96,112},{112,96},{1... | collective-permute-start | bytes 589832 | tf_op jit(solution)/shard_map/ppermute | solution.py:374
  90.6 9.4 %all-to-all-start = ((f32[16,24,128]{2,1,0:T(8,128)}), f32[16,24,128]{2,1,0:T(8,128)S(1)}, u32[]{:S(2)}, u32[]{:S(2)}) async-start(f32[16,24,128]{2,1,0:T(8,128)} %bitcast.10), calls=%async_computation | async-start | bytes 393216 | tf_op jit(solution)/shard_map/all_to_all | solution.py:323
  100.0 1.0 pad_maximum_fusion.4.refs_8_
  101.1 4.6 %collective-permute-start.15 = (f32[2,4,8,2560]{3,2,1,0:T(8,128)S(1)}, f32[2,4,8,2560]{3,2,1,0:T(8,128)S(1)}, u32[]{:S(2)}, u32[]{:S(2)}) collective-permute-start(f32[2,4,8,2560]{3,2,1,0:T(8,128)S(1)} %pad_maximum_fusion.4.refs_8_), channel_id=1, source_target_pairs={{0,12},{1,13},{2,14},{3,15},{4,8},{5,9},{6,10},{7,11},{8,4},{9,5},... | collective-permute-start | bytes 1966088 | tf_op jit(solution)/shard_map/ppermute | solution.py:309
  105.7 2.1 %collective-permute-start.16 = (f32[4,4,8,1280]{3,2,1,0:T(8,128)}, f32[4,4,8,1280]{3,2,1,0:T(8,128)}, u32[]{:S(2)}, u32[]{:S(2)}) collective-permute-start(f32[4,4,8,1280]{3,2,1,0:T(8,128)} %fusion), channel_id=1, source_target_pairs={{0,3},{1,2},{2,1},{3,0},{4,7},{5,6},{6,5},{7,4},{8,11},{9,10},{10,... | collective-permute-start | bytes 1966088 | tf_op jit(solution)/shard_map/ppermute | solution.py:309
  107.8 4.4 %collective-permute-start.17 = (f32[4,4,8,1280]{3,2,1,0:T(8,128)}, f32[4,4,8,1280]{3,2,1,0:T(8,128)}, u32[]{:S(2)}, u32[]{:S(2)}) collective-permute-start(f32[4,4,8,1280]{3,2,1,0:T(8,128)} %fusion.1), channel_id=1, source_target_pairs={{0,3},{1,2},{2,1},{3,0},{4,7},{5,6},{6,5},{7,4},{8,11},{9,10},{10,... | collective-permute-start | bytes 1966088 | tf_op jit(solution)/shard_map/ppermute | solution.py:309
  112.2 1.0 slice.60
  113.2 1.0 slice.61
  114.3 1.0 slice.63
  116.4 5.7 %collective-permute-done.16.refs_12_ = f32[4,4,8,1280]{3,2,1,0:T(8,128)} collective-permute-done((f32[4,4,8,1280]{3,2,1,0:T(8,128)}, f32[4,4,8,1280]{3,2,1,0:T(8,128)}, u32[]{:S(2)}, u32[]{:S(2)}) %collective-permute-start.16) | collective-permute-done | bytes 655392 | tf_op jit(solution)/shard_map/ppermute | solution.py:309
  122.1 6.7 %collective-permute-done.17.refs_14_ = f32[4,4,8,1280]{3,2,1,0:T(8,128)} collective-permute-done((f32[4,4,8,1280]{3,2,1,0:T(8,128)}, f32[4,4,8,1280]{3,2,1,0:T(8,128)}, u32[]{:S(2)}, u32[]{:S(2)}) %collective-permute-start.17) | collective-permute-done | bytes 655392 | tf_op jit(solution)/shard_map/ppermute | solution.py:309
  129.6 11.7 %all-to-all-start.1 = ((f32[16,24,128]{2,1,0:T(8,128)}), f32[16,24,128]{2,1,0:T(8,128)S(1)}, u32[]{:S(2)}, u32[]{:S(2)}) async-start(f32[16,24,128]{2,1,0:T(8,128)} %broadcast_in_dim.7), calls=%async_computation.1 | async-start | bytes 393216 | tf_op jit(solution)/shard_map/all_to_all | solution.py:323
  141.4 3.6 %collective-permute-start.19 = (f32[2,4,8,2560]{3,2,1,0:T(8,128)S(1)}, f32[2,4,8,2560]{3,2,1,0:T(8,128)S(1)}, u32[]{:S(2)}, u32[]{:S(2)}) collective-permute-start(f32[2,4,8,2560]{3,2,1,0:T(8,128)S(1)} %pad_maximum_fusion.4.refs_8_), channel_id=1, source_target_pairs={{0,4},{1,5},{2,6},{3,7},{4,0},{5,1},{6,2},{7,3},{8,12},{9,13},{10,... | collective-permute-start | bytes 1966088 | tf_op jit(solution)/shard_map/ppermute | solution.py:309
  145.0 1.9 %collective-permute-start.18 = (f32[2,4,8,2560]{3,2,1,0:T(8,128)S(1)}, f32[2,4,8,2560]{3,2,1,0:T(8,128)S(1)}, u32[]{:S(2)}, u32[]{:S(2)}) collective-permute-start(f32[2,4,8,2560]{3,2,1,0:T(8,128)S(1)} %collective-permute-done.15.refs_9_), channel_id=1, source_target_pairs={{0,4},{1,5},{2,6},{3,7},{4,0},{5,1},{6,2},{7,3},{8,12},{9,13},{10,... | collective-permute-start | bytes 1966088 | tf_op jit(solution)/shard_map/ppermute | solution.py:309
  147.0 3.2 %collective-permute-start.20 = (f32[4,4,8,1280]{3,2,1,0:T(8,128)}, f32[4,4,8,1280]{3,2,1,0:T(8,128)S(1)}, u32[]{:S(2)}, u32[]{:S(2)}) collective-permute-start(f32[4,4,8,1280]{3,2,1,0:T(8,128)} %pad_maximum_fusion.5), channel_id=1, source_target_pairs={{0,3},{1,2},{2,1},{3,0},{4,7},{5,6},{6,5},{7,4},{8,11},{9,10},{10,... | collective-permute-start | bytes 1966088 | tf_op jit(solution)/shard_map/ppermute | solution.py:309
  150.1 3.3 %collective-permute-start.21 = (f32[4,4,8,1280]{3,2,1,0:T(8,128)S(1)}, f32[4,4,8,1280]{3,2,1,0:T(8,128)}, u32[]{:S(2)}, u32[]{:S(2)}) collective-permute-start(f32[4,4,8,1280]{3,2,1,0:T(8,128)S(1)} %pad_maximum_fusion.6), channel_id=1, source_target_pairs={{0,3},{1,2},{2,1},{3,0},{4,7},{5,6},{6,5},{7,4},{8,11},{9,10},{10,... | collective-permute-start | bytes 1966088 | tf_op jit(solution)/shard_map/ppermute | solution.py:309
  153.5 6.8 %collective-permute-done.18.refs_11_ = f32[2,4,8,2560]{3,2,1,0:T(8,128)S(1)} collective-permute-done((f32[2,4,8,2560]{3,2,1,0:T(8,128)S(1)}, f32[2,4,8,2560]{3,2,1,0:T(8,128)S(1)}, u32[]{:S(2)}, u32[]{:S(2)}) %collective-permute-start.18) | collective-permute-done | bytes 655392 | tf_op jit(solution)/shard_map/ppermute | solution.py:309
  162.1 5.0 %collective-permute-done.21.refs_15_ = f32[4,4,8,1280]{3,2,1,0:T(8,128)} collective-permute-done((f32[4,4,8,1280]{3,2,1,0:T(8,128)S(1)}, f32[4,4,8,1280]{3,2,1,0:T(8,128)}, u32[]{:S(2)}, u32[]{:S(2)}) %collective-permute-start.21) | collective-permute-done | bytes 655392 | tf_op jit(solution)/shard_map/ppermute | solution.py:309
  167.1 2.5 %all_gather.3.sum_ref = f32[768,128]{1,0:T(8,128)S(1)} all-gather(f32[384,128]{1,0:T(8,128)S(1)} %bitcast.20), channel_id=1, replica_groups={{0,16},{32,48},{64,80},{96,112},{128,144},{160,176},{192,208},{224,240}..., dimensions={0}, use_global_device_ids=true | all-gather | bytes 589824 | tf_op jit(solution)/shard_map/all_gather | solution.py:385
  169.6 3.4 %collective-permute-start.22 = (f32[384,128]{1,0:T(8,128)S(1)}, f32[384,128]{1,0:T(8,128)S(1)}, u32[]{:S(2)}, u32[]{:S(2)}) collective-permute-start(f32[384,128]{1,0:T(8,128)S(1)} %slice.64), channel_id=1, source_target_pairs={{0,3},{1,2},{2,1},{3,0},{4,7},{5,6},{6,5},{7,4},{8,11},{9,10},{10,... | collective-permute-start | bytes 589832 | tf_op jit(solution)/shard_map/ppermute | solution.py:309
  173.1 4.5 %collective-permute-done.22.rest_ref = f32[384,128]{1,0:T(8,128)S(1)} collective-permute-done((f32[384,128]{1,0:T(8,128)S(1)}, f32[384,128]{1,0:T(8,128)S(1)}, u32[]{:S(2)}, u32[]{:S(2)}) %collective-permute-start.22) | collective-permute-done | bytes 196640 | tf_op jit(solution)/shard_map/ppermute | solution.py:309
  177.5 10.6 %update.1 = f32[96,4864]{1,0:T(8,128)} custom-call(s32[2,16]{1,0:T(2,128)S(1)} %select_xor_fusion.1.order_ref, s32[3,16]{1,0:T(4,128)S(1)} %select_xor_fusion.late_ref, s32[2]{0:T(128)S(1)} %pad_add_fusion.info_ref, f32[768,128]{1,0:T(8,128)S(1)} %all_gather.3.sum_ref, f32[384,128]{1,0:T(8,128)S(1)} %collective-permute-done.22.rest_ref, ...), custom_call_target="tpu_custom_call" | custom-call | flops 1434451968 | bytes 13697024 | tf_op jit(solution)/shard_map/update/pallas_call | solution.py:266
  (82 shorter events, 6.7 us)
Async XLA Ops:
  0.0 8.2 %copy-start.18 = (f32[4,8,128]{2,1,0:T(8,128)S(1)}, f32[4,8,128]{2,1,0:T(8,128)}, u32[]{:S(2)}) copy-start(f32[4,8,128]{2,1,0:T(8,128)} %param.9) | copy-start | bytes 49156
  0.0 17.8 %copy-start = (f32[96,4864]{1,0:T(8,128)S(1)}, f32[96,4864]{1,0:T(8,128)}, u32[]{:S(2)}) copy-start(f32[96,4864]{1,0:T(8,128)} %eig_ref.3) | copy-start | bytes 5603332
  2.2 22.1 %copy-start.6 = (f32[4,8,1280]{2,1,0:T(8,128)}, f32[4,8,1280]{2,1,0:T(8,128)S(1)}, u32[]{:S(2)}) copy-start(f32[4,8,1280]{2,1,0:T(8,128)S(1)} %get-tuple-element.35) | copy-start | bytes 491524
  3.0 21.4 %copy-start.9 = (f32[4,8,2560]{2,1,0:T(8,128)}, f32[4,8,2560]{2,1,0:T(8,128)S(1)}, u32[]{:S(2)}) copy-start(f32[4,8,2560]{2,1,0:T(8,128)S(1)} %pad_maximum_fusion.7) | copy-start | bytes 983044
  3.0 11.9 %collective-permute-start = (f32[4,8,2560]{2,1,0:T(8,128)S(1)}, f32[4,8,2560]{2,1,0:T(8,128)S(1)}, u32[]{:S(2)}, u32[]{:S(2)}) collective-permute-start(f32[4,8,2560]{2,1,0:T(8,128)S(1)} %pad_maximum_fusion.7), channel_id=1, source_target_pairs={{0,3},{1,2},{2,1},{3,0},{4,7},{5,6},{6,5},{7,4},{8,11},{9,10},{10,... | collective-permute-start | bytes 983048 | tf_op jit(solution)/shard_map/ppermute | solution.py:309
  8.2 18.9 %copy-start.7 = (f32[1,4,8,1280]{3,2,1,0:T(8,128)}, f32[1,4,8,1280]{3,2,1,0:T(8,128)S(1)}, u32[]{:S(2)}) copy-start(f32[1,4,8,1280]{3,2,1,0:T(8,128)S(1)} %get-tuple-element.43) | copy-start | bytes 491524
  8.2 18.9 %collective-permute-start.2 = (f32[4,8,1280]{2,1,0:T(8,128)S(1)}, f32[4,8,1280]{2,1,0:T(8,128)S(1)}, u32[]{:S(2)}, u32[]{:S(2)}) collective-permute-start(f32[4,8,1280]{2,1,0:T(8,128)S(1)} %get-tuple-element.44), channel_id=1, source_target_pairs={{0,1},{1,0},{2,3},{3,2},{4,5},{5,4},{6,7},{7,6},{8,9},{9,8},{10,11... | collective-permute-start | bytes 491528 | tf_op jit(solution)/shard_map/ppermute | solution.py:309
  10.2 14.1 %collective-permute-start.7 = (f32[4,8,1280]{2,1,0:T(8,128)S(1)}, f32[4,8,1280]{2,1,0:T(8,128)S(1)}, u32[]{:S(2)}, u32[]{:S(2)}) collective-permute-start(f32[4,8,1280]{2,1,0:T(8,128)S(1)} %get-tuple-element.35), channel_id=1, source_target_pairs={{0,12},{1,13},{2,14},{3,15},{4,8},{5,9},{6,10},{7,11},{8,4},{9,5},... | collective-permute-start | bytes 491528 | tf_op jit(solution)/shard_map/ppermute | solution.py:309
  14.9 30.4 %copy-start.21 = (s32[2,16]{1,0:T(2,128)S(1)}, s32[2,16]{1,0:T(2,128)}, u32[]{:S(2)}) copy-start(s32[2,16]{1,0:T(2,128)} %constant.37.clone) | copy-start | bytes 388
  14.9 30.4 %copy-start.22 = (s32[2,16]{1,0:T(2,128)S(1)}, s32[2,16]{1,0:T(2,128)}, u32[]{:S(2)}) copy-start(s32[2,16]{1,0:T(2,128)} %constant.36.clone) | copy-start | bytes 388
  14.9 9.4 %collective-permute-start.8 = (f32[4,8,1280]{2,1,0:T(8,128)S(1)}, f32[4,8,1280]{2,1,0:T(8,128)S(1)}, u32[]{:S(2)}, u32[]{:S(2)}) collective-permute-start(f32[4,8,1280]{2,1,0:T(8,128)S(1)} %get-tuple-element.41), channel_id=1, source_target_pairs={{0,12},{1,13},{2,14},{3,15},{4,8},{5,9},{6,10},{7,11},{8,4},{9,5},... | collective-permute-start | bytes 491528 | tf_op jit(solution)/shard_map/ppermute | solution.py:309
  17.9 9.2 %collective-permute-start.3 = (f32[4,8,1280]{2,1,0:T(8,128)S(1)}, f32[4,8,1280]{2,1,0:T(8,128)S(1)}, u32[]{:S(2)}, u32[]{:S(2)}) collective-permute-start(f32[4,8,1280]{2,1,0:T(8,128)S(1)} %get-tuple-element.42), channel_id=1, source_target_pairs={{0,1},{1,0},{2,3},{3,2},{4,5},{5,4},{6,7},{7,6},{8,9},{9,8},{10,11... | collective-permute-start | bytes 491528 | tf_op jit(solution)/shard_map/ppermute | solution.py:309
  20.3 17.6 %collective-permute-start.1 = (f32[96,2432]{1,0:T(8,128)S(1)}, f32[96,2432]{1,0:T(8,128)S(1)}, u32[]{:S(2)}, u32[]{:S(2)}) collective-permute-start(f32[96,2432]{1,0:T(8,128)S(1)} %constant_dynamic-slice_fusion.5), channel_id=1, source_target_pairs={{0,3},{1,2},{2,1},{3,0},{4,7},{5,6},{6,5},{7,4},{8,11},{9,10},{10,... | collective-permute-start | bytes 2801672 | tf_op jit(solution)/shard_map/ppermute | solution.py:309
  24.3 2.9 %copy-start.17 = (f32[4,8,1280]{2,1,0:T(8,128)}, f32[4,8,1280]{2,1,0:T(8,128)S(1)}, u32[]{:S(2)}) copy-start(f32[4,8,1280]{2,1,0:T(8,128)S(1)} %collective-permute-done.7) | copy-start | bytes 491524
  24.4 35.7 %copy-start.1 = (f32[4,4,8,1280]{3,2,1,0:T(8,128)}, f32[4,4,8,1280]{3,2,1,0:T(8,128)S(1)}, u32[]{:S(2)}) copy-start(f32[4,4,8,1280]{3,2,1,0:T(8,128)S(1)} %pad_maximum_fusion.2.refs_4_) | copy-start | bytes 1966084
  24.4 11.6 %collective-permute-start.9 = (f32[4,4,8,1280]{3,2,1,0:T(8,128)S(1)}, f32[4,4,8,1280]{3,2,1,0:T(8,128)S(1)}, u32[]{:S(2)}, u32[]{:S(2)}) collective-permute-start(f32[4,4,8,1280]{3,2,1,0:T(8,128)S(1)} %pad_maximum_fusion.2.refs_4_), channel_id=1, source_target_pairs={{0,1},{1,0},{2,3},{3,2},{4,5},{5,4},{6,7},{7,6},{8,9},{9,8},{10,11... | collective-permute-start | bytes 1966088 | tf_op jit(solution)/shard_map/ppermute | solution.py:309
  27.1 12.8 %copy-start.15 = (f32[4,8,1280]{2,1,0:T(8,128)}, f32[4,8,1280]{2,1,0:T(8,128)S(1)}, u32[]{:S(2)}) copy-start(f32[4,8,1280]{2,1,0:T(8,128)S(1)} %collective-permute-done.2) | copy-start | bytes 491524
  27.2 12.7 %collective-permute-start.4 = (f32[4,4,8,1280]{3,2,1,0:T(8,128)S(1)}, f32[4,4,8,1280]{3,2,1,0:T(8,128)S(1)}, u32[]{:S(2)}, u32[]{:S(2)}) collective-permute-start(f32[4,4,8,1280]{3,2,1,0:T(8,128)S(1)} %pad_maximum_fusion.refs_0_), channel_id=1, source_target_pairs={{0,4},{1,5},{2,6},{3,7},{4,0},{5,1},{6,2},{7,3},{8,12},{9,13},{10,... | collective-permute-start | bytes 1966088 | tf_op jit(solution)/shard_map/ppermute | solution.py:309
  29.2 23.8 %collective-permute-start.10 = (f32[4,4,8,1280]{3,2,1,0:T(8,128)S(1)}, f32[4,4,8,1280]{3,2,1,0:T(8,128)S(1)}, u32[]{:S(2)}, u32[]{:S(2)}) collective-permute-start(f32[4,4,8,1280]{3,2,1,0:T(8,128)S(1)} %pad_maximum_fusion.2.refs_4_), channel_id=1, source_target_pairs={{0,4},{1,5},{2,6},{3,7},{4,0},{5,1},{6,2},{7,3},{8,12},{9,13},{10,... | collective-permute-start | bytes 1966088 | tf_op jit(solution)/shard_map/ppermute | solution.py:309
  32.5 20.5 %collective-permute-start.5 = (f32[4,4,8,1280]{3,2,1,0:T(8,128)S(1)}, f32[4,4,8,1280]{3,2,1,0:T(8,128)}, u32[]{:S(2)}, u32[]{:S(2)}) collective-permute-start(f32[4,4,8,1280]{3,2,1,0:T(8,128)S(1)} %pad_maximum_fusion.refs_0_), channel_id=1, source_target_pairs={{0,12},{1,13},{2,14},{3,15},{4,8},{5,9},{6,10},{7,11},{8,4},{9,5},... | collective-permute-start | bytes 1966088 | tf_op jit(solution)/shard_map/ppermute | solution.py:309
  36.0 24.0 %copy-start.3 = (f32[4,4,8,1280]{3,2,1,0:T(8,128)}, f32[4,4,8,1280]{3,2,1,0:T(8,128)S(1)}, u32[]{:S(2)}) copy-start(f32[4,4,8,1280]{3,2,1,0:T(8,128)S(1)} %collective-permute-done.9.refs_5_) | copy-start | bytes 1966084
  37.9 5.4 %copy-start.23 = (f32[96,2432]{1,0:T(8,128)}, f32[96,2432]{1,0:T(8,128)S(1)}, u32[]{:S(2)}) copy-start(f32[96,2432]{1,0:T(8,128)S(1)} %collective-permute-done.1.mate_ref) | copy-start | bytes 2801668
  40.0 16.4 %copy-start.4 = (f32[4,4,8,1280]{3,2,1,0:T(8,128)}, f32[4,4,8,1280]{3,2,1,0:T(8,128)S(1)}, u32[]{:S(2)}) copy-start(f32[4,4,8,1280]{3,2,1,0:T(8,128)S(1)} %collective-permute-done.4.refs_1_) | copy-start | bytes 1966084
  40.0 16.4 %collective-permute-start.6 = (f32[4,4,8,1280]{3,2,1,0:T(8,128)S(1)}, f32[4,4,8,1280]{3,2,1,0:T(8,128)}, u32[]{:S(2)}, u32[]{:S(2)}) collective-permute-start(f32[4,4,8,1280]{3,2,1,0:T(8,128)S(1)} %collective-permute-done.4.refs_1_), channel_id=1, source_target_pairs={{0,12},{1,13},{2,14},{3,15},{4,8},{5,9},{6,10},{7,11},{8,4},{9,5},... | collective-permute-start | bytes 1966088 | tf_op jit(solution)/shard_map/ppermute | solution.py:309
  43.3 16.7 %collective-permute-start.11 = (f32[4,4,8,1280]{3,2,1,0:T(8,128)S(1)}, f32[4,4,8,1280]{3,2,1,0:T(8,128)}, u32[]{:S(2)}, u32[]{:S(2)}) collective-permute-start(f32[4,4,8,1280]{3,2,1,0:T(8,128)S(1)} %collective-permute-done.9.refs_5_), channel_id=1, source_target_pairs={{0,4},{1,5},{2,6},{3,7},{4,0},{5,1},{6,2},{7,3},{8,12},{9,13},{10,... | collective-permute-start | bytes 1966088 | tf_op jit(solution)/shard_map/ppermute | solution.py:309
  53.0 3.4 %copy-start.5 = (f32[4,4,8,1280]{3,2,1,0:T(8,128)}, f32[4,4,8,1280]{3,2,1,0:T(8,128)S(1)}, u32[]{:S(2)}) copy-start(f32[4,4,8,1280]{3,2,1,0:T(8,128)S(1)} %collective-permute-done.10.refs_6_) | copy-start | bytes 1966084
  68.8 8.3 %copy-start.10 = (f32[4,8,2560]{2,1,0:T(8,128)S(1)}, f32[4,8,2560]{2,1,0:T(8,128)}, u32[]{:S(2)}) copy-start(f32[4,8,2560]{2,1,0:T(8,128)} %copy-done.9) | copy-start | bytes 983044
  68.8 10.2 %collective-permute-start.12 = (f32[768,128]{1,0:T(8,128)S(1)}, f32[768,128]{1,0:T(8,128)S(1)}, u32[]{:S(2)}, u32[]{:S(2)}) collective-permute-start(f32[768,128]{1,0:T(8,128)S(1)} %get-tuple-element.24), channel_id=1, source_target_pairs={{0,3},{1,2},{2,1},{3,0},{4,7},{5,6},{6,5},{7,4},{8,11},{9,10},{10,... | collective-permute-start | bytes 1179656 | tf_op jit(solution)/shard_map/ppermute | solution.py:309
  74.1 14.8 %copy-start.8 = (f32[1,4,8,1280]{3,2,1,0:T(8,128)S(1)}, f32[1,4,8,1280]{3,2,1,0:T(8,128)}, u32[]{:S(2)}) copy-start(f32[1,4,8,1280]{3,2,1,0:T(8,128)} %copy-done.7) | copy-start | bytes 491524
  74.1 14.8 %copy-start.16 = (f32[4,8,1280]{2,1,0:T(8,128)S(1)}, f32[4,8,1280]{2,1,0:T(8,128)}, u32[]{:S(2)}) copy-start(f32[4,8,1280]{2,1,0:T(8,128)} %copy-done.15) | copy-start | bytes 491524
  77.1 22.9 %collective-permute-start.14 = (f32[1,4,8,2560]{3,2,1,0:T(8,128)S(1)}, f32[1,4,8,2560]{3,2,1,0:T(8,128)}, u32[]{:S(2)}, u32[]{:S(2)}) collective-permute-start(f32[1,4,8,2560]{3,2,1,0:T(8,128)S(1)} %bitcast.18), channel_id=1, source_target_pairs={{0,1},{1,0},{2,3},{3,2},{4,5},{5,4},{6,7},{7,6},{8,9},{9,8},{10,11... | collective-permute-start | bytes 983048 | tf_op jit(solution)/shard_map/ppermute | solution.py:309
  79.1 10.8 %collective-permute-start.13 = (f32[384,128]{1,0:T(8,128)S(1)}, f32[384,128]{1,0:T(8,128)S(1)}, u32[]{:S(2)}, u32[]{:S(2)}) collective-permute-start(f32[384,128]{1,0:T(8,128)S(1)} %constant_dynamic-slice_fusion.2), channel_id=1, source_target_pairs={{0,16},{16,0},{32,48},{48,32},{64,80},{80,64},{96,112},{112,96},{1... | collective-permute-start | bytes 589832 | tf_op jit(solution)/shard_map/ppermute | solution.py:374
  90.6 25.5 %all-to-all-start = ((f32[16,24,128]{2,1,0:T(8,128)}), f32[16,24,128]{2,1,0:T(8,128)S(1)}, u32[]{:S(2)}, u32[]{:S(2)}) async-start(f32[16,24,128]{2,1,0:T(8,128)} %bitcast.10), calls=%async_computation | async-start | bytes 393216 | tf_op jit(solution)/shard_map/all_to_all | solution.py:323
  101.1 40.3 %copy-start.2 = (f32[2,4,8,2560]{3,2,1,0:T(8,128)}, f32[2,4,8,2560]{3,2,1,0:T(8,128)S(1)}, u32[]{:S(2)}) copy-start(f32[2,4,8,2560]{3,2,1,0:T(8,128)S(1)} %pad_maximum_fusion.4.refs_8_) | copy-start | bytes 1966084
  101.1 15.4 %collective-permute-start.15 = (f32[2,4,8,2560]{3,2,1,0:T(8,128)S(1)}, f32[2,4,8,2560]{3,2,1,0:T(8,128)S(1)}, u32[]{:S(2)}, u32[]{:S(2)}) collective-permute-start(f32[2,4,8,2560]{3,2,1,0:T(8,128)S(1)} %pad_maximum_fusion.4.refs_8_), channel_id=1, source_target_pairs={{0,12},{1,13},{2,14},{3,15},{4,8},{5,9},{6,10},{7,11},{8,4},{9,5},... | collective-permute-start | bytes 1966088 | tf_op jit(solution)/shard_map/ppermute | solution.py:309
  105.7 16.4 %collective-permute-start.16 = (f32[4,4,8,1280]{3,2,1,0:T(8,128)}, f32[4,4,8,1280]{3,2,1,0:T(8,128)}, u32[]{:S(2)}, u32[]{:S(2)}) collective-permute-start(f32[4,4,8,1280]{3,2,1,0:T(8,128)} %fusion), channel_id=1, source_target_pairs={{0,3},{1,2},{2,1},{3,0},{4,7},{5,6},{6,5},{7,4},{8,11},{9,10},{10,... | collective-permute-start | bytes 1966088 | tf_op jit(solution)/shard_map/ppermute | solution.py:309
  107.8 21.0 %collective-permute-start.17 = (f32[4,4,8,1280]{3,2,1,0:T(8,128)}, f32[4,4,8,1280]{3,2,1,0:T(8,128)}, u32[]{:S(2)}, u32[]{:S(2)}) collective-permute-start(f32[4,4,8,1280]{3,2,1,0:T(8,128)} %fusion.1), channel_id=1, source_target_pairs={{0,3},{1,2},{2,1},{3,0},{4,7},{5,6},{6,5},{7,4},{8,11},{9,10},{10,... | collective-permute-start | bytes 1966088 | tf_op jit(solution)/shard_map/ppermute | solution.py:309
  113.2 28.1 %slice-start = ((f32[4,4,8,1280]{3,2,1,0:T(8,128)}), f32[2,4,8,1280]{3,2,1,0:T(8,128)S(1)}, s32[]{:S(2)}) async-start(f32[4,4,8,1280]{3,2,1,0:T(8,128)} %copy-done.5), calls=%async_computation.2 | async-start | bytes 655360 | tf_op jit(solution)/shard_map/slice | solution.py:380
  116.2 56.9 %copy-start.19 = (s32[3,16]{1,0:T(4,128)S(1)}, s32[3,16]{1,0:T(4,128)}, u32[]{:S(2)}) copy-start(s32[3,16]{1,0:T(4,128)} %constant.39.clone) | copy-start | bytes 580
  116.2 56.9 %copy-start.20 = (s32[3,16]{1,0:T(4,128)S(1)}, s32[3,16]{1,0:T(4,128)}, u32[]{:S(2)}) copy-start(s32[3,16]{1,0:T(4,128)} %constant.38.clone) | copy-start | bytes 580
  116.4 61.1 %copy-start.11 = (f32[2,4,8,2560]{3,2,1,0:T(8,128)}, f32[2,4,8,2560]{3,2,1,0:T(8,128)S(1)}, u32[]{:S(2)}) copy-start(f32[2,4,8,2560]{3,2,1,0:T(8,128)S(1)} %collective-permute-done.15.refs_9_) | copy-start | bytes 1966084
  129.6 37.6 %all-to-all-start.1 = ((f32[16,24,128]{2,1,0:T(8,128)}), f32[16,24,128]{2,1,0:T(8,128)S(1)}, u32[]{:S(2)}, u32[]{:S(2)}) async-start(f32[16,24,128]{2,1,0:T(8,128)} %broadcast_in_dim.7), calls=%async_computation.1 | async-start | bytes 393216 | tf_op jit(solution)/shard_map/all_to_all | solution.py:323
  141.4 12.1 %collective-permute-start.19 = (f32[2,4,8,2560]{3,2,1,0:T(8,128)S(1)}, f32[2,4,8,2560]{3,2,1,0:T(8,128)S(1)}, u32[]{:S(2)}, u32[]{:S(2)}) collective-permute-start(f32[2,4,8,2560]{3,2,1,0:T(8,128)S(1)} %pad_maximum_fusion.4.refs_8_), channel_id=1, source_target_pairs={{0,4},{1,5},{2,6},{3,7},{4,0},{5,1},{6,2},{7,3},{8,12},{9,13},{10,... | collective-permute-start | bytes 1966088 | tf_op jit(solution)/shard_map/ppermute | solution.py:309
  145.0 15.3 %collective-permute-start.18 = (f32[2,4,8,2560]{3,2,1,0:T(8,128)S(1)}, f32[2,4,8,2560]{3,2,1,0:T(8,128)S(1)}, u32[]{:S(2)}, u32[]{:S(2)}) collective-permute-start(f32[2,4,8,2560]{3,2,1,0:T(8,128)S(1)} %collective-permute-done.15.refs_9_), channel_id=1, source_target_pairs={{0,4},{1,5},{2,6},{3,7},{4,0},{5,1},{6,2},{7,3},{8,12},{9,13},{10,... | collective-permute-start | bytes 1966088 | tf_op jit(solution)/shard_map/ppermute | solution.py:309
  147.0 13.4 %collective-permute-start.20 = (f32[4,4,8,1280]{3,2,1,0:T(8,128)}, f32[4,4,8,1280]{3,2,1,0:T(8,128)S(1)}, u32[]{:S(2)}, u32[]{:S(2)}) collective-permute-start(f32[4,4,8,1280]{3,2,1,0:T(8,128)} %pad_maximum_fusion.5), channel_id=1, source_target_pairs={{0,3},{1,2},{2,1},{3,0},{4,7},{5,6},{6,5},{7,4},{8,11},{9,10},{10,... | collective-permute-start | bytes 1966088 | tf_op jit(solution)/shard_map/ppermute | solution.py:309
  150.1 17.0 %collective-permute-start.21 = (f32[4,4,8,1280]{3,2,1,0:T(8,128)S(1)}, f32[4,4,8,1280]{3,2,1,0:T(8,128)}, u32[]{:S(2)}, u32[]{:S(2)}) collective-permute-start(f32[4,4,8,1280]{3,2,1,0:T(8,128)S(1)} %pad_maximum_fusion.6), channel_id=1, source_target_pairs={{0,3},{1,2},{2,1},{3,0},{4,7},{5,6},{6,5},{7,4},{8,11},{9,10},{10,... | collective-permute-start | bytes 1966088 | tf_op jit(solution)/shard_map/ppermute | solution.py:309
  153.5 24.1 %copy-start.12 = (f32[2,4,8,2560]{3,2,1,0:T(8,128)}, f32[2,4,8,2560]{3,2,1,0:T(8,128)S(1)}, u32[]{:S(2)}) copy-start(f32[2,4,8,2560]{3,2,1,0:T(8,128)S(1)} %collective-permute-done.19.refs_10_) | copy-start | bytes 1966084
  169.6 7.9 %collective-permute-start.22 = (f32[384,128]{1,0:T(8,128)S(1)}, f32[384,128]{1,0:T(8,128)S(1)}, u32[]{:S(2)}, u32[]{:S(2)}) collective-permute-start(f32[384,128]{1,0:T(8,128)S(1)} %slice.64), channel_id=1, source_target_pairs={{0,3},{1,2},{2,1},{3,0},{4,7},{5,6},{6,5},{7,4},{8,11},{9,10},{10,... | collective-permute-start | bytes 589832 | tf_op jit(solution)/shard_map/ppermute | solution.py:309
  (2 other events, 1.8 us)

commit v4 on v0

v4 whole, which is shorter than its diff:
```python
import jax
import jax.numpy as jnp
import numpy as np
from jax import lax
from jax.experimental import pallas as pl
from jax.experimental.pallas import tpu as pltpu
from jax.sharding import PartitionSpec as P

F32 = jnp.float32
BF16 = jnp.bfloat16
NT = (((1,), (1,)), ((), ()))
NN = (((1,), (0,)), ((), ()))
X_NEAR, X_WRAP, Y_NEAR, Y_WRAP = 4, 12, 1, 3
ROUTES = (
    ((X_NEAR, X_WRAP, Y_NEAR, Y_WRAP), (Y_NEAR, Y_WRAP, X_NEAR, X_WRAP)),
    ((X_WRAP, X_NEAR, Y_WRAP, Y_NEAR), (Y_WRAP, Y_NEAR, X_WRAP, X_NEAR)),
)
PARTNER = (Y_WRAP, X_WRAP)


def split(x):
    high = x.astype(BF16)
    low = (x - high.astype(F32)).astype(BF16)
    return high, low


def product(left, right, dims):
    def dot(x, y):
        return lax.dot_general(x, y, dims, preferred_element_type=F32)

    return dot(left[0], right[0]) + (dot(left[1], right[0]) + dot(left[0], right[1]))


def exact(left, right, dims):
    return lax.dot_general(
        left, right, dims, precision=lax.Precision.HIGHEST, preferred_element_type=F32
    )


def pair_list(nblk):
    return [(b, c) for b in range(nblk) for c in range(b + 1, nblk)]


def block_row(block, rows, kb):
    return block * kb + (rows if block > 0 else 0)


def arrival_order(route):
    order = [0]
    for mask in route:
        order = order + [mask ^ at for at in order]
    return order


def inner_kernel(part, data, order_ref, info_ref, eig_ref, *refs):
    first = part == 0
    bufs, refs = refs[:4], refs[4:]
    if first:
        sum_ref, fac_ref, vecs, high, low = refs
    else:
        before_ref, keep_ref, give_ref, vecs, high, low, sum_ref = refs
    rows, cols = eig_ref.shape
    owners, nblk, share, _ = vecs.shape
    kb = owners * share
    start = 0 if first else cols - data

    for k, buf in enumerate(bufs):
        for i in range(buf.shape[0]):
            vecs[order_ref[part, k * buf.shape[0] + i]] = buf[i]

    eig_rows = slice(kb, kb + rows)
    high[eig_rows], low[eig_rows] = split(eig_ref[:, start : start + data])
    block = []
    for b in range(nblk):
        at = block_row(b, rows, kb)
        block.append(slice(at, at + kb))
        high[block[b]], low[block[b]] = split(vecs[:, b, :, :data].reshape(kb, data))
    if first:
        for b in range(nblk):
            fac_ref[b] = vecs[:, b, :, data:].reshape(kb, kb)

    def inner(left, right):
        return product((high[left], low[left]), (high[right], low[right]), NT)

    def add(at, term):
        here = slice(at, at + term.shape[0])
        sum_ref[here] = term if first else before_ref[here] + term

    below = nblk * rows
    add(0, inner(eig_rows, block[0]))

    @pl.when(info_ref[0] == 0)
    def _():
        left = slice(0, kb + rows)
        out = inner(left, block[1])
        add(below, out[:kb])
        add(rows, out[kb:])
        out = inner(left, slice(block[2].start, block[3].stop))
        for c in (2, 3):
            lane = slice((c - 2) * kb, (c - 1) * kb)
            add(below + (c - 1) * kb, out[:kb, lane])
            add(c * rows, out[kb:, lane])

    @pl.when(info_ref[0] == 1)
    def _():
        add(rows, inner(eig_rows, block[1]))
        out = inner(slice(kb, block[2].stop), slice(block[2].start, block[3].stop))
        add(2 * rows, out[:rows, :kb])
        add(3 * rows, out[:rows, kb:])
        add(below, out[rows : rows + kb, :kb])
        add(below + kb, out[rows : rows + kb, kb:])
        add(below + 2 * kb, out[rows + kb :, kb:])

    if not first:
        half = keep_ref.shape[0]
        core = info_ref[1]
        keep_ref[...] = sum_ref[pl.ds(pl.multiple_of(core * half, 8), half)]
        give_ref[...] = sum_ref[pl.ds(pl.multiple_of((1 - core) * half, 8), half)]


def inner_sums(part, data, order, info, eig, bufs, before=None):
    rows, _ = eig.shape
    _, nblk, share, width = bufs[0].shape
    owners = sum(buf.shape[0] for buf in bufs)
    kb = owners * share
    depth = rows + nblk * kb
    count = nblk * rows + len(pair_list(nblk)) // 2 * kb
    vmem = pl.BlockSpec(memory_space=pltpu.VMEM)
    smem = pl.BlockSpec(memory_space=pltpu.SMEM)
    sums = jax.ShapeDtypeStruct((count, kb), F32)
    scratch = [pltpu.VMEM((owners, nblk, share, width), F32)]
    scratch += [pltpu.VMEM((depth, data), BF16)] * 2
    if part == 0:
        outs = [sums, jax.ShapeDtypeStruct((nblk, kb, kb), F32)]
    else:
        outs = [jax.ShapeDtypeStruct((count // 2, kb), F32)] * 2
        scratch.append(pltpu.VMEM((count, kb), F32))
    return pl.pallas_call(
        lambda *refs: inner_kernel(part, data, *refs),
        out_shape=outs,
        in_specs=[smem, smem] + [vmem] * (5 + part),
        out_specs=[vmem] * len(outs),
        scratch_shapes=scratch,
        compiler_params=pltpu.CompilerParams(vmem_limit_bytes=24 * 2**20),
        cost_estimate=pl.CostEstimate(
            flops=6 * data * kb * count, bytes_accessed=4 * data * depth, transcendentals=0
        ),
        name="inner_sums",
    )(order, info, eig, *bufs, *([before] if part == 1 else []))


def owner_copies(order_ref, part, bufs, into, sems):
    copies = []
    for k, buf in enumerate(bufs):
        for i in range(buf.shape[0]):
            slot = k * buf.shape[0] + i
            copies.append(
                pltpu.make_async_copy(
                    buf.at[i], into.at[order_ref[part, slot]], sems.at[part, slot]
                )
            )
    return copies


def update_kernel(order_ref, info_ref, sum_ref, rest_ref, fac_ref, eig_ref, *refs):
    bufs = (refs[0:4], refs[4:8])
    out_ref, vecs, out, high, low, sems, out_sems = refs[8], refs[9:11], *refs[11:]
    rows, cols = eig_ref.shape
    nblk, kb, _ = fac_ref.shape
    below = nblk * rows
    pairs = pair_list(nblk)
    parity = info_ref[0]
    width_b = vecs[1].shape[3]
    spans = ((0, cols - width_b), (cols - width_b, width_b))

    copies = [owner_copies(order_ref, part, bufs[part], vecs[part], sems) for part in range(2)]
    for copy in copies[0] + copies[1]:
        copy.start()

    scaled = []
    for c in range(nblk):
        proj = sum_ref[c * rows : (c + 1) * rows]
        for b in range(c):
            index = pairs.index((b, c))
            at = index % (len(pairs) // 2) * kb
            mine = sum_ref[below + at : below + at + kb]
            rest = rest_ref[at : at + kb]
            gram = jnp.where((parity == 0) == (index < len(pairs) // 2), mine, rest)
            proj = proj - exact(scaled[b], gram, NN)
        scaled.append(exact(proj, fac_ref[c], NT))
        lane = slice(c * kb, (c + 1) * kb)
        high[:, lane], low[:, lane] = split(scaled[c])

    left = (high[...], low[...])
    out_copies = []
    for part, (start, width) in enumerate(spans):
        for copy in copies[part]:
            copy.wait()
        for at in range(0, width, 256):
            size = min(256, width - at)
            here = slice(start + at, start + at + size)
            right = jnp.concatenate(
                [vecs[part][:, b, :, at : at + size].reshape(kb, size) for b in range(nblk)],
                axis=0,
            )
            out[:, here] = eig_ref[:, here] - product(left, split(right), NN)
        lane = pl.ds(start, width)
        out_copies.append(
            pltpu.make_async_copy(out.at[:, lane], out_ref.at[:, lane], out_sems.at[part])
        )
        out_copies[part].start()
    for copy in out_copies:
        copy.wait()


def update(order, info, sums, rest, factors, eig, parts):
    rows, cols = eig.shape
    nblk, kb, _ = factors.shape
    _, _, share, _ = parts[0][0].shape
    owners = kb // share
    vmem = pl.BlockSpec(memory_space=pltpu.VMEM)
    smem = pl.BlockSpec(memory_space=pltpu.SMEM)
    hbm = pl.BlockSpec(memory_space=pl.ANY)
    return pl.pallas_call(
        update_kernel,
        out_shape=jax.ShapeDtypeStruct(eig.shape, F32),
        in_specs=[smem] * 2 + [vmem] * 4 + [hbm] * 8,
        out_specs=hbm,
        scratch_shapes=[
            pltpu.VMEM((owners, nblk, share, parts[0][0].shape[3]), F32),
            pltpu.VMEM((owners, nblk, share, parts[1][0].shape[3]), F32),
            pltpu.VMEM((rows, cols), F32),
            pltpu.VMEM((rows, nblk * kb), BF16),
            pltpu.VMEM((rows, nblk * kb), BF16),
            pltpu.SemaphoreType.DMA((2, owners)),
            pltpu.SemaphoreType.DMA((2,)),
        ],
        compiler_params=pltpu.CompilerParams(vmem_limit_bytes=40 * 2**20),
        cost_estimate=pl.CostEstimate(
            flops=6 * rows * nblk * kb * cols,
            bytes_accessed=4 * cols * (2 * rows + nblk * kb),
            transcendentals=0,
        ),
        name="update",
    )(order, info, sums, rest, factors, eig, *parts[0], *parts[1])


def solution(mesh):
    placed = (P("pcol", "prow"), P(None, "pcol", "prow"), P(None, "pcol", None))
    nprow, npcol = mesh.shape["prow"], mesh.shape["pcol"]
    nz = nprow // 2
    orders = np.array([[arrival_order(route) for route in routes] for routes in ROUTES], np.int32)
    in_chip = [[2 * z, 2 * z + 1] for z in range(nz)]

    def send(x, masks):
        pairs = []
        for row in range(nprow):
            mask = masks[row % 2]
            pairs += [(row * npcol + at, row * npcol + (at ^ mask)) for at in range(npcol)]
        return lax.ppermute(x, ("prow", "pcol"), pairs)

    def gather_in_plane(own, part):
        steps = [(ROUTES[part][0][n], ROUTES[part][1][n]) for n in range(4)]
        held = own[None]
        held = jnp.concatenate([held, send(held, steps[0])], axis=0)
        held = jnp.concatenate([held, send(held, steps[1])], axis=0)
        third = send(held, steps[2])
        return held, third, send(held, steps[3]), send(third, steps[3])

    def along_z(x):
        groups = [list(range(core, nprow, 2)) for core in range(2)]
        return lax.all_to_all(x, "prow", 0, 0, axis_index_groups=groups)

    def sum_over_rows(keep, give):
        half, kb = keep.shape
        mine = keep + lax.ppermute(give, "prow", [(i, i ^ 1) for i in range(nprow)])
        part = jnp.sum(along_z(mine.reshape(nz, half // nz, kb)), axis=0)
        whole = along_z(jnp.broadcast_to(part, (nz,) + part.shape)).reshape(half, kb)
        return lax.all_gather(whole, "prow", axis=0, tiled=True, axis_index_groups=in_chip)

    def per_device(eig, house_vecs, wy_factor):
        nblk, _, kb = wy_factor.shape
        rows, cols = eig.shape
        data = (cols // 128 - 1) // 2 * 128
        at = lax.axis_index("pcol").astype(jnp.int32)
        core = lax.rem(lax.axis_index("prow"), 2).astype(jnp.int32)
        parity = jnp.bitwise_and(jnp.bitwise_xor(at >> 1, at >> 3), 1)
        info = jnp.stack([parity, core])
        order = jnp.bitwise_xor(at, jnp.where(core == 0, orders[:, 0], orders[:, 1]))
        own_a = jnp.concatenate([house_vecs[:, :, :data], wy_factor], axis=2)
        own_b = house_vecs[:, :, data:]
        part_a = gather_in_plane(own_a, 0)
        part_b = gather_in_plane(own_b, 1)
        order_a, third_b = lax.optimization_barrier((order, part_b[2]))
        part_b = part_b[:2] + (third_b,) + part_b[3:]
        before, factors = inner_sums(0, data, order_a, info, eig, part_a)
        keep, give = inner_sums(1, cols - data, order, info, eig, part_b, before)
        sums = sum_over_rows(keep, give)
        rest = send(sums[nblk * rows :], PARTNER)
        return update(order, info, sums, rest, factors, eig, (part_a, part_b))

    return jax.shard_map(
        per_device, mesh=mesh, in_specs=placed, out_specs=P("pcol", "prow"), check_vma=False
    )
```

time: 513 us -> 161 us (0.31)
  blocking collectives: 459 us -> 48.8 us
  starting transfers between devices: 0.12 us -> 44.5 us
  waiting for transfers between devices: 1.96 us -> 43.1 us
  matrix products: 35.9 us -> 0 us
  Pallas kernels: 0 us -> 20 us
  between operations: 13.2 us -> 0.38 us
    psum x4 -> x0, blocking collectives: 386 us -> none  [reduce_scale(): summed = lax.psum(partial_sums, 'prow')]
    all_gather x4 -> x1, blocking collectives: 72.2 us -> 6.54 us  [sum_over_rows(): lax.all_gather(whole, 'prow', axis=0, tiled=True, axis_index_groups=in_chip)]
    ppermute x0 -> x12, starting transfers between devices: none -> 44.5 us  [the longest x11 36.5 us: send(): return lax.ppermute(x, ('prow', 'pcol'), pairs)]
    ppermute x0 -> x12, waiting for transfers between devices: none -> 43.1 us  [the longest x11 42 us: send(): return lax.ppermute(x, ('prow', 'pcol'), pairs)]
    all_to_all x0 -> x2, blocking collectives: none -> 42.3 us  [along_z(): return lax.all_to_all(x, 'prow', 0, 0, axis_index_groups=groups)]
    dot_general x12 -> x0, matrix products: 35.9 us -> none  [the longest x8 18.9 us: inner_rows(): lax.dot_general(left, right, (((1,), (1,)), ((), ())), precision=lax.Prec...]
    pallas_call x0 -> x3, Pallas kernels: none -> 20 us  [the longest x2 12.6 us: inner_sums(): pl.pallas_call(lambda *refs: inner_kernel(part, data, *refs), out_shape=o...]
  transfers between devices with their start and end apart: 4 -> 12, of which waited for: 0 -> 9; matrix products, arithmetic and copies ran while one was open for 5% -> 1% of each run, Pallas kernels for 0% -> 4%
where the time goes in v4:
time: 161 us
  blocking collectives  48.8 us (30%)
  starting transfers between devices  44.5 us (28%)
  waiting for transfers between devices  43.1 us (27%)
  Pallas kernels  20 us (12%)
  other arithmetic  3.07 us (2%)
    all_to_all x2, blocking collectives, along_z(): return lax.all_to_all(x, 'prow', 0, 0, axis_index_groups=groups)  42.3 us
    ppermute x11, waiting for transfers between devices, send(): return lax.ppermute(x, ('prow', 'pcol'), pairs)  42 us
    ppermute x11, starting transfers between devices, send(): return lax.ppermute(x, ('prow', 'pcol'), pairs)  36.5 us
    pallas_call x2, Pallas kernels, inner_sums(): pl.pallas_call(lambda *refs: inner_kernel(part, data, *refs), out_shape=o...  12.6 us
    ppermute x1, starting transfers between devices, sum_over_rows(): mine = keep + lax.ppermute(give, 'prow', [(i, i ^ 1) for i in range(nprow)])  8.01 us
    pallas_call x1, Pallas kernels, update(): pl.pallas_call(update_kernel, out_shape=jax.ShapeDtypeStruct(eig.shape, F...  7.37 us
    all_gather x1, blocking collectives, sum_over_rows(): lax.all_gather(whole, 'prow', axis=0, tiled=True, axis_index_groups=in_chip)  6.54 us
  transfers between devices with their start and end apart: 12, of which 9 were waited for; matrix products, arithmetic and copies ran while one was open for 1% of the time, Pallas kernels for 4%

profile of v4, /device:TPU:1, one launch (start us, length us, event | category | flops | bytes accessed | tf_op | source)
XLA Modules:
  0.0 160.9 jit_solution(12826793187870653778)
XLA Ops:
  0.0 0.0 slice-start
  0.0 1.0 slice_bitcast_fusion
  1.0 5.5 %collective-permute-start = (f32[1,4,8,2560]{3,2,1,0:T(8,128)S(1)}, f32[1,4,8,2560]{3,2,1,0:T(8,128)S(1)}, u32[]{:S(2)}, u32[]{:S(2)}) collective-permute-start(f32[1,4,8,2560]{3,2,1,0:T(8,128)S(1)} %slice_bitcast_fusion), channel_id=1, source_target_pairs={{0,12},{1,13},{2,14},{3,15},{4,8},{5,9},{6,10},{7,11},{8,4},{9,5},... | collective-permute-start | bytes 983048 | tf_op jit(solution)/shard_map/ppermute | solution.py:260
  6.5 0.0 slice-done
  6.5 0.7 maximum_bitcast_fusion
  7.3 1.9 %collective-permute-start.5 = (f32[1,4,8,2432]{3,2,1,0:T(8,128)S(1)}, f32[1,4,8,2432]{3,2,1,0:T(8,128)S(1)}, u32[]{:S(2)}, u32[]{:S(2)}) collective-permute-start(f32[1,4,8,2432]{3,2,1,0:T(8,128)S(1)} %maximum_bitcast_fusion), channel_id=1, source_target_pairs={{0,4},{1,5},{2,6},{3,7},{4,0},{5,1},{6,2},{7,3},{8,12},{9,13},{10,... | collective-permute-start | bytes 933896 | tf_op jit(solution)/shard_map/ppermute | solution.py:260
  9.2 1.8 %collective-permute-done = f32[1,4,8,2560]{3,2,1,0:T(8,128)S(1)} collective-permute-done((f32[1,4,8,2560]{3,2,1,0:T(8,128)S(1)}, f32[1,4,8,2560]{3,2,1,0:T(8,128)S(1)}, u32[]{:S(2)}, u32[]{:S(2)}) %collective-permute-start) | collective-permute-done | bytes 327712 | tf_op jit(solution)/shard_map/ppermute | solution.py:260
  11.0 2.2 %collective-permute-start.1 = (f32[2,4,8,2560]{3,2,1,0:T(8,128)S(1)}, f32[2,4,8,2560]{3,2,1,0:T(8,128)S(1)}, u32[]{:S(2)}, u32[]{:S(2)}) collective-permute-start(f32[2,4,8,2560]{3,2,1,0:T(8,128)S(1)} %pad_maximum_fusion.2), channel_id=1, source_target_pairs={{0,4},{1,5},{2,6},{3,7},{4,0},{5,1},{6,2},{7,3},{8,12},{9,13},{10,... | collective-permute-start | bytes 1966088 | tf_op jit(solution)/shard_map/ppermute | solution.py:260
  13.2 2.0 %collective-permute-done.5 = f32[1,4,8,2432]{3,2,1,0:T(8,128)S(1)} collective-permute-done((f32[1,4,8,2432]{3,2,1,0:T(8,128)S(1)}, f32[1,4,8,2432]{3,2,1,0:T(8,128)S(1)}, u32[]{:S(2)}, u32[]{:S(2)}) %collective-permute-start.5) | collective-permute-done | bytes 311328 | tf_op jit(solution)/shard_map/ppermute | solution.py:260
  15.3 2.6 %collective-permute-start.6 = (f32[2,4,8,2432]{3,2,1,0:T(8,128)S(1)}, f32[2,4,8,2432]{3,2,1,0:T(8,128)S(1)}, u32[]{:S(2)}, u32[]{:S(2)}) collective-permute-start(f32[2,4,8,2432]{3,2,1,0:T(8,128)S(1)} %pad_maximum_fusion.3), channel_id=1, source_target_pairs={{0,12},{1,13},{2,14},{3,15},{4,8},{5,9},{6,10},{7,11},{8,4},{9,5},... | collective-permute-start | bytes 1867784 | tf_op jit(solution)/shard_map/ppermute | solution.py:260
  17.9 4.5 %collective-permute-done.1 = f32[2,4,8,2560]{3,2,1,0:T(8,128)S(1)} collective-permute-done((f32[2,4,8,2560]{3,2,1,0:T(8,128)S(1)}, f32[2,4,8,2560]{3,2,1,0:T(8,128)S(1)}, u32[]{:S(2)}, u32[]{:S(2)}) %collective-permute-start.1) | collective-permute-done | bytes 655392 | tf_op jit(solution)/shard_map/ppermute | solution.py:260
  22.4 0.1 pad_maximum_fusion.refs_3_.refs_4_
  22.4 0.0 copy-start.1
  22.5 0.0 copy-start.2
  22.5 0.0 copy-start
  22.5 4.8 %collective-permute-start.2 = (f32[4,4,8,2560]{3,2,1,0:T(8,128)S(1)}, f32[4,4,8,2560]{3,2,1,0:T(8,128)}, u32[]{:S(2)}, u32[]{:S(2)}) collective-permute-start(f32[4,4,8,2560]{3,2,1,0:T(8,128)S(1)} %pad_maximum_fusion.refs_3_.refs_4_), channel_id=1, source_target_pairs={{0,3},{1,2},{2,1},{3,0},{4,7},{5,6},{6,5},{7,4},{8,11},{9,10},{10,... | collective-permute-start | bytes 3932168 | tf_op jit(solution)/shard_map/ppermute | solution.py:260
  27.3 0.4 collective-permute-done.6
  27.7 1.1 pad_maximum_fusion.1.refs_3_.refs_0_
  28.9 2.8 %collective-permute-start.7 = (f32[4,4,8,2432]{3,2,1,0:T(8,128)}, f32[4,4,8,2432]{3,2,1,0:T(8,128)}, u32[]{:S(2)}, u32[]{:S(2)}) collective-permute-start(f32[4,4,8,2432]{3,2,1,0:T(8,128)} %pad_maximum_fusion.1.refs_3_.refs_0_), channel_id=1, source_target_pairs={{0,1},{1,0},{2,3},{3,2},{4,5},{5,4},{6,7},{7,6},{8,9},{9,8},{10,11... | collective-permute-start | bytes 3735560 | tf_op jit(solution)/shard_map/ppermute | solution.py:260
  31.7 2.5 %collective-permute-start.3 = (f32[4,4,8,2560]{3,2,1,0:T(8,128)S(1)}, f32[4,4,8,2560]{3,2,1,0:T(8,128)}, u32[]{:S(2)}, u32[]{:S(2)}) collective-permute-start(f32[4,4,8,2560]{3,2,1,0:T(8,128)S(1)} %pad_maximum_fusion.refs_3_.refs_4_), channel_id=1, source_target_pairs={{0,1},{1,0},{2,3},{3,2},{4,5},{5,4},{6,7},{7,6},{8,9},{9,8},{10,11... | collective-permute-start | bytes 3932168 | tf_op jit(solution)/shard_map/ppermute | solution.py:260
  34.1 4.1 %collective-permute-start.8 = (f32[4,4,8,2432]{3,2,1,0:T(8,128)}, f32[4,4,8,2432]{3,2,1,0:T(8,128)}, u32[]{:S(2)}, u32[]{:S(2)}) collective-permute-start(f32[4,4,8,2432]{3,2,1,0:T(8,128)} %pad_maximum_fusion.1.refs_3_.refs_0_), channel_id=1, source_target_pairs={{0,3},{1,2},{2,1},{3,0},{4,7},{5,6},{6,5},{7,4},{8,11},{9,10},{10,... | collective-permute-start | bytes 3735560 | tf_op jit(solution)/shard_map/ppermute | solution.py:260
  38.3 8.8 %collective-permute-done.7.refs_4_.refs_1_ = f32[4,4,8,2432]{3,2,1,0:T(8,128)} collective-permute-done((f32[4,4,8,2432]{3,2,1,0:T(8,128)}, f32[4,4,8,2432]{3,2,1,0:T(8,128)}, u32[]{:S(2)}, u32[]{:S(2)}) %collective-permute-start.7) | collective-permute-done | bytes 1245216 | tf_op jit(solution)/shard_map/ppermute | solution.py:260
  47.1 4.1 %collective-permute-start.9 = (f32[4,4,8,2432]{3,2,1,0:T(8,128)}, f32[4,4,8,2432]{3,2,1,0:T(8,128)}, u32[]{:S(2)}, u32[]{:S(2)}) collective-permute-start(f32[4,4,8,2432]{3,2,1,0:T(8,128)} %collective-permute-done.7.refs_4_.refs_1_), channel_id=1, source_target_pairs={{0,3},{1,2},{2,1},{3,0},{4,7},{5,6},{6,5},{7,4},{8,11},{9,10},{10,... | collective-permute-start | bytes 3735560 | tf_op jit(solution)/shard_map/ppermute | solution.py:260
  51.2 0.0 collective-permute-done.2.refs_4_.refs_5_
  51.2 1.9 %collective-permute-start.4 = (f32[4,4,8,2560]{3,2,1,0:T(8,128)}, f32[4,4,8,2560]{3,2,1,0:T(8,128)}, u32[]{:S(2)}, u32[]{:S(2)}) collective-permute-start(f32[4,4,8,2560]{3,2,1,0:T(8,128)} %collective-permute-done.2.refs_4_.refs_5_), channel_id=1, source_target_pairs={{0,1},{1,0},{2,3},{3,2},{4,5},{5,4},{6,7},{7,6},{8,9},{9,8},{10,11... | collective-permute-start | bytes 3932168 | tf_op jit(solution)/shard_map/ppermute | solution.py:260
  53.2 0.1 pad_add_fusion.refs_1_.info_ref
  53.3 0.0 copy-done.1
  53.3 0.0 copy-done.2
  53.3 7.9 %collective-permute-done.3.refs_5_.refs_6_ = f32[4,4,8,2560]{3,2,1,0:T(8,128)} collective-permute-done((f32[4,4,8,2560]{3,2,1,0:T(8,128)S(1)}, f32[4,4,8,2560]{3,2,1,0:T(8,128)}, u32[]{:S(2)}, u32[]{:S(2)}) %collective-permute-start.3) | collective-permute-done | bytes 1310752 | tf_op jit(solution)/shard_map/ppermute | solution.py:260
  61.1 0.0 collective-permute-done.8.refs_5_.refs_2_
  61.1 12.8 %collective-permute-done.9.refs_6_.refs_3_ = f32[4,4,8,2432]{3,2,1,0:T(8,128)} collective-permute-done((f32[4,4,8,2432]{3,2,1,0:T(8,128)}, f32[4,4,8,2432]{3,2,1,0:T(8,128)}, u32[]{:S(2)}, u32[]{:S(2)}) %collective-permute-start.9) | collective-permute-done | bytes 1245216 | tf_op jit(solution)/shard_map/ppermute | solution.py:260
  73.9 0.0 copy-done
  73.9 6.2 %inner_sums.2 = (f32[768,128]{1,0:T(8,128)S(1)}, f32[4,128,128]{2,1,0:T(8,128)S(1)}) custom-call(s32[2,16]{1,0:T(2,128)S(1)} %select_xor_fusion.refs_0_.order_ref, s32[2]{0:T(128)S(1)} %pad_add_fusion.refs_1_.info_ref, f32[96,4864]{1,0:T(8,128)S(1)} %copy-done, f32[4,4,8,2432]{3,2,1,0:T(8,128)} %pad_maximum_fusion.1.refs_3_.refs_0_, ...), custom_call_target="tpu_custom_call" | custom-call | flops 1358954496 | bytes 5603328 | tf_op jit(solution)/shard_map/inner_sums/pallas_call | solution.py:138
  80.1 0.0 collective-permute-done.4.refs_6_.refs_7_
  80.2 6.4 %inner_sums.3 = (f32[384,128]{1,0:T(8,128)S(1)}, f32[384,128]{1,0:T(8,128)S(1)}) custom-call(s32[2,16]{1,0:T(2,128)S(1)} %select_xor_fusion.refs_0_.order_ref, s32[2]{0:T(128)S(1)} %pad_add_fusion.refs_1_.info_ref, f32[96,4864]{1,0:T(8,128)S(1)} %copy-done, f32[4,4,8,2560]{3,2,1,0:T(8,128)S(1)} %pad_maximum_fusion.refs_3_.refs_4_, ...), custom_call_target="tpu_custom_call" | custom-call | flops 1509949440 | bytes 6225920 | tf_op jit(solution)/shard_map/inner_sums/pallas_call | solution.py:138
  86.5 8.0 %collective-permute-start.10 = (f32[384,128]{1,0:T(8,128)S(1)}, f32[384,128]{1,0:T(8,128)S(1)}, u32[]{:S(2)}, u32[]{:S(2)}) collective-permute-start(f32[384,128]{1,0:T(8,128)S(1)} %get-tuple-element.15), channel_id=1, source_target_pairs={{0,16},{16,0},{32,48},{48,32},{64,80},{80,64},{96,112},{112,96},{1... | collective-permute-start | bytes 589832 | tf_op jit(solution)/shard_map/ppermute | solution.py:276
  94.5 1.0 collective-permute-done.10
  95.6 21.5 %all_to_all.10 = f32[16,24,128]{2,1,0:T(8,128)} all-to-all(f32[16,24,128]{2,1,0:T(8,128)S(1)} %bitcast.8), channel_id=1, replica_groups={{0,32,64,96,128,160,192,224,256,288,320,352,384,416,448,480},{16,48,80,..., dimensions={0} | all-to-all | bytes 393216 | tf_op jit(solution)/shard_map/all_to_all | solution.py:272
  117.1 0.9 reduce_sum.9
  118.0 20.8 %all_to_all.11 = f32[16,24,128]{2,1,0:T(8,128)S(1)} all-to-all(f32[16,24,128]{2,1,0:T(8,128)S(1)} %broadcast_in_dim.11), channel_id=1, replica_groups={{0,32,64,96,128,160,192,224,256,288,320,352,384,416,448,480},{16,48,80,..., dimensions={0} | all-to-all | bytes 393216 | tf_op jit(solution)/shard_map/all_to_all | solution.py:272
  138.8 6.5 %all_gather.3.sum_ref = f32[768,128]{1,0:T(8,128)S(1)} all-gather(f32[384,128]{1,0:T(8,128)S(1)} %bitcast.9), channel_id=1, replica_groups={{0,16},{32,48},{64,80},{96,112},{128,144},{160,176},{192,208},{224,240}..., dimensions={0}, use_global_device_ids=true | all-gather | bytes 589824 | tf_op jit(solution)/shard_map/all_gather | solution.py:279
  145.4 4.0 %collective-permute-start.11 = (f32[384,128]{1,0:T(8,128)S(1)}, f32[384,128]{1,0:T(8,128)S(1)}, u32[]{:S(2)}, u32[]{:S(2)}) collective-permute-start(f32[384,128]{1,0:T(8,128)S(1)} %slice.12), channel_id=1, source_target_pairs={{0,3},{1,2},{2,1},{3,0},{4,7},{5,6},{6,5},{7,4},{8,11},{9,10},{10,... | collective-permute-start | bytes 589832 | tf_op jit(solution)/shard_map/ppermute | solution.py:260
  149.4 3.9 %collective-permute-done.11.rest_ref = f32[384,128]{1,0:T(8,128)S(1)} collective-permute-done((f32[384,128]{1,0:T(8,128)S(1)}, f32[384,128]{1,0:T(8,128)S(1)}, u32[]{:S(2)}, u32[]{:S(2)}) %collective-permute-start.11) | collective-permute-done | bytes 196640 | tf_op jit(solution)/shard_map/ppermute | solution.py:260
  153.3 7.4 %update.1 = f32[96,4864]{1,0:T(8,128)} custom-call(s32[2,16]{1,0:T(2,128)S(1)} %select_xor_fusion.refs_0_.order_ref, s32[2]{0:T(128)S(1)} %pad_add_fusion.refs_1_.info_ref, f32[768,128]{1,0:T(8,128)S(1)} %all_gather.3.sum_ref, f32[384,128]{1,0:T(8,128)S(1)} %collective-permute-done.11.rest_ref, f32[4,128,128]{2,1,0:T(8,128)S(1)} %get-tuple-element.16.fac_ref, ...), custom_call_target="tpu_custom_call" | custom-call | flops 1434451968 | bytes 13697024 | tf_op jit(solution)/shard_map/update/pallas_call | solution.py:224
  (6 shorter events, 0.1 us)
Async XLA Ops:
  0.0 6.5 %slice-start = ((f32[4,8,4864]{2,1,0:T(8,128)}), f32[4,8,2304]{2,1,0:T(8,128)S(1)}, s32[]{:S(2)}) async-start(f32[4,8,4864]{2,1,0:T(8,128)} %param.6), calls=%async_computation.2 | async-start | bytes 589824 | tf_op jit(solution)/shard_map/slice | solution.py:290
  1.0 9.9 %collective-permute-start = (f32[1,4,8,2560]{3,2,1,0:T(8,128)S(1)}, f32[1,4,8,2560]{3,2,1,0:T(8,128)S(1)}, u32[]{:S(2)}, u32[]{:S(2)}) collective-permute-start(f32[1,4,8,2560]{3,2,1,0:T(8,128)S(1)} %slice_bitcast_fusion), channel_id=1, source_target_pairs={{0,12},{1,13},{2,14},{3,15},{4,8},{5,9},{6,10},{7,11},{8,4},{9,5},... | collective-permute-start | bytes 983048 | tf_op jit(solution)/shard_map/ppermute | solution.py:260
  7.3 7.9 %collective-permute-start.5 = (f32[1,4,8,2432]{3,2,1,0:T(8,128)S(1)}, f32[1,4,8,2432]{3,2,1,0:T(8,128)S(1)}, u32[]{:S(2)}, u32[]{:S(2)}) collective-permute-start(f32[1,4,8,2432]{3,2,1,0:T(8,128)S(1)} %maximum_bitcast_fusion), channel_id=1, source_target_pairs={{0,4},{1,5},{2,6},{3,7},{4,0},{5,1},{6,2},{7,3},{8,12},{9,13},{10,... | collective-permute-start | bytes 933896 | tf_op jit(solution)/shard_map/ppermute | solution.py:260
  11.0 11.3 %collective-permute-start.1 = (f32[2,4,8,2560]{3,2,1,0:T(8,128)S(1)}, f32[2,4,8,2560]{3,2,1,0:T(8,128)S(1)}, u32[]{:S(2)}, u32[]{:S(2)}) collective-permute-start(f32[2,4,8,2560]{3,2,1,0:T(8,128)S(1)} %pad_maximum_fusion.2), channel_id=1, source_target_pairs={{0,4},{1,5},{2,6},{3,7},{4,0},{5,1},{6,2},{7,3},{8,12},{9,13},{10,... | collective-permute-start | bytes 1966088 | tf_op jit(solution)/shard_map/ppermute | solution.py:260
  15.3 12.5 %collective-permute-start.6 = (f32[2,4,8,2432]{3,2,1,0:T(8,128)S(1)}, f32[2,4,8,2432]{3,2,1,0:T(8,128)S(1)}, u32[]{:S(2)}, u32[]{:S(2)}) collective-permute-start(f32[2,4,8,2432]{3,2,1,0:T(8,128)S(1)} %pad_maximum_fusion.3), channel_id=1, source_target_pairs={{0,12},{1,13},{2,14},{3,15},{4,8},{5,9},{6,10},{7,11},{8,4},{9,5},... | collective-permute-start | bytes 1867784 | tf_op jit(solution)/shard_map/ppermute | solution.py:260
  22.4 30.8 %copy-start.1 = (s32[2,16]{1,0:T(2,128)S(1)}, s32[2,16]{1,0:T(2,128)}, u32[]{:S(2)}) copy-start(s32[2,16]{1,0:T(2,128)} %constant.25.clone) | copy-start | bytes 388
  22.5 30.8 %copy-start.2 = (s32[2,16]{1,0:T(2,128)S(1)}, s32[2,16]{1,0:T(2,128)}, u32[]{:S(2)}) copy-start(s32[2,16]{1,0:T(2,128)} %constant.24.clone) | copy-start | bytes 388
  22.5 51.4 %copy-start = (f32[96,4864]{1,0:T(8,128)S(1)}, f32[96,4864]{1,0:T(8,128)}, u32[]{:S(2)}) copy-start(f32[96,4864]{1,0:T(8,128)} %eig_ref.1) | copy-start | bytes 5603332
  22.5 28.8 %collective-permute-start.2 = (f32[4,4,8,2560]{3,2,1,0:T(8,128)S(1)}, f32[4,4,8,2560]{3,2,1,0:T(8,128)}, u32[]{:S(2)}, u32[]{:S(2)}) collective-permute-start(f32[4,4,8,2560]{3,2,1,0:T(8,128)S(1)} %pad_maximum_fusion.refs_3_.refs_4_), channel_id=1, source_target_pairs={{0,3},{1,2},{2,1},{3,0},{4,7},{5,6},{6,5},{7,4},{8,11},{9,10},{10,... | collective-permute-start | bytes 3932168 | tf_op jit(solution)/shard_map/ppermute | solution.py:260
  28.9 18.2 %collective-permute-start.7 = (f32[4,4,8,2432]{3,2,1,0:T(8,128)}, f32[4,4,8,2432]{3,2,1,0:T(8,128)}, u32[]{:S(2)}, u32[]{:S(2)}) collective-permute-start(f32[4,4,8,2432]{3,2,1,0:T(8,128)} %pad_maximum_fusion.1.refs_3_.refs_0_), channel_id=1, source_target_pairs={{0,1},{1,0},{2,3},{3,2},{4,5},{5,4},{6,7},{7,6},{8,9},{9,8},{10,11... | collective-permute-start | bytes 3735560 | tf_op jit(solution)/shard_map/ppermute | solution.py:260
  31.7 29.5 %collective-permute-start.3 = (f32[4,4,8,2560]{3,2,1,0:T(8,128)S(1)}, f32[4,4,8,2560]{3,2,1,0:T(8,128)}, u32[]{:S(2)}, u32[]{:S(2)}) collective-permute-start(f32[4,4,8,2560]{3,2,1,0:T(8,128)S(1)} %pad_maximum_fusion.refs_3_.refs_4_), channel_id=1, source_target_pairs={{0,1},{1,0},{2,3},{3,2},{4,5},{5,4},{6,7},{7,6},{8,9},{9,8},{10,11... | collective-permute-start | bytes 3932168 | tf_op jit(solution)/shard_map/ppermute | solution.py:260
  34.1 27.0 %collective-permute-start.8 = (f32[4,4,8,2432]{3,2,1,0:T(8,128)}, f32[4,4,8,2432]{3,2,1,0:T(8,128)}, u32[]{:S(2)}, u32[]{:S(2)}) collective-permute-start(f32[4,4,8,2432]{3,2,1,0:T(8,128)} %pad_maximum_fusion.1.refs_3_.refs_0_), channel_id=1, source_target_pairs={{0,3},{1,2},{2,1},{3,0},{4,7},{5,6},{6,5},{7,4},{8,11},{9,10},{10,... | collective-permute-start | bytes 3735560 | tf_op jit(solution)/shard_map/ppermute | solution.py:260
  47.1 26.8 %collective-permute-start.9 = (f32[4,4,8,2432]{3,2,1,0:T(8,128)}, f32[4,4,8,2432]{3,2,1,0:T(8,128)}, u32[]{:S(2)}, u32[]{:S(2)}) collective-permute-start(f32[4,4,8,2432]{3,2,1,0:T(8,128)} %collective-permute-done.7.refs_4_.refs_1_), channel_id=1, source_target_pairs={{0,3},{1,2},{2,1},{3,0},{4,7},{5,6},{6,5},{7,4},{8,11},{9,10},{10,... | collective-permute-start | bytes 3735560 | tf_op jit(solution)/shard_map/ppermute | solution.py:260
  51.2 28.9 %collective-permute-start.4 = (f32[4,4,8,2560]{3,2,1,0:T(8,128)}, f32[4,4,8,2560]{3,2,1,0:T(8,128)}, u32[]{:S(2)}, u32[]{:S(2)}) collective-permute-start(f32[4,4,8,2560]{3,2,1,0:T(8,128)} %collective-permute-done.2.refs_4_.refs_5_), channel_id=1, source_target_pairs={{0,1},{1,0},{2,3},{3,2},{4,5},{5,4},{6,7},{7,6},{8,9},{9,8},{10,11... | collective-permute-start | bytes 3932168 | tf_op jit(solution)/shard_map/ppermute | solution.py:260
  86.5 9.1 %collective-permute-start.10 = (f32[384,128]{1,0:T(8,128)S(1)}, f32[384,128]{1,0:T(8,128)S(1)}, u32[]{:S(2)}, u32[]{:S(2)}) collective-permute-start(f32[384,128]{1,0:T(8,128)S(1)} %get-tuple-element.15), channel_id=1, source_target_pairs={{0,16},{16,0},{32,48},{48,32},{64,80},{80,64},{96,112},{112,96},{1... | collective-permute-start | bytes 589832 | tf_op jit(solution)/shard_map/ppermute | solution.py:276
  145.4 7.9 %collective-permute-start.11 = (f32[384,128]{1,0:T(8,128)S(1)}, f32[384,128]{1,0:T(8,128)S(1)}, u32[]{:S(2)}, u32[]{:S(2)}) collective-permute-start(f32[384,128]{1,0:T(8,128)S(1)} %slice.12), channel_id=1, source_target_pairs={{0,3},{1,2},{2,1},{3,0},{4,7},{5,6},{6,5},{7,4},{8,11},{9,10},{10,... | collective-permute-start | bytes 589832 | tf_op jit(solution)/shard_map/ppermute | solution.py:260

commit v5 on v4

--- a/solution.py
+++ b/solution.py
@@ -25,10 +25,12 @@
 
 
 def product(left, right, dims):
-    def dot(x, y):
-        return lax.dot_general(x, y, dims, preferred_element_type=F32)
-
-    return dot(left[0], right[0]) + (dot(left[1], right[0]) + dot(left[0], right[1]))
+    rows = left[0].shape[0]
+    both = lax.dot_general(
+        jnp.concatenate(left, axis=0), right[0], dims, preferred_element_type=F32
+    )
+    cross = lax.dot_general(left[0], right[1], dims, preferred_element_type=F32)
+    return both[:rows] + (both[rows:] + cross)
 
 
 def exact(left, right, dims):
@@ -52,9 +54,49 @@
     return order
 
 
+def owner_copies(order_ref, part, bufs, into, sems):
+    copies = []
+    for k, buf in enumerate(bufs):
+        for i in range(buf.shape[0]):
+            slot = k * buf.shape[0] + i
+            copies.append(
+                pltpu.make_async_copy(
+                    buf.at[i], into.at[order_ref[part, slot]], sems.at[part, slot]
+                )
+            )
+    return copies
+
+
+def collect_kernel(part, order_ref, *refs):
+    bufs, out_ref, sems = refs[:-2], refs[-2], refs[-1]
+    copies = owner_copies(order_ref, part, bufs, out_ref, sems)
+    for copy in copies:
+        copy.start()
+    for copy in copies:
+        copy.wait()
+
+
+def collect(part, order, bufs):
+    _, nblk, share, width = bufs[0].shape
+    owners = order.shape[1]
+    return pl.pallas_call(
+        lambda *refs: collect_kernel(part, *refs),
+        out_shape=jax.ShapeDtypeStruct((owners, nblk, share, width), F32),
+        in_specs=[pl.BlockSpec(memory_space=pltpu.SMEM)]
+        + [pl.BlockSpec(memory_space=pl.ANY)] * len(bufs),
+        out_specs=pl.BlockSpec(memory_space=pltpu.VMEM),
+        scratch_shapes=[pltpu.SemaphoreType.DMA((2, owners))],
+        compiler_params=pltpu.CompilerParams(vmem_limit_bytes=8 * 2**20),
+        cost_estimate=pl.CostEstimate(
+            flops=0, bytes_accessed=8 * owners * nblk * share * width, transcendentals=0
+        ),
+        name="collect",
+    )(order, *bufs)
+
+
 def inner_kernel(part, data, order_ref, info_ref, eig_ref, *refs):
     first = part == 0
-    bufs, refs = refs[:4], refs[4:]
+    early_ref, late_ref, refs = refs[0], refs[1], refs[2:]
     if first:
         sum_ref, fac_ref, vecs, high, low = refs
     else:
@@ -64,9 +106,10 @@
     kb = owners * share
     start = 0 if first else cols - data
 
-    for k, buf in enumerate(bufs):
-        for i in range(buf.shape[0]):
-            vecs[order_ref[part, k * buf.shape[0] + i]] = buf[i]
+    vecs[...] = early_ref[...]
+    count = late_ref.shape[0]
+    for i in range(count):
+        vecs[order_ref[part, owners - count + i]] = late_ref[i]
 
     eig_rows = slice(kb, kb + rows)
     high[eig_rows], low[eig_rows] = split(eig_ref[:, start : start + data])
@@ -74,7 +117,10 @@
     for b in range(nblk):
         at = block_row(b, rows, kb)
         block.append(slice(at, at + kb))
-        high[block[b]], low[block[b]] = split(vecs[:, b, :, :data].reshape(kb, data))
+        for owner in range(0, owners, 2):
+            two = vecs[owner : owner + 2, b, :, :data].reshape(2 * share, data)
+            here = slice(at + owner * share, at + (owner + 2) * share)
+            high[here], low[here] = split(two)
     if first:
         for b in range(nblk):
             fac_ref[b] = vecs[:, b, :, data:].reshape(kb, kb)
@@ -120,8 +166,8 @@
 
 def inner_sums(part, data, order, info, eig, bufs, before=None):
     rows, _ = eig.shape
-    _, nblk, share, width = bufs[0].shape
-    owners = sum(buf.shape[0] for buf in bufs)
+    _, nblk, share, width = bufs[-1].shape
+    owners = order.shape[1]
     kb = owners * share
     depth = rows + nblk * kb
     count = nblk * rows + len(pair_list(nblk)) // 2 * kb
@@ -138,7 +184,7 @@
     return pl.pallas_call(
         lambda *refs: inner_kernel(part, data, *refs),
         out_shape=outs,
-        in_specs=[smem, smem] + [vmem] * (5 + part),
+        in_specs=[smem, smem] + [vmem] * (1 + len(bufs) + part),
         out_specs=[vmem] * len(outs),
         scratch_shapes=scratch,
         compiler_params=pltpu.CompilerParams(vmem_limit_bytes=24 * 2**20),
@@ -147,19 +193,6 @@
         ),
         name="inner_sums",
     )(order, info, eig, *bufs, *([before] if part == 1 else []))
-
-
-def owner_copies(order_ref, part, bufs, into, sems):
-    copies = []
-    for k, buf in enumerate(bufs):
-        for i in range(buf.shape[0]):
-            slot = k * buf.shape[0] + i
-            copies.append(
-                pltpu.make_async_copy(
-                    buf.at[i], into.at[order_ref[part, slot]], sems.at[part, slot]
-                )
-            )
-    return copies
 
 
 def update_kernel(order_ref, info_ref, sum_ref, rest_ref, fac_ref, eig_ref, *refs):
@@ -291,10 +324,13 @@
         own_b = house_vecs[:, :, data:]
         part_a = gather_in_plane(own_a, 0)
         part_b = gather_in_plane(own_b, 1)
-        order_a, third_b = lax.optimization_barrier((order, part_b[2]))
-        part_b = part_b[:2] + (third_b,) + part_b[3:]
-        before, factors = inner_sums(0, data, order_a, info, eig, part_a)
-        keep, give = inner_sums(1, cols - data, order, info, eig, part_b, before)
+        early_a = collect(0, order, part_a[:3])
+        early_b = collect(1, order, part_b[:3])
+        order_a, early_b = lax.optimization_barrier((order, early_b))
+        before, factors = inner_sums(0, data, order_a, info, eig, (early_a, part_a[3]))
+        keep, give = inner_sums(
+            1, cols - data, order, info, eig, (early_b, part_b[3]), before
+        )
         sums = sum_over_rows(keep, give)
         rest = send(sums[nblk * rows :], PARTNER)
         return update(order, info, sums, rest, factors, eig, (part_a, part_b))

time: 161 us -> 159 us (0.988)
  waiting for transfers between devices: 43.1 us -> 38.2 us
  Pallas kernels: 20 us -> 22.7 us
    pallas_call x0 -> x2, Pallas kernels: none -> 5.7 us  [collect(): pl.pallas_call(lambda *refs: collect_kernel(part, *refs), out_shape=jax.S...]
    ppermute x11, waiting for transfers between devices: 42 us -> 37.1 us  [send(): return lax.ppermute(x, ('prow', 'pcol'), pairs)]
    pallas_call x2, Pallas kernels: 12.6 us -> 9.73 us  [inner_sums(): pl.pallas_call(lambda *refs: inner_kernel(part, data, *refs), out_shape=o...]
  transfers between devices with their start and end apart: 12 -> 12, of which waited for: 9 -> 9; matrix products, arithmetic and copies ran while one was open for 1% -> 1% of each run, Pallas kernels for 4% -> 7%
where the time goes in v5:
time: 159 us
  blocking collectives  48.9 us (31%)
  starting transfers between devices  44.2 us (28%)
  waiting for transfers between devices  38.2 us (24%)
  Pallas kernels  22.7 us (14%)
  local copies, waits for them, and re-layouts  2.12 us (1%)
  other arithmetic  2.07 us (1%)
    all_to_all x2, blocking collectives, along_z(): return lax.all_to_all(x, 'prow', 0, 0, axis_index_groups=groups)  42.4 us
    ppermute x11, waiting for transfers between devices, send(): return lax.ppermute(x, ('prow', 'pcol'), pairs)  37.1 us
    ppermute x11, starting transfers between devices, send(): return lax.ppermute(x, ('prow', 'pcol'), pairs)  35.6 us
    pallas_call x2, Pallas kernels, inner_sums(): pl.pallas_call(lambda *refs: inner_kernel(part, data, *refs), out_shape=o...  9.73 us
    ppermute x1, starting transfers between devices, sum_over_rows(): mine = keep + lax.ppermute(give, 'prow', [(i, i ^ 1) for i in range(nprow)])  8.55 us
    pallas_call x1, Pallas kernels, update(): pl.pallas_call(update_kernel, out_shape=jax.ShapeDtypeStruct(eig.shape, F...  7.28 us
    all_gather x1, blocking collectives, sum_over_rows(): lax.all_gather(whole, 'prow', axis=0, tiled=True, axis_index_groups=in_chip)  6.54 us
    pallas_call x2, Pallas kernels, collect(): pl.pallas_call(lambda *refs: collect_kernel(part, *refs), out_shape=jax.S...  5.7 us
  transfers between devices with their start and end apart: 12, of which 9 were waited for; matrix products, arithmetic and copies ran while one was open for 1% of the time, Pallas kernels for 7%

profile of v5, /device:TPU:1, one launch (start us, length us, event | category | flops | bytes accessed | tf_op | source)
XLA Modules:
  0.0 158.6 jit_solution(16636716929674265344)
XLA Ops:
  0.0 1.0 slice_bitcast_fusion
  1.0 5.5 %collective-permute-start = (f32[1,4,8,2560]{3,2,1,0:T(8,128)S(1)}, f32[1,4,8,2560]{3,2,1,0:T(8,128)S(1)}, u32[]{:S(2)}, u32[]{:S(2)}) collective-permute-start(f32[1,4,8,2560]{3,2,1,0:T(8,128)S(1)} %slice_bitcast_fusion), channel_id=1, source_target_pairs={{0,12},{1,13},{2,14},{3,15},{4,8},{5,9},{6,10},{7,11},{8,4},{9,5},... | collective-permute-start | bytes 983048 | tf_op jit(solution)/shard_map/ppermute | solution.py:293
  6.5 0.0 slice-done
  6.5 0.7 maximum_bitcast_fusion
  7.3 1.9 %collective-permute-start.5 = (f32[1,4,8,2432]{3,2,1,0:T(8,128)S(1)}, f32[1,4,8,2432]{3,2,1,0:T(8,128)S(1)}, u32[]{:S(2)}, u32[]{:S(2)}) collective-permute-start(f32[1,4,8,2432]{3,2,1,0:T(8,128)S(1)} %maximum_bitcast_fusion), channel_id=1, source_target_pairs={{0,4},{1,5},{2,6},{3,7},{4,0},{5,1},{6,2},{7,3},{8,12},{9,13},{10,... | collective-permute-start | bytes 933896 | tf_op jit(solution)/shard_map/ppermute | solution.py:293
  9.2 1.8 %collective-permute-done = f32[1,4,8,2560]{3,2,1,0:T(8,128)S(1)} collective-permute-done((f32[1,4,8,2560]{3,2,1,0:T(8,128)S(1)}, f32[1,4,8,2560]{3,2,1,0:T(8,128)S(1)}, u32[]{:S(2)}, u32[]{:S(2)}) %collective-permute-start) | collective-permute-done | bytes 327712 | tf_op jit(solution)/shard_map/ppermute | solution.py:293
  11.0 2.2 %collective-permute-start.1 = (f32[2,4,8,2560]{3,2,1,0:T(8,128)S(1)}, f32[2,4,8,2560]{3,2,1,0:T(8,128)S(1)}, u32[]{:S(2)}, u32[]{:S(2)}) collective-permute-start(f32[2,4,8,2560]{3,2,1,0:T(8,128)S(1)} %pad_maximum_fusion.2), channel_id=1, source_target_pairs={{0,4},{1,5},{2,6},{3,7},{4,0},{5,1},{6,2},{7,3},{8,12},{9,13},{10,... | collective-permute-start | bytes 1966088 | tf_op jit(solution)/shard_map/ppermute | solution.py:293
  13.2 2.0 %collective-permute-done.5 = f32[1,4,8,2432]{3,2,1,0:T(8,128)S(1)} collective-permute-done((f32[1,4,8,2432]{3,2,1,0:T(8,128)S(1)}, f32[1,4,8,2432]{3,2,1,0:T(8,128)S(1)}, u32[]{:S(2)}, u32[]{:S(2)}) %collective-permute-start.5) | collective-permute-done | bytes 311328 | tf_op jit(solution)/shard_map/ppermute | solution.py:293
  15.3 2.6 %collective-permute-start.6 = (f32[2,4,8,2432]{3,2,1,0:T(8,128)S(1)}, f32[2,4,8,2432]{3,2,1,0:T(8,128)S(1)}, u32[]{:S(2)}, u32[]{:S(2)}) collective-permute-start(f32[2,4,8,2432]{3,2,1,0:T(8,128)S(1)} %pad_maximum_fusion.3), channel_id=1, source_target_pairs={{0,12},{1,13},{2,14},{3,15},{4,8},{5,9},{6,10},{7,11},{8,4},{9,5},... | collective-permute-start | bytes 1867784 | tf_op jit(solution)/shard_map/ppermute | solution.py:293
  17.9 4.5 %collective-permute-done.1 = f32[2,4,8,2560]{3,2,1,0:T(8,128)S(1)} collective-permute-done((f32[2,4,8,2560]{3,2,1,0:T(8,128)S(1)}, f32[2,4,8,2560]{3,2,1,0:T(8,128)S(1)}, u32[]{:S(2)}, u32[]{:S(2)}) %collective-permute-start.1) | collective-permute-done | bytes 655392 | tf_op jit(solution)/shard_map/ppermute | solution.py:293
  22.4 0.1 pad_maximum_fusion.refs_1_.refs_4_
  22.4 0.0 copy-start.3
  22.5 0.0 copy-start.4
  22.5 4.7 %collective-permute-start.2 = (f32[4,4,8,2560]{3,2,1,0:T(8,128)S(1)}, f32[4,4,8,2560]{3,2,1,0:T(8,128)}, u32[]{:S(2)}, u32[]{:S(2)}) collective-permute-start(f32[4,4,8,2560]{3,2,1,0:T(8,128)S(1)} %pad_maximum_fusion.refs_1_.refs_4_), channel_id=1, source_target_pairs={{0,3},{1,2},{2,1},{3,0},{4,7},{5,6},{6,5},{7,4},{8,11},{9,10},{10,... | collective-permute-start | bytes 3932168 | tf_op jit(solution)/shard_map/ppermute | solution.py:293
  27.2 0.6 collective-permute-done.6
  27.7 0.1 pad_maximum_fusion.1.refs_1_.refs_0_
  27.8 2.8 %collective-permute-start.7 = (f32[4,4,8,2432]{3,2,1,0:T(8,128)S(1)}, f32[4,4,8,2432]{3,2,1,0:T(8,128)}, u32[]{:S(2)}, u32[]{:S(2)}) collective-permute-start(f32[4,4,8,2432]{3,2,1,0:T(8,128)S(1)} %pad_maximum_fusion.1.refs_1_.refs_0_), channel_id=1, source_target_pairs={{0,1},{1,0},{2,3},{3,2},{4,5},{5,4},{6,7},{7,6},{8,9},{9,8},{10,11... | collective-permute-start | bytes 3735560 | tf_op jit(solution)/shard_map/ppermute | solution.py:293
  30.7 2.5 %collective-permute-start.3 = (f32[4,4,8,2560]{3,2,1,0:T(8,128)S(1)}, f32[4,4,8,2560]{3,2,1,0:T(8,128)}, u32[]{:S(2)}, u32[]{:S(2)}) collective-permute-start(f32[4,4,8,2560]{3,2,1,0:T(8,128)S(1)} %pad_maximum_fusion.refs_1_.refs_4_), channel_id=1, source_target_pairs={{0,1},{1,0},{2,3},{3,2},{4,5},{5,4},{6,7},{7,6},{8,9},{9,8},{10,11... | collective-permute-start | bytes 3932168 | tf_op jit(solution)/shard_map/ppermute | solution.py:293
  33.1 4.1 %collective-permute-start.8 = (f32[4,4,8,2432]{3,2,1,0:T(8,128)S(1)}, f32[4,4,8,2432]{3,2,1,0:T(8,128)}, u32[]{:S(2)}, u32[]{:S(2)}) collective-permute-start(f32[4,4,8,2432]{3,2,1,0:T(8,128)S(1)} %pad_maximum_fusion.1.refs_1_.refs_0_), channel_id=1, source_target_pairs={{0,3},{1,2},{2,1},{3,0},{4,7},{5,6},{6,5},{7,4},{8,11},{9,10},{10,... | collective-permute-start | bytes 3735560 | tf_op jit(solution)/shard_map/ppermute | solution.py:293
  37.3 8.6 %collective-permute-done.7.refs_2_.refs_1_ = f32[4,4,8,2432]{3,2,1,0:T(8,128)} collective-permute-done((f32[4,4,8,2432]{3,2,1,0:T(8,128)S(1)}, f32[4,4,8,2432]{3,2,1,0:T(8,128)}, u32[]{:S(2)}, u32[]{:S(2)}) %collective-permute-start.7) | collective-permute-done | bytes 1245216 | tf_op jit(solution)/shard_map/ppermute | solution.py:293
  45.9 4.1 %collective-permute-start.9 = (f32[4,4,8,2432]{3,2,1,0:T(8,128)}, f32[4,4,8,2432]{3,2,1,0:T(8,128)}, u32[]{:S(2)}, u32[]{:S(2)}) collective-permute-start(f32[4,4,8,2432]{3,2,1,0:T(8,128)} %collective-permute-done.7.refs_2_.refs_1_), channel_id=1, source_target_pairs={{0,3},{1,2},{2,1},{3,0},{4,7},{5,6},{6,5},{7,4},{8,11},{9,10},{10,... | collective-permute-start | bytes 3735560 | tf_op jit(solution)/shard_map/ppermute | solution.py:293
  50.0 0.0 collective-permute-done.2.refs_2_.refs_5_
  50.0 1.9 %collective-permute-start.4 = (f32[4,4,8,2560]{3,2,1,0:T(8,128)}, f32[4,4,8,2560]{3,2,1,0:T(8,128)}, u32[]{:S(2)}, u32[]{:S(2)}) collective-permute-start(f32[4,4,8,2560]{3,2,1,0:T(8,128)} %collective-permute-done.2.refs_2_.refs_5_), channel_id=1, source_target_pairs={{0,1},{1,0},{2,3},{3,2},{4,5},{5,4},{6,7},{7,6},{8,9},{9,8},{10,11... | collective-permute-start | bytes 3932168 | tf_op jit(solution)/shard_map/ppermute | solution.py:293
  52.0 0.1 pad_add_fusion.refs_1_.info_ref
  52.1 0.0 copy-done.3
  52.1 0.0 copy-done.4
  52.1 8.5 %collective-permute-done.8.refs_3_.refs_2_ = f32[4,4,8,2432]{3,2,1,0:T(8,128)} collective-permute-done((f32[4,4,8,2432]{3,2,1,0:T(8,128)S(1)}, f32[4,4,8,2432]{3,2,1,0:T(8,128)}, u32[]{:S(2)}, u32[]{:S(2)}) %collective-permute-start.8) | collective-permute-done | bytes 1245216 | tf_op jit(solution)/shard_map/ppermute | solution.py:293
  60.6 2.8 %collect.3.refs_3_ = f32[16,4,8,2432]{3,2,1,0:T(8,128)S(1)} custom-call(s32[2,16]{1,0:T(2,128)S(1)} %select_xor_fusion.refs_0_.order_ref, f32[4,4,8,2432]{3,2,1,0:T(8,128)S(1)} %pad_maximum_fusion.1.refs_1_.refs_0_, f32[4,4,8,2432]{3,2,1,0:T(8,128)} %collective-permute-done.7.refs_2_.refs_1_, f32[4,4,8,2432]{3,2,1,0:T(8,128)} %collective-permute-done.8.refs_3_.refs_2_), custom_call_target="tpu_custom_call" | custom-call | bytes 9961472 | tf_op jit(solution)/shard_map/collect/pallas_call | solution.py:82
  63.4 0.0 copy-start.1
  63.4 1.0 copy-done.1
  64.4 0.0 collective-permute-done.3.refs_3_.refs_6_
  64.4 2.9 %collect.2.refs_3_ = f32[16,4,8,2560]{3,2,1,0:T(8,128)S(1)} custom-call(s32[2,16]{1,0:T(2,128)S(1)} %select_xor_fusion.refs_0_.order_ref, f32[4,4,8,2560]{3,2,1,0:T(8,128)S(1)} %pad_maximum_fusion.refs_1_.refs_4_, f32[4,4,8,2560]{3,2,1,0:T(8,128)} %collective-permute-done.2.refs_2_.refs_5_, f32[4,4,8,2560]{3,2,1,0:T(8,128)} %collective-permute-done.3.refs_3_.refs_6_), custom_call_target="tpu_custom_call" | custom-call | bytes 10485760 | tf_op jit(solution)/shard_map/collect/pallas_call | solution.py:82
  67.3 6.6 %collective-permute-done.9.refs_4_.refs_3_ = f32[4,4,8,2432]{3,2,1,0:T(8,128)} collective-permute-done((f32[4,4,8,2432]{3,2,1,0:T(8,128)}, f32[4,4,8,2432]{3,2,1,0:T(8,128)}, u32[]{:S(2)}, u32[]{:S(2)}) %collective-permute-start.9) | collective-permute-done | bytes 1245216 | tf_op jit(solution)/shard_map/ppermute | solution.py:293
  73.9 0.0 copy-done
  73.9 4.6 %inner_sums.2 = (f32[768,128]{1,0:T(8,128)S(1)}, f32[4,128,128]{2,1,0:T(8,128)S(1)}) custom-call(s32[2,16]{1,0:T(2,128)S(1)} %select_xor_fusion.refs_0_.order_ref, s32[2]{0:T(128)S(1)} %pad_add_fusion.refs_1_.info_ref, f32[96,4864]{1,0:T(8,128)S(1)} %copy-done, f32[16,4,8,2432]{3,2,1,0:T(8,128)S(1)} %collect.3.refs_3_, ...), custom_call_target="tpu_custom_call" | custom-call | flops 1358954496 | bytes 5603328 | tf_op jit(solution)/shard_map/inner_sums/pallas_call | solution.py:184
  78.5 0.0 collective-permute-done.4.refs_4_.refs_7_
  78.6 5.1 %inner_sums.3 = (f32[384,128]{1,0:T(8,128)S(1)}, f32[384,128]{1,0:T(8,128)S(1)}) custom-call(s32[2,16]{1,0:T(2,128)S(1)} %select_xor_fusion.refs_0_.order_ref, s32[2]{0:T(128)S(1)} %pad_add_fusion.refs_1_.info_ref, f32[96,4864]{1,0:T(8,128)S(1)} %copy-done, f32[16,4,8,2560]{3,2,1,0:T(8,128)S(1)} %collect.2.refs_3_, ...), custom_call_target="tpu_custom_call" | custom-call | flops 1509949440 | bytes 6225920 | tf_op jit(solution)/shard_map/inner_sums/pallas_call | solution.py:184
  83.7 8.5 %collective-permute-start.10 = (f32[384,128]{1,0:T(8,128)S(1)}, f32[384,128]{1,0:T(8,128)S(1)}, u32[]{:S(2)}, u32[]{:S(2)}) collective-permute-start(f32[384,128]{1,0:T(8,128)S(1)} %get-tuple-element.15), channel_id=1, source_target_pairs={{0,16},{16,0},{32,48},{48,32},{64,80},{80,64},{96,112},{112,96},{1... | collective-permute-start | bytes 589832 | tf_op jit(solution)/shard_map/ppermute | solution.py:309
  92.2 1.0 collective-permute-done.10
  93.3 21.4 %all_to_all.10 = f32[16,24,128]{2,1,0:T(8,128)} all-to-all(f32[16,24,128]{2,1,0:T(8,128)S(1)} %bitcast.8), channel_id=1, replica_groups={{0,32,64,96,128,160,192,224,256,288,320,352,384,416,448,480},{16,48,80,..., dimensions={0} | all-to-all | bytes 393216 | tf_op jit(solution)/shard_map/all_to_all | solution.py:305
  114.8 0.9 reduce_sum.9
  115.7 0.0 copy-start.2
  115.7 20.9 %all_to_all.11 = f32[16,24,128]{2,1,0:T(8,128)S(1)} all-to-all(f32[16,24,128]{2,1,0:T(8,128)S(1)} %broadcast_in_dim.11), channel_id=1, replica_groups={{0,32,64,96,128,160,192,224,256,288,320,352,384,416,448,480},{16,48,80,..., dimensions={0} | all-to-all | bytes 393216 | tf_op jit(solution)/shard_map/all_to_all | solution.py:305
  136.7 6.5 %all_gather.3.sum_ref = f32[768,128]{1,0:T(8,128)S(1)} all-gather(f32[384,128]{1,0:T(8,128)S(1)} %bitcast.9), channel_id=1, replica_groups={{0,16},{32,48},{64,80},{96,112},{128,144},{160,176},{192,208},{224,240}..., dimensions={0}, use_global_device_ids=true | all-gather | bytes 589824 | tf_op jit(solution)/shard_map/all_gather | solution.py:312
  143.2 3.3 %collective-permute-start.11 = (f32[384,128]{1,0:T(8,128)S(1)}, f32[384,128]{1,0:T(8,128)S(1)}, u32[]{:S(2)}, u32[]{:S(2)}) collective-permute-start(f32[384,128]{1,0:T(8,128)S(1)} %slice.12), channel_id=1, source_target_pairs={{0,3},{1,2},{2,1},{3,0},{4,7},{5,6},{6,5},{7,4},{8,11},{9,10},{10,... | collective-permute-start | bytes 589832 | tf_op jit(solution)/shard_map/ppermute | solution.py:293
  146.5 4.6 %collective-permute-done.11.rest_ref = f32[384,128]{1,0:T(8,128)S(1)} collective-permute-done((f32[384,128]{1,0:T(8,128)S(1)}, f32[384,128]{1,0:T(8,128)S(1)}, u32[]{:S(2)}, u32[]{:S(2)}) %collective-permute-start.11) | collective-permute-done | bytes 196640 | tf_op jit(solution)/shard_map/ppermute | solution.py:293
  151.2 0.0 copy-done.2
  151.2 7.3 %update.1 = f32[96,4864]{1,0:T(8,128)} custom-call(s32[2,16]{1,0:T(2,128)S(1)} %select_xor_fusion.refs_0_.order_ref, s32[2]{0:T(128)S(1)} %pad_add_fusion.refs_1_.info_ref, f32[768,128]{1,0:T(8,128)S(1)} %all_gather.3.sum_ref, f32[384,128]{1,0:T(8,128)S(1)} %collective-permute-done.11.rest_ref, f32[4,128,128]{2,1,0:T(8,128)S(1)} %get-tuple-element.16.fac_ref, ...), custom_call_target="tpu_custom_call" | custom-call | flops 1434451968 | bytes 13697024 | tf_op jit(solution)/shard_map/update/pallas_call | solution.py:257
  (8 shorter events, 0.1 us)
Async XLA Ops:
  0.0 6.5 %slice-start = ((f32[4,8,4864]{2,1,0:T(8,128)}), f32[4,8,2304]{2,1,0:T(8,128)S(1)}, s32[]{:S(2)}) async-start(f32[4,8,4864]{2,1,0:T(8,128)} %param.6), calls=%async_computation.2 | async-start | bytes 589824 | tf_op jit(solution)/shard_map/slice | solution.py:323
  1.0 9.9 %collective-permute-start = (f32[1,4,8,2560]{3,2,1,0:T(8,128)S(1)}, f32[1,4,8,2560]{3,2,1,0:T(8,128)S(1)}, u32[]{:S(2)}, u32[]{:S(2)}) collective-permute-start(f32[1,4,8,2560]{3,2,1,0:T(8,128)S(1)} %slice_bitcast_fusion), channel_id=1, source_target_pairs={{0,12},{1,13},{2,14},{3,15},{4,8},{5,9},{6,10},{7,11},{8,4},{9,5},... | collective-permute-start | bytes 983048 | tf_op jit(solution)/shard_map/ppermute | solution.py:293
  7.3 7.9 %collective-permute-start.5 = (f32[1,4,8,2432]{3,2,1,0:T(8,128)S(1)}, f32[1,4,8,2432]{3,2,1,0:T(8,128)S(1)}, u32[]{:S(2)}, u32[]{:S(2)}) collective-permute-start(f32[1,4,8,2432]{3,2,1,0:T(8,128)S(1)} %maximum_bitcast_fusion), channel_id=1, source_target_pairs={{0,4},{1,5},{2,6},{3,7},{4,0},{5,1},{6,2},{7,3},{8,12},{9,13},{10,... | collective-permute-start | bytes 933896 | tf_op jit(solution)/shard_map/ppermute | solution.py:293
  11.0 11.3 %collective-permute-start.1 = (f32[2,4,8,2560]{3,2,1,0:T(8,128)S(1)}, f32[2,4,8,2560]{3,2,1,0:T(8,128)S(1)}, u32[]{:S(2)}, u32[]{:S(2)}) collective-permute-start(f32[2,4,8,2560]{3,2,1,0:T(8,128)S(1)} %pad_maximum_fusion.2), channel_id=1, source_target_pairs={{0,4},{1,5},{2,6},{3,7},{4,0},{5,1},{6,2},{7,3},{8,12},{9,13},{10,... | collective-permute-start | bytes 1966088 | tf_op jit(solution)/shard_map/ppermute | solution.py:293
  15.3 12.5 %collective-permute-start.6 = (f32[2,4,8,2432]{3,2,1,0:T(8,128)S(1)}, f32[2,4,8,2432]{3,2,1,0:T(8,128)S(1)}, u32[]{:S(2)}, u32[]{:S(2)}) collective-permute-start(f32[2,4,8,2432]{3,2,1,0:T(8,128)S(1)} %pad_maximum_fusion.3), channel_id=1, source_target_pairs={{0,12},{1,13},{2,14},{3,15},{4,8},{5,9},{6,10},{7,11},{8,4},{9,5},... | collective-permute-start | bytes 1867784 | tf_op jit(solution)/shard_map/ppermute | solution.py:293
  22.4 29.6 %copy-start.3 = (s32[2,16]{1,0:T(2,128)S(1)}, s32[2,16]{1,0:T(2,128)}, u32[]{:S(2)}) copy-start(s32[2,16]{1,0:T(2,128)} %constant.24.clone) | copy-start | bytes 388
  22.5 29.6 %copy-start.4 = (s32[2,16]{1,0:T(2,128)S(1)}, s32[2,16]{1,0:T(2,128)}, u32[]{:S(2)}) copy-start(s32[2,16]{1,0:T(2,128)} %constant.25.clone) | copy-start | bytes 388
  22.5 27.6 %collective-permute-start.2 = (f32[4,4,8,2560]{3,2,1,0:T(8,128)S(1)}, f32[4,4,8,2560]{3,2,1,0:T(8,128)}, u32[]{:S(2)}, u32[]{:S(2)}) collective-permute-start(f32[4,4,8,2560]{3,2,1,0:T(8,128)S(1)} %pad_maximum_fusion.refs_1_.refs_4_), channel_id=1, source_target_pairs={{0,3},{1,2},{2,1},{3,0},{4,7},{5,6},{6,5},{7,4},{8,11},{9,10},{10,... | collective-permute-start | bytes 3932168 | tf_op jit(solution)/shard_map/ppermute | solution.py:293
  27.8 18.1 %collective-permute-start.7 = (f32[4,4,8,2432]{3,2,1,0:T(8,128)S(1)}, f32[4,4,8,2432]{3,2,1,0:T(8,128)}, u32[]{:S(2)}, u32[]{:S(2)}) collective-permute-start(f32[4,4,8,2432]{3,2,1,0:T(8,128)S(1)} %pad_maximum_fusion.1.refs_1_.refs_0_), channel_id=1, source_target_pairs={{0,1},{1,0},{2,3},{3,2},{4,5},{5,4},{6,7},{7,6},{8,9},{9,8},{10,11... | collective-permute-start | bytes 3735560 | tf_op jit(solution)/shard_map/ppermute | solution.py:293
  30.7 33.7 %collective-permute-start.3 = (f32[4,4,8,2560]{3,2,1,0:T(8,128)S(1)}, f32[4,4,8,2560]{3,2,1,0:T(8,128)}, u32[]{:S(2)}, u32[]{:S(2)}) collective-permute-start(f32[4,4,8,2560]{3,2,1,0:T(8,128)S(1)} %pad_maximum_fusion.refs_1_.refs_4_), channel_id=1, source_target_pairs={{0,1},{1,0},{2,3},{3,2},{4,5},{5,4},{6,7},{7,6},{8,9},{9,8},{10,11... | collective-permute-start | bytes 3932168 | tf_op jit(solution)/shard_map/ppermute | solution.py:293
  33.1 27.4 %collective-permute-start.8 = (f32[4,4,8,2432]{3,2,1,0:T(8,128)S(1)}, f32[4,4,8,2432]{3,2,1,0:T(8,128)}, u32[]{:S(2)}, u32[]{:S(2)}) collective-permute-start(f32[4,4,8,2432]{3,2,1,0:T(8,128)S(1)} %pad_maximum_fusion.1.refs_1_.refs_0_), channel_id=1, source_target_pairs={{0,3},{1,2},{2,1},{3,0},{4,7},{5,6},{6,5},{7,4},{8,11},{9,10},{10,... | collective-permute-start | bytes 3735560 | tf_op jit(solution)/shard_map/ppermute | solution.py:293
  45.9 28.0 %collective-permute-start.9 = (f32[4,4,8,2432]{3,2,1,0:T(8,128)}, f32[4,4,8,2432]{3,2,1,0:T(8,128)}, u32[]{:S(2)}, u32[]{:S(2)}) collective-permute-start(f32[4,4,8,2432]{3,2,1,0:T(8,128)} %collective-permute-done.7.refs_2_.refs_1_), channel_id=1, source_target_pairs={{0,3},{1,2},{2,1},{3,0},{4,7},{5,6},{6,5},{7,4},{8,11},{9,10},{10,... | collective-permute-start | bytes 3735560 | tf_op jit(solution)/shard_map/ppermute | solution.py:293
  50.0 28.5 %collective-permute-start.4 = (f32[4,4,8,2560]{3,2,1,0:T(8,128)}, f32[4,4,8,2560]{3,2,1,0:T(8,128)}, u32[]{:S(2)}, u32[]{:S(2)}) collective-permute-start(f32[4,4,8,2560]{3,2,1,0:T(8,128)} %collective-permute-done.2.refs_2_.refs_5_), channel_id=1, source_target_pairs={{0,1},{1,0},{2,3},{3,2},{4,5},{5,4},{6,7},{7,6},{8,9},{9,8},{10,11... | collective-permute-start | bytes 3932168 | tf_op jit(solution)/shard_map/ppermute | solution.py:293
  63.4 1.0 copy-start.1
  64.4 9.5 %copy-start = (f32[96,4864]{1,0:T(8,128)S(1)}, f32[96,4864]{1,0:T(8,128)}, u32[]{:S(2)}) copy-start(f32[96,4864]{1,0:T(8,128)} %eig_ref.1) | copy-start | bytes 5603332
  83.7 9.6 %collective-permute-start.10 = (f32[384,128]{1,0:T(8,128)S(1)}, f32[384,128]{1,0:T(8,128)S(1)}, u32[]{:S(2)}, u32[]{:S(2)}) collective-permute-start(f32[384,128]{1,0:T(8,128)S(1)} %get-tuple-element.15), channel_id=1, source_target_pairs={{0,16},{16,0},{32,48},{48,32},{64,80},{80,64},{96,112},{112,96},{1... | collective-permute-start | bytes 589832 | tf_op jit(solution)/shard_map/ppermute | solution.py:309
  115.7 35.5 %copy-start.2 = (f32[4,4,8,2432]{3,2,1,0:T(8,128)S(1)}, f32[4,4,8,2432]{3,2,1,0:T(8,128)}, u32[]{:S(2)}) copy-start(f32[4,4,8,2432]{3,2,1,0:T(8,128)} %copy-done.1) | copy-start | bytes 3735556
  143.2 7.9 %collective-permute-start.11 = (f32[384,128]{1,0:T(8,128)S(1)}, f32[384,128]{1,0:T(8,128)S(1)}, u32[]{:S(2)}, u32[]{:S(2)}) collective-permute-start(f32[384,128]{1,0:T(8,128)S(1)} %slice.12), channel_id=1, source_target_pairs={{0,3},{1,2},{2,1},{3,0},{4,7},{5,6},{6,5},{7,4},{8,11},{9,10},{10,... | collective-permute-start | bytes 589832 | tf_op jit(solution)/shard_map/ppermute | solution.py:293

commit v6 on v5

--- a/solution.py
+++ b/solution.py
@@ -15,7 +15,7 @@
     ((X_NEAR, X_WRAP, Y_NEAR, Y_WRAP), (Y_NEAR, Y_WRAP, X_NEAR, X_WRAP)),
     ((X_WRAP, X_NEAR, Y_WRAP, Y_NEAR), (Y_WRAP, Y_NEAR, X_WRAP, X_NEAR)),
 )
-PARTNER = (Y_WRAP, X_WRAP)
+PARTNER = X_WRAP
 
 
 def split(x):
@@ -309,7 +309,16 @@
         mine = keep + lax.ppermute(give, "prow", [(i, i ^ 1) for i in range(nprow)])
         part = jnp.sum(along_z(mine.reshape(nz, half // nz, kb)), axis=0)
         whole = along_z(jnp.broadcast_to(part, (nz,) + part.shape)).reshape(half, kb)
-        return lax.all_gather(whole, "prow", axis=0, tiled=True, axis_index_groups=in_chip)
+        pairs = [
+            (row * npcol + at, row * npcol + (at ^ PARTNER))
+            for row in range(1, nprow, 2)
+            for at in range(npcol)
+        ]
+        other = lax.ppermute(whole, ("prow", "pcol"), pairs)
+        sums = lax.all_gather(whole, "prow", axis=0, tiled=True, axis_index_groups=in_chip)
+        sums, other = lax.optimization_barrier((sums, other))
+        rest = lax.all_gather(other, "prow", axis=0, tiled=True, axis_index_groups=in_chip)
+        return sums, rest[half:]
 
     def per_device(eig, house_vecs, wy_factor):
         nblk, _, kb = wy_factor.shape
@@ -331,8 +340,7 @@
         keep, give = inner_sums(
             1, cols - data, order, info, eig, (early_b, part_b[3]), before
         )
-        sums = sum_over_rows(keep, give)
-        rest = send(sums[nblk * rows :], PARTNER)
+        sums, rest = sum_over_rows(keep, give)
         return update(order, info, sums, rest, factors, eig, (part_a, part_b))
 
     return jax.shard_map(

time: 159 us -> 157 us (0.987)
  the two profiles are of different devices: /device:TPU:1 before, /device:TPU:41 now
where the time goes in v6:
time: 157 us
  blocking collectives  56.1 us (36%)
  starting transfers between devices  40.4 us (26%)
  waiting for transfers between devices  32.9 us (21%)
  Pallas kernels  22.7 us (14%)
  local copies, waits for them, and re-layouts  2.12 us (1%)
  other arithmetic  2.07 us (1%)
    all_to_all x2, blocking collectives, along_z(): return lax.all_to_all(x, 'prow', 0, 0, axis_index_groups=groups)  51.7 us
    ppermute x10, starting transfers between devices, send(): return lax.ppermute(x, ('prow', 'pcol'), pairs)  32.2 us
    ppermute x10, waiting for transfers between devices, send(): return lax.ppermute(x, ('prow', 'pcol'), pairs)  28.2 us
    pallas_call x2, Pallas kernels, inner_sums(): pl.pallas_call(lambda *refs: inner_kernel(part, data, *refs), out_shape=o...  9.74 us
    pallas_call x1, Pallas kernels, update(): pl.pallas_call(update_kernel, out_shape=jax.ShapeDtypeStruct(eig.shape, F...  7.28 us
    ppermute x1, starting transfers between devices, sum_over_rows(): mine = keep + lax.ppermute(give, 'prow', [(i, i ^ 1) for i in range(nprow)])  6.32 us
    pallas_call x2, Pallas kernels, collect(): pl.pallas_call(lambda *refs: collect_kernel(part, *refs), out_shape=jax.S...  5.7 us
    ppermute x1, waiting for transfers between devices, sum_over_rows(): other = lax.ppermute(whole, ('prow', 'pcol'), pairs)  3.61 us
  transfers between devices with their start and end apart: 12, of which 8 were waited for; matrix products, arithmetic and copies ran while one was open for 1% of the time, Pallas kernels for 7%

profile of v6, /device:TPU:41, one launch (start us, length us, event | category | flops | bytes accessed | tf_op | source)
XLA Modules:
  0.0 156.7 jit_solution(14494306291317549230)
XLA Ops:
  0.0 1.0 slice_bitcast_fusion
  1.0 3.2 %collective-permute-start = (f32[1,4,8,2560]{3,2,1,0:T(8,128)S(1)}, f32[1,4,8,2560]{3,2,1,0:T(8,128)S(1)}, u32[]{:S(2)}, u32[]{:S(2)}) collective-permute-start(f32[1,4,8,2560]{3,2,1,0:T(8,128)S(1)} %slice_bitcast_fusion), channel_id=1, source_target_pairs={{0,12},{1,13},{2,14},{3,15},{4,8},{5,9},{6,10},{7,11},{8,4},{9,5},... | collective-permute-start | bytes 983048 | tf_op jit(solution)/shard_map/ppermute | solution.py:293
  4.3 0.0 slice-done
  4.3 0.7 maximum_bitcast_fusion
  5.0 3.5 %collective-permute-start.5 = (f32[1,4,8,2432]{3,2,1,0:T(8,128)S(1)}, f32[1,4,8,2432]{3,2,1,0:T(8,128)S(1)}, u32[]{:S(2)}, u32[]{:S(2)}) collective-permute-start(f32[1,4,8,2432]{3,2,1,0:T(8,128)S(1)} %maximum_bitcast_fusion), channel_id=1, source_target_pairs={{0,4},{1,5},{2,6},{3,7},{4,0},{5,1},{6,2},{7,3},{8,12},{9,13},{10,... | collective-permute-start | bytes 933896 | tf_op jit(solution)/shard_map/ppermute | solution.py:293
  8.5 0.6 collective-permute-done
  9.2 3.4 %collective-permute-start.1 = (f32[2,4,8,2560]{3,2,1,0:T(8,128)S(1)}, f32[2,4,8,2560]{3,2,1,0:T(8,128)S(1)}, u32[]{:S(2)}, u32[]{:S(2)}) collective-permute-start(f32[2,4,8,2560]{3,2,1,0:T(8,128)S(1)} %pad_maximum_fusion.2), channel_id=1, source_target_pairs={{0,4},{1,5},{2,6},{3,7},{4,0},{5,1},{6,2},{7,3},{8,12},{9,13},{10,... | collective-permute-start | bytes 1966088 | tf_op jit(solution)/shard_map/ppermute | solution.py:293
  12.6 0.5 collective-permute-done.5
  13.1 3.5 %collective-permute-start.6 = (f32[2,4,8,2432]{3,2,1,0:T(8,128)S(1)}, f32[2,4,8,2432]{3,2,1,0:T(8,128)S(1)}, u32[]{:S(2)}, u32[]{:S(2)}) collective-permute-start(f32[2,4,8,2432]{3,2,1,0:T(8,128)S(1)} %pad_maximum_fusion.3), channel_id=1, source_target_pairs={{0,12},{1,13},{2,14},{3,15},{4,8},{5,9},{6,10},{7,11},{8,4},{9,5},... | collective-permute-start | bytes 1867784 | tf_op jit(solution)/shard_map/ppermute | solution.py:293
  16.6 4.2 %collective-permute-done.1 = f32[2,4,8,2560]{3,2,1,0:T(8,128)S(1)} collective-permute-done((f32[2,4,8,2560]{3,2,1,0:T(8,128)S(1)}, f32[2,4,8,2560]{3,2,1,0:T(8,128)S(1)}, u32[]{:S(2)}, u32[]{:S(2)}) %collective-permute-start.1) | collective-permute-done | bytes 655392 | tf_op jit(solution)/shard_map/ppermute | solution.py:293
  20.8 0.1 pad_maximum_fusion.refs_1_.refs_4_
  20.9 0.0 copy-start.3
  20.9 0.0 copy-start.4
  21.0 4.4 %collective-permute-start.2 = (f32[4,4,8,2560]{3,2,1,0:T(8,128)S(1)}, f32[4,4,8,2560]{3,2,1,0:T(8,128)}, u32[]{:S(2)}, u32[]{:S(2)}) collective-permute-start(f32[4,4,8,2560]{3,2,1,0:T(8,128)S(1)} %pad_maximum_fusion.refs_1_.refs_4_), channel_id=1, source_target_pairs={{0,3},{1,2},{2,1},{3,0},{4,7},{5,6},{6,5},{7,4},{8,11},{9,10},{10,... | collective-permute-start | bytes 3932168 | tf_op jit(solution)/shard_map/ppermute | solution.py:293
  25.3 0.0 collective-permute-done.6
  25.4 0.1 pad_maximum_fusion.1.refs_1_.refs_0_
  25.5 2.2 %collective-permute-start.7 = (f32[4,4,8,2432]{3,2,1,0:T(8,128)S(1)}, f32[4,4,8,2432]{3,2,1,0:T(8,128)}, u32[]{:S(2)}, u32[]{:S(2)}) collective-permute-start(f32[4,4,8,2432]{3,2,1,0:T(8,128)S(1)} %pad_maximum_fusion.1.refs_1_.refs_0_), channel_id=1, source_target_pairs={{0,1},{1,0},{2,3},{3,2},{4,5},{5,4},{6,7},{7,6},{8,9},{9,8},{10,11... | collective-permute-start | bytes 3735560 | tf_op jit(solution)/shard_map/ppermute | solution.py:293
  27.7 3.1 %collective-permute-start.3 = (f32[4,4,8,2560]{3,2,1,0:T(8,128)S(1)}, f32[4,4,8,2560]{3,2,1,0:T(8,128)}, u32[]{:S(2)}, u32[]{:S(2)}) collective-permute-start(f32[4,4,8,2560]{3,2,1,0:T(8,128)S(1)} %pad_maximum_fusion.refs_1_.refs_4_), channel_id=1, source_target_pairs={{0,1},{1,0},{2,3},{3,2},{4,5},{5,4},{6,7},{7,6},{8,9},{9,8},{10,11... | collective-permute-start | bytes 3932168 | tf_op jit(solution)/shard_map/ppermute | solution.py:293
  30.8 3.5 %collective-permute-start.8 = (f32[4,4,8,2432]{3,2,1,0:T(8,128)S(1)}, f32[4,4,8,2432]{3,2,1,0:T(8,128)}, u32[]{:S(2)}, u32[]{:S(2)}) collective-permute-start(f32[4,4,8,2432]{3,2,1,0:T(8,128)S(1)} %pad_maximum_fusion.1.refs_1_.refs_0_), channel_id=1, source_target_pairs={{0,3},{1,2},{2,1},{3,0},{4,7},{5,6},{6,5},{7,4},{8,11},{9,10},{10,... | collective-permute-start | bytes 3735560 | tf_op jit(solution)/shard_map/ppermute | solution.py:293
  34.3 9.2 %collective-permute-done.7.refs_2_.refs_1_ = f32[4,4,8,2432]{3,2,1,0:T(8,128)} collective-permute-done((f32[4,4,8,2432]{3,2,1,0:T(8,128)S(1)}, f32[4,4,8,2432]{3,2,1,0:T(8,128)}, u32[]{:S(2)}, u32[]{:S(2)}) %collective-permute-start.7) | collective-permute-done | bytes 1245216 | tf_op jit(solution)/shard_map/ppermute | solution.py:293
  43.5 3.5 %collective-permute-start.9 = (f32[4,4,8,2432]{3,2,1,0:T(8,128)}, f32[4,4,8,2432]{3,2,1,0:T(8,128)}, u32[]{:S(2)}, u32[]{:S(2)}) collective-permute-start(f32[4,4,8,2432]{3,2,1,0:T(8,128)} %collective-permute-done.7.refs_2_.refs_1_), channel_id=1, source_target_pairs={{0,3},{1,2},{2,1},{3,0},{4,7},{5,6},{6,5},{7,4},{8,11},{9,10},{10,... | collective-permute-start | bytes 3735560 | tf_op jit(solution)/shard_map/ppermute | solution.py:293
  47.1 0.0 collective-permute-done.2.refs_2_.refs_5_
  47.1 1.9 %collective-permute-start.4 = (f32[4,4,8,2560]{3,2,1,0:T(8,128)}, f32[4,4,8,2560]{3,2,1,0:T(8,128)}, u32[]{:S(2)}, u32[]{:S(2)}) collective-permute-start(f32[4,4,8,2560]{3,2,1,0:T(8,128)} %collective-permute-done.2.refs_2_.refs_5_), channel_id=1, source_target_pairs={{0,1},{1,0},{2,3},{3,2},{4,5},{5,4},{6,7},{7,6},{8,9},{9,8},{10,11... | collective-permute-start | bytes 3932168 | tf_op jit(solution)/shard_map/ppermute | solution.py:293
  49.0 0.1 pad_add_fusion.refs_1_.info_ref
  49.1 0.0 copy-done.3
  49.1 0.0 copy-done.4
  49.1 7.0 %collective-permute-done.8.refs_3_.refs_2_ = f32[4,4,8,2432]{3,2,1,0:T(8,128)} collective-permute-done((f32[4,4,8,2432]{3,2,1,0:T(8,128)S(1)}, f32[4,4,8,2432]{3,2,1,0:T(8,128)}, u32[]{:S(2)}, u32[]{:S(2)}) %collective-permute-start.8) | collective-permute-done | bytes 1245216 | tf_op jit(solution)/shard_map/ppermute | solution.py:293
  56.1 2.8 %collect.3.refs_3_ = f32[16,4,8,2432]{3,2,1,0:T(8,128)S(1)} custom-call(s32[2,16]{1,0:T(2,128)S(1)} %select_xor_fusion.refs_0_.order_ref, f32[4,4,8,2432]{3,2,1,0:T(8,128)S(1)} %pad_maximum_fusion.1.refs_1_.refs_0_, f32[4,4,8,2432]{3,2,1,0:T(8,128)} %collective-permute-done.7.refs_2_.refs_1_, f32[4,4,8,2432]{3,2,1,0:T(8,128)} %collective-permute-done.8.refs_3_.refs_2_), custom_call_target="tpu_custom_call" | custom-call | bytes 9961472 | tf_op jit(solution)/shard_map/collect/pallas_call | solution.py:82
  58.9 0.0 copy-start.1
  58.9 1.0 copy-done.1
  60.0 0.0 collective-permute-done.3.refs_3_.refs_6_
  60.0 2.9 %collect.2.refs_3_ = f32[16,4,8,2560]{3,2,1,0:T(8,128)S(1)} custom-call(s32[2,16]{1,0:T(2,128)S(1)} %select_xor_fusion.refs_0_.order_ref, f32[4,4,8,2560]{3,2,1,0:T(8,128)S(1)} %pad_maximum_fusion.refs_1_.refs_4_, f32[4,4,8,2560]{3,2,1,0:T(8,128)} %collective-permute-done.2.refs_2_.refs_5_, f32[4,4,8,2560]{3,2,1,0:T(8,128)} %collective-permute-done.3.refs_3_.refs_6_), custom_call_target="tpu_custom_call" | custom-call | bytes 10485760 | tf_op jit(solution)/shard_map/collect/pallas_call | solution.py:82
  62.9 6.6 %collective-permute-done.9.refs_4_.refs_3_ = f32[4,4,8,2432]{3,2,1,0:T(8,128)} collective-permute-done((f32[4,4,8,2432]{3,2,1,0:T(8,128)}, f32[4,4,8,2432]{3,2,1,0:T(8,128)}, u32[]{:S(2)}, u32[]{:S(2)}) %collective-permute-start.9) | collective-permute-done | bytes 1245216 | tf_op jit(solution)/shard_map/ppermute | solution.py:293
  69.5 0.0 copy-done
  69.5 4.6 %inner_sums.2 = (f32[768,128]{1,0:T(8,128)S(1)}, f32[4,128,128]{2,1,0:T(8,128)S(1)}) custom-call(s32[2,16]{1,0:T(2,128)S(1)} %select_xor_fusion.refs_0_.order_ref, s32[2]{0:T(128)S(1)} %pad_add_fusion.refs_1_.info_ref, f32[96,4864]{1,0:T(8,128)S(1)} %copy-done, f32[16,4,8,2432]{3,2,1,0:T(8,128)S(1)} %collect.3.refs_3_, ...), custom_call_target="tpu_custom_call" | custom-call | flops 1358954496 | bytes 5603328 | tf_op jit(solution)/shard_map/inner_sums/pallas_call | solution.py:184
  74.1 0.0 collective-permute-done.4.refs_4_.refs_7_
  74.1 5.1 %inner_sums.3 = (f32[384,128]{1,0:T(8,128)S(1)}, f32[384,128]{1,0:T(8,128)S(1)}) custom-call(s32[2,16]{1,0:T(2,128)S(1)} %select_xor_fusion.refs_0_.order_ref, s32[2]{0:T(128)S(1)} %pad_add_fusion.refs_1_.info_ref, f32[96,4864]{1,0:T(8,128)S(1)} %copy-done, f32[16,4,8,2560]{3,2,1,0:T(8,128)S(1)} %collect.2.refs_3_, ...), custom_call_target="tpu_custom_call" | custom-call | flops 1509949440 | bytes 6225920 | tf_op jit(solution)/shard_map/inner_sums/pallas_call | solution.py:184
  79.2 6.3 %collective-permute-start.10 = (f32[384,128]{1,0:T(8,128)S(1)}, f32[384,128]{1,0:T(8,128)S(1)}, u32[]{:S(2)}, u32[]{:S(2)}) collective-permute-start(f32[384,128]{1,0:T(8,128)S(1)} %get-tuple-element.17), channel_id=1, source_target_pairs={{0,16},{16,0},{32,48},{48,32},{64,80},{80,64},{96,112},{112,96},{1... | collective-permute-start | bytes 589832 | tf_op jit(solution)/shard_map/ppermute | solution.py:309
  85.6 1.0 collective-permute-done.10
  86.6 30.6 %all_to_all.10 = f32[16,24,128]{2,1,0:T(8,128)} all-to-all(f32[16,24,128]{2,1,0:T(8,128)S(1)} %bitcast.10), channel_id=1, replica_groups={{0,32,64,96,128,160,192,224,256,288,320,352,384,416,448,480},{16,48,80,..., dimensions={0} | all-to-all | bytes 393216 | tf_op jit(solution)/shard_map/all_to_all | solution.py:305
  117.3 0.9 reduce_sum.9
  118.2 0.0 copy-start.2
  118.3 21.1 %all_to_all.11 = f32[16,24,128]{2,1,0:T(8,128)S(1)} all-to-all(f32[16,24,128]{2,1,0:T(8,128)S(1)} %broadcast_in_dim.11), channel_id=1, replica_groups={{0,32,64,96,128,160,192,224,256,288,320,352,384,416,448,480},{16,48,80,..., dimensions={0} | all-to-all | bytes 393216 | tf_op jit(solution)/shard_map/all_to_all | solution.py:305
  139.3 1.9 %collective-permute-start.11 = (f32[384,128]{1,0:T(8,128)S(1)}, f32[384,128]{1,0:T(8,128)S(1)}, u32[]{:S(2)}, u32[]{:S(2)}) collective-permute-start(f32[384,128]{1,0:T(8,128)S(1)} %bitcast.8), channel_id=1, source_target_pairs={{16,28},{17,29},{18,30},{19,31},{20,24},{21,25},{22,26},{23,27},{2... | collective-permute-start | bytes 589832 | tf_op jit(solution)/shard_map/ppermute | solution.py:317
  141.3 2.1 %all_gather.6.sum_ref = f32[768,128]{1,0:T(8,128)S(1)} all-gather(f32[384,128]{1,0:T(8,128)S(1)} %bitcast.9), channel_id=1, replica_groups={{0,16},{32,48},{64,80},{96,112},{128,144},{160,176},{192,208},{224,240}..., dimensions={0}, use_global_device_ids=true | all-gather | bytes 589824 | tf_op jit(solution)/shard_map/all_gather | solution.py:318
  143.3 3.6 %collective-permute-done.11 = f32[384,128]{1,0:T(8,128)S(1)} collective-permute-done((f32[384,128]{1,0:T(8,128)S(1)}, f32[384,128]{1,0:T(8,128)S(1)}, u32[]{:S(2)}, u32[]{:S(2)}) %collective-permute-start.11) | collective-permute-done | bytes 196640 | tf_op jit(solution)/shard_map/ppermute | solution.py:317
  147.0 2.3 %all_gather.7 = f32[768,128]{1,0:T(8,128)S(1)} all-gather(f32[384,128]{1,0:T(8,128)S(1)} %collective-permute-done.11), channel_id=1, replica_groups={{0,16},{32,48},{64,80},{96,112},{128,144},{160,176},{192,208},{224,240}..., dimensions={0}, use_global_device_ids=true | all-gather | bytes 589824 | tf_op jit(solution)/shard_map/all_gather | solution.py:320
  149.2 7.3 %update.1 = f32[96,4864]{1,0:T(8,128)} custom-call(s32[2,16]{1,0:T(2,128)S(1)} %select_xor_fusion.refs_0_.order_ref, s32[2]{0:T(128)S(1)} %pad_add_fusion.refs_1_.info_ref, f32[768,128]{1,0:T(8,128)S(1)} %all_gather.6.sum_ref, f32[384,128]{1,0:T(8,128)S(1)} %slice.12.rest_ref, f32[4,128,128]{2,1,0:T(8,128)S(1)} %get-tuple-element.20.fac_ref, ...), custom_call_target="tpu_custom_call" | custom-call | flops 1434451968 | bytes 13697024 | tf_op jit(solution)/shard_map/update/pallas_call | solution.py:257
  (9 shorter events, 0.1 us)
Async XLA Ops:
  0.0 4.3 %slice-start = ((f32[4,8,4864]{2,1,0:T(8,128)}), f32[4,8,2304]{2,1,0:T(8,128)S(1)}, s32[]{:S(2)}) async-start(f32[4,8,4864]{2,1,0:T(8,128)} %param.6), calls=%async_computation.2 | async-start | bytes 589824 | tf_op jit(solution)/shard_map/slice | solution.py:332
  1.0 8.1 %collective-permute-start = (f32[1,4,8,2560]{3,2,1,0:T(8,128)S(1)}, f32[1,4,8,2560]{3,2,1,0:T(8,128)S(1)}, u32[]{:S(2)}, u32[]{:S(2)}) collective-permute-start(f32[1,4,8,2560]{3,2,1,0:T(8,128)S(1)} %slice_bitcast_fusion), channel_id=1, source_target_pairs={{0,12},{1,13},{2,14},{3,15},{4,8},{5,9},{6,10},{7,11},{8,4},{9,5},... | collective-permute-start | bytes 983048 | tf_op jit(solution)/shard_map/ppermute | solution.py:293
  5.0 8.1 %collective-permute-start.5 = (f32[1,4,8,2432]{3,2,1,0:T(8,128)S(1)}, f32[1,4,8,2432]{3,2,1,0:T(8,128)S(1)}, u32[]{:S(2)}, u32[]{:S(2)}) collective-permute-start(f32[1,4,8,2432]{3,2,1,0:T(8,128)S(1)} %maximum_bitcast_fusion), channel_id=1, source_target_pairs={{0,4},{1,5},{2,6},{3,7},{4,0},{5,1},{6,2},{7,3},{8,12},{9,13},{10,... | collective-permute-start | bytes 933896 | tf_op jit(solution)/shard_map/ppermute | solution.py:293
  9.2 11.6 %collective-permute-start.1 = (f32[2,4,8,2560]{3,2,1,0:T(8,128)S(1)}, f32[2,4,8,2560]{3,2,1,0:T(8,128)S(1)}, u32[]{:S(2)}, u32[]{:S(2)}) collective-permute-start(f32[2,4,8,2560]{3,2,1,0:T(8,128)S(1)} %pad_maximum_fusion.2), channel_id=1, source_target_pairs={{0,4},{1,5},{2,6},{3,7},{4,0},{5,1},{6,2},{7,3},{8,12},{9,13},{10,... | collective-permute-start | bytes 1966088 | tf_op jit(solution)/shard_map/ppermute | solution.py:293
  13.1 12.2 %collective-permute-start.6 = (f32[2,4,8,2432]{3,2,1,0:T(8,128)S(1)}, f32[2,4,8,2432]{3,2,1,0:T(8,128)S(1)}, u32[]{:S(2)}, u32[]{:S(2)}) collective-permute-start(f32[2,4,8,2432]{3,2,1,0:T(8,128)S(1)} %pad_maximum_fusion.3), channel_id=1, source_target_pairs={{0,12},{1,13},{2,14},{3,15},{4,8},{5,9},{6,10},{7,11},{8,4},{9,5},... | collective-permute-start | bytes 1867784 | tf_op jit(solution)/shard_map/ppermute | solution.py:293
  20.9 28.2 %copy-start.3 = (s32[2,16]{1,0:T(2,128)S(1)}, s32[2,16]{1,0:T(2,128)}, u32[]{:S(2)}) copy-start(s32[2,16]{1,0:T(2,128)} %constant.24.clone) | copy-start | bytes 388
  20.9 28.1 %copy-start.4 = (s32[2,16]{1,0:T(2,128)S(1)}, s32[2,16]{1,0:T(2,128)}, u32[]{:S(2)}) copy-start(s32[2,16]{1,0:T(2,128)} %constant.25.clone) | copy-start | bytes 388
  21.0 26.1 %collective-permute-start.2 = (f32[4,4,8,2560]{3,2,1,0:T(8,128)S(1)}, f32[4,4,8,2560]{3,2,1,0:T(8,128)}, u32[]{:S(2)}, u32[]{:S(2)}) collective-permute-start(f32[4,4,8,2560]{3,2,1,0:T(8,128)S(1)} %pad_maximum_fusion.refs_1_.refs_4_), channel_id=1, source_target_pairs={{0,3},{1,2},{2,1},{3,0},{4,7},{5,6},{6,5},{7,4},{8,11},{9,10},{10,... | collective-permute-start | bytes 3932168 | tf_op jit(solution)/shard_map/ppermute | solution.py:293
  25.5 18.1 %collective-permute-start.7 = (f32[4,4,8,2432]{3,2,1,0:T(8,128)S(1)}, f32[4,4,8,2432]{3,2,1,0:T(8,128)}, u32[]{:S(2)}, u32[]{:S(2)}) collective-permute-start(f32[4,4,8,2432]{3,2,1,0:T(8,128)S(1)} %pad_maximum_fusion.1.refs_1_.refs_0_), channel_id=1, source_target_pairs={{0,1},{1,0},{2,3},{3,2},{4,5},{5,4},{6,7},{7,6},{8,9},{9,8},{10,11... | collective-permute-start | bytes 3735560 | tf_op jit(solution)/shard_map/ppermute | solution.py:293
  27.7 32.3 %collective-permute-start.3 = (f32[4,4,8,2560]{3,2,1,0:T(8,128)S(1)}, f32[4,4,8,2560]{3,2,1,0:T(8,128)}, u32[]{:S(2)}, u32[]{:S(2)}) collective-permute-start(f32[4,4,8,2560]{3,2,1,0:T(8,128)S(1)} %pad_maximum_fusion.refs_1_.refs_4_), channel_id=1, source_target_pairs={{0,1},{1,0},{2,3},{3,2},{4,5},{5,4},{6,7},{7,6},{8,9},{9,8},{10,11... | collective-permute-start | bytes 3932168 | tf_op jit(solution)/shard_map/ppermute | solution.py:293
  30.8 25.4 %collective-permute-start.8 = (f32[4,4,8,2432]{3,2,1,0:T(8,128)S(1)}, f32[4,4,8,2432]{3,2,1,0:T(8,128)}, u32[]{:S(2)}, u32[]{:S(2)}) collective-permute-start(f32[4,4,8,2432]{3,2,1,0:T(8,128)S(1)} %pad_maximum_fusion.1.refs_1_.refs_0_), channel_id=1, source_target_pairs={{0,3},{1,2},{2,1},{3,0},{4,7},{5,6},{6,5},{7,4},{8,11},{9,10},{10,... | collective-permute-start | bytes 3735560 | tf_op jit(solution)/shard_map/ppermute | solution.py:293
  43.5 26.0 %collective-permute-start.9 = (f32[4,4,8,2432]{3,2,1,0:T(8,128)}, f32[4,4,8,2432]{3,2,1,0:T(8,128)}, u32[]{:S(2)}, u32[]{:S(2)}) collective-permute-start(f32[4,4,8,2432]{3,2,1,0:T(8,128)} %collective-permute-done.7.refs_2_.refs_1_), channel_id=1, source_target_pairs={{0,3},{1,2},{2,1},{3,0},{4,7},{5,6},{6,5},{7,4},{8,11},{9,10},{10,... | collective-permute-start | bytes 3735560 | tf_op jit(solution)/shard_map/ppermute | solution.py:293
  47.1 27.0 %collective-permute-start.4 = (f32[4,4,8,2560]{3,2,1,0:T(8,128)}, f32[4,4,8,2560]{3,2,1,0:T(8,128)}, u32[]{:S(2)}, u32[]{:S(2)}) collective-permute-start(f32[4,4,8,2560]{3,2,1,0:T(8,128)} %collective-permute-done.2.refs_2_.refs_5_), channel_id=1, source_target_pairs={{0,1},{1,0},{2,3},{3,2},{4,5},{5,4},{6,7},{7,6},{8,9},{9,8},{10,11... | collective-permute-start | bytes 3932168 | tf_op jit(solution)/shard_map/ppermute | solution.py:293
  58.9 1.0 copy-start.1
  60.0 9.5 %copy-start = (f32[96,4864]{1,0:T(8,128)S(1)}, f32[96,4864]{1,0:T(8,128)}, u32[]{:S(2)}) copy-start(f32[96,4864]{1,0:T(8,128)} %eig_ref.1) | copy-start | bytes 5603332
  79.2 7.4 %collective-permute-start.10 = (f32[384,128]{1,0:T(8,128)S(1)}, f32[384,128]{1,0:T(8,128)S(1)}, u32[]{:S(2)}, u32[]{:S(2)}) collective-permute-start(f32[384,128]{1,0:T(8,128)S(1)} %get-tuple-element.17), channel_id=1, source_target_pairs={{0,16},{16,0},{32,48},{48,32},{64,80},{80,64},{96,112},{112,96},{1... | collective-permute-start | bytes 589832 | tf_op jit(solution)/shard_map/ppermute | solution.py:309
  118.2 31.0 %copy-start.2 = (f32[4,4,8,2432]{3,2,1,0:T(8,128)S(1)}, f32[4,4,8,2432]{3,2,1,0:T(8,128)}, u32[]{:S(2)}) copy-start(f32[4,4,8,2432]{3,2,1,0:T(8,128)} %copy-done.1) | copy-start | bytes 3735556
  139.3 7.6 %collective-permute-start.11 = (f32[384,128]{1,0:T(8,128)S(1)}, f32[384,128]{1,0:T(8,128)S(1)}, u32[]{:S(2)}, u32[]{:S(2)}) collective-permute-start(f32[384,128]{1,0:T(8,128)S(1)} %bitcast.8), channel_id=1, source_target_pairs={{16,28},{17,29},{18,30},{19,31},{20,24},{21,25},{22,26},{23,27},{2... | collective-permute-start | bytes 589832 | tf_op jit(solution)/shard_map/ppermute | solution.py:317

commit v7 on v6

--- a/solution.py
+++ b/solution.py
@@ -219,10 +219,10 @@
             mine = sum_ref[below + at : below + at + kb]
             rest = rest_ref[at : at + kb]
             gram = jnp.where((parity == 0) == (index < len(pairs) // 2), mine, rest)
-            proj = proj - exact(scaled[b], gram, NN)
-        scaled.append(exact(proj, fac_ref[c], NT))
+            proj = proj - product(scaled[b], split(gram), NN)
+        scaled.append(split(product(split(proj), split(fac_ref[c]), NT)))
         lane = slice(c * kb, (c + 1) * kb)
-        high[:, lane], low[:, lane] = split(scaled[c])
+        high[:, lane], low[:, lane] = scaled[c]
 
     left = (high[...], low[...])
     out_copies = []
@@ -237,11 +237,15 @@
                 axis=0,
             )
             out[:, here] = eig_ref[:, here] - product(left, split(right), NN)
-        lane = pl.ds(start, width)
-        out_copies.append(
-            pltpu.make_async_copy(out.at[:, lane], out_ref.at[:, lane], out_sems.at[part])
-        )
-        out_copies[part].start()
+            if at + 256 >= width or at % 1024 == 768:
+                first = at // 1024 * 1024
+                lane = pl.ds(start + first, at + size - first)
+                out_copies.append(
+                    pltpu.make_async_copy(
+                        out.at[:, lane], out_ref.at[:, lane], out_sems.at[len(out_copies)]
+                    )
+                )
+                out_copies[-1].start()
     for copy in out_copies:
         copy.wait()
 
@@ -266,7 +270,7 @@
             pltpu.VMEM((rows, nblk * kb), BF16),
             pltpu.VMEM((rows, nblk * kb), BF16),
             pltpu.SemaphoreType.DMA((2, owners)),
-            pltpu.SemaphoreType.DMA((2,)),
+            pltpu.SemaphoreType.DMA((8,)),
         ],
         compiler_params=pltpu.CompilerParams(vmem_limit_bytes=40 * 2**20),
         cost_estimate=pl.CostEstimate(

time: 157 us -> 157 us (level)
  no operation moved by 1% of the time
where the time goes in v7:
time: 157 us; the launch traced here: 156 us
  blocking collectives  56.1 us (36%)
  starting transfers between devices  40.4 us (26%)
  waiting for transfers between devices  32.9 us (21%)
  Pallas kernels  22.1 us (14%)
  local copies, waits for them, and re-layouts  2.12 us (1%)
  other arithmetic  2.07 us (1%)
    all_to_all x2, blocking collectives, along_z(): return lax.all_to_all(x, 'prow', 0, 0, axis_index_groups=groups)  51.7 us
    ppermute x10, starting transfers between devices, send(): return lax.ppermute(x, ('prow', 'pcol'), pairs)  32.2 us
    ppermute x10, waiting for transfers between devices, send(): return lax.ppermute(x, ('prow', 'pcol'), pairs)  28.2 us
    pallas_call x2, Pallas kernels, inner_sums(): pl.pallas_call(lambda *refs: inner_kernel(part, data, *refs), out_shape=o...  9.74 us
    pallas_call x1, Pallas kernels, update(): pl.pallas_call(update_kernel, out_shape=jax.ShapeDtypeStruct(eig.shape, F...  6.64 us
    ppermute x1, starting transfers between devices, sum_over_rows(): mine = keep + lax.ppermute(give, 'prow', [(i, i ^ 1) for i in range(nprow)])  6.32 us
    pallas_call x2, Pallas kernels, collect(): pl.pallas_call(lambda *refs: collect_kernel(part, *refs), out_shape=jax.S...  5.7 us
    ppermute x1, waiting for transfers between devices, sum_over_rows(): other = lax.ppermute(whole, ('prow', 'pcol'), pairs)  3.61 us
  transfers between devices with their start and end apart: 12, of which 8 were waited for; matrix products, arithmetic and copies ran while one was open for 1% of the time, Pallas kernels for 7%

profile of v7, /device:TPU:41, one launch (start us, length us, event | category | flops | bytes accessed | tf_op | source)
XLA Modules:
  0.0 156.0 jit_solution(11139015278374586442)
XLA Ops:
  0.0 1.0 slice_bitcast_fusion
  1.0 3.2 %collective-permute-start = (f32[1,4,8,2560]{3,2,1,0:T(8,128)S(1)}, f32[1,4,8,2560]{3,2,1,0:T(8,128)S(1)}, u32[]{:S(2)}, u32[]{:S(2)}) collective-permute-start(f32[1,4,8,2560]{3,2,1,0:T(8,128)S(1)} %slice_bitcast_fusion), channel_id=1, source_target_pairs={{0,12},{1,13},{2,14},{3,15},{4,8},{5,9},{6,10},{7,11},{8,4},{9,5},... | collective-permute-start | bytes 983048 | tf_op jit(solution)/shard_map/ppermute | solution.py:297
  4.3 0.0 slice-done
  4.3 0.7 maximum_bitcast_fusion
  5.0 3.5 %collective-permute-start.5 = (f32[1,4,8,2432]{3,2,1,0:T(8,128)S(1)}, f32[1,4,8,2432]{3,2,1,0:T(8,128)S(1)}, u32[]{:S(2)}, u32[]{:S(2)}) collective-permute-start(f32[1,4,8,2432]{3,2,1,0:T(8,128)S(1)} %maximum_bitcast_fusion), channel_id=1, source_target_pairs={{0,4},{1,5},{2,6},{3,7},{4,0},{5,1},{6,2},{7,3},{8,12},{9,13},{10,... | collective-permute-start | bytes 933896 | tf_op jit(solution)/shard_map/ppermute | solution.py:297
  8.5 0.6 collective-permute-done
  9.2 3.4 %collective-permute-start.1 = (f32[2,4,8,2560]{3,2,1,0:T(8,128)S(1)}, f32[2,4,8,2560]{3,2,1,0:T(8,128)S(1)}, u32[]{:S(2)}, u32[]{:S(2)}) collective-permute-start(f32[2,4,8,2560]{3,2,1,0:T(8,128)S(1)} %pad_maximum_fusion.2), channel_id=1, source_target_pairs={{0,4},{1,5},{2,6},{3,7},{4,0},{5,1},{6,2},{7,3},{8,12},{9,13},{10,... | collective-permute-start | bytes 1966088 | tf_op jit(solution)/shard_map/ppermute | solution.py:297
  12.6 0.5 collective-permute-done.5
  13.1 3.5 %collective-permute-start.6 = (f32[2,4,8,2432]{3,2,1,0:T(8,128)S(1)}, f32[2,4,8,2432]{3,2,1,0:T(8,128)S(1)}, u32[]{:S(2)}, u32[]{:S(2)}) collective-permute-start(f32[2,4,8,2432]{3,2,1,0:T(8,128)S(1)} %pad_maximum_fusion.3), channel_id=1, source_target_pairs={{0,12},{1,13},{2,14},{3,15},{4,8},{5,9},{6,10},{7,11},{8,4},{9,5},... | collective-permute-start | bytes 1867784 | tf_op jit(solution)/shard_map/ppermute | solution.py:297
  16.6 4.2 %collective-permute-done.1 = f32[2,4,8,2560]{3,2,1,0:T(8,128)S(1)} collective-permute-done((f32[2,4,8,2560]{3,2,1,0:T(8,128)S(1)}, f32[2,4,8,2560]{3,2,1,0:T(8,128)S(1)}, u32[]{:S(2)}, u32[]{:S(2)}) %collective-permute-start.1) | collective-permute-done | bytes 655392 | tf_op jit(solution)/shard_map/ppermute | solution.py:297
  20.8 0.1 pad_maximum_fusion.refs_1_.refs_4_
  20.9 0.0 copy-start.3
  20.9 0.0 copy-start.4
  21.0 4.4 %collective-permute-start.2 = (f32[4,4,8,2560]{3,2,1,0:T(8,128)S(1)}, f32[4,4,8,2560]{3,2,1,0:T(8,128)}, u32[]{:S(2)}, u32[]{:S(2)}) collective-permute-start(f32[4,4,8,2560]{3,2,1,0:T(8,128)S(1)} %pad_maximum_fusion.refs_1_.refs_4_), channel_id=1, source_target_pairs={{0,3},{1,2},{2,1},{3,0},{4,7},{5,6},{6,5},{7,4},{8,11},{9,10},{10,... | collective-permute-start | bytes 3932168 | tf_op jit(solution)/shard_map/ppermute | solution.py:297
  25.3 0.0 collective-permute-done.6
  25.4 0.1 pad_maximum_fusion.1.refs_1_.refs_0_
  25.5 2.2 %collective-permute-start.7 = (f32[4,4,8,2432]{3,2,1,0:T(8,128)S(1)}, f32[4,4,8,2432]{3,2,1,0:T(8,128)}, u32[]{:S(2)}, u32[]{:S(2)}) collective-permute-start(f32[4,4,8,2432]{3,2,1,0:T(8,128)S(1)} %pad_maximum_fusion.1.refs_1_.refs_0_), channel_id=1, source_target_pairs={{0,1},{1,0},{2,3},{3,2},{4,5},{5,4},{6,7},{7,6},{8,9},{9,8},{10,11... | collective-permute-start | bytes 3735560 | tf_op jit(solution)/shard_map/ppermute | solution.py:297
  27.7 3.1 %collective-permute-start.3 = (f32[4,4,8,2560]{3,2,1,0:T(8,128)S(1)}, f32[4,4,8,2560]{3,2,1,0:T(8,128)}, u32[]{:S(2)}, u32[]{:S(2)}) collective-permute-start(f32[4,4,8,2560]{3,2,1,0:T(8,128)S(1)} %pad_maximum_fusion.refs_1_.refs_4_), channel_id=1, source_target_pairs={{0,1},{1,0},{2,3},{3,2},{4,5},{5,4},{6,7},{7,6},{8,9},{9,8},{10,11... | collective-permute-start | bytes 3932168 | tf_op jit(solution)/shard_map/ppermute | solution.py:297
  30.8 3.5 %collective-permute-start.8 = (f32[4,4,8,2432]{3,2,1,0:T(8,128)S(1)}, f32[4,4,8,2432]{3,2,1,0:T(8,128)}, u32[]{:S(2)}, u32[]{:S(2)}) collective-permute-start(f32[4,4,8,2432]{3,2,1,0:T(8,128)S(1)} %pad_maximum_fusion.1.refs_1_.refs_0_), channel_id=1, source_target_pairs={{0,3},{1,2},{2,1},{3,0},{4,7},{5,6},{6,5},{7,4},{8,11},{9,10},{10,... | collective-permute-start | bytes 3735560 | tf_op jit(solution)/shard_map/ppermute | solution.py:297
  34.3 9.2 %collective-permute-done.7.refs_2_.refs_1_ = f32[4,4,8,2432]{3,2,1,0:T(8,128)} collective-permute-done((f32[4,4,8,2432]{3,2,1,0:T(8,128)S(1)}, f32[4,4,8,2432]{3,2,1,0:T(8,128)}, u32[]{:S(2)}, u32[]{:S(2)}) %collective-permute-start.7) | collective-permute-done | bytes 1245216 | tf_op jit(solution)/shard_map/ppermute | solution.py:297
  43.5 3.5 %collective-permute-start.9 = (f32[4,4,8,2432]{3,2,1,0:T(8,128)}, f32[4,4,8,2432]{3,2,1,0:T(8,128)}, u32[]{:S(2)}, u32[]{:S(2)}) collective-permute-start(f32[4,4,8,2432]{3,2,1,0:T(8,128)} %collective-permute-done.7.refs_2_.refs_1_), channel_id=1, source_target_pairs={{0,3},{1,2},{2,1},{3,0},{4,7},{5,6},{6,5},{7,4},{8,11},{9,10},{10,... | collective-permute-start | bytes 3735560 | tf_op jit(solution)/shard_map/ppermute | solution.py:297
  47.1 0.0 collective-permute-done.2.refs_2_.refs_5_
  47.1 1.9 %collective-permute-start.4 = (f32[4,4,8,2560]{3,2,1,0:T(8,128)}, f32[4,4,8,2560]{3,2,1,0:T(8,128)}, u32[]{:S(2)}, u32[]{:S(2)}) collective-permute-start(f32[4,4,8,2560]{3,2,1,0:T(8,128)} %collective-permute-done.2.refs_2_.refs_5_), channel_id=1, source_target_pairs={{0,1},{1,0},{2,3},{3,2},{4,5},{5,4},{6,7},{7,6},{8,9},{9,8},{10,11... | collective-permute-start | bytes 3932168 | tf_op jit(solution)/shard_map/ppermute | solution.py:297
  49.0 0.1 pad_add_fusion.refs_1_.info_ref
  49.1 0.0 copy-done.3
  49.1 0.0 copy-done.4
  49.1 7.0 %collective-permute-done.8.refs_3_.refs_2_ = f32[4,4,8,2432]{3,2,1,0:T(8,128)} collective-permute-done((f32[4,4,8,2432]{3,2,1,0:T(8,128)S(1)}, f32[4,4,8,2432]{3,2,1,0:T(8,128)}, u32[]{:S(2)}, u32[]{:S(2)}) %collective-permute-start.8) | collective-permute-done | bytes 1245216 | tf_op jit(solution)/shard_map/ppermute | solution.py:297
  56.1 2.8 %collect.3.refs_3_ = f32[16,4,8,2432]{3,2,1,0:T(8,128)S(1)} custom-call(s32[2,16]{1,0:T(2,128)S(1)} %select_xor_fusion.refs_0_.order_ref, f32[4,4,8,2432]{3,2,1,0:T(8,128)S(1)} %pad_maximum_fusion.1.refs_1_.refs_0_, f32[4,4,8,2432]{3,2,1,0:T(8,128)} %collective-permute-done.7.refs_2_.refs_1_, f32[4,4,8,2432]{3,2,1,0:T(8,128)} %collective-permute-done.8.refs_3_.refs_2_), custom_call_target="tpu_custom_call" | custom-call | bytes 9961472 | tf_op jit(solution)/shard_map/collect/pallas_call | solution.py:82
  58.9 0.0 copy-start.1
  58.9 1.0 copy-done.1
  60.0 0.0 collective-permute-done.3.refs_3_.refs_6_
  60.0 2.9 %collect.2.refs_3_ = f32[16,4,8,2560]{3,2,1,0:T(8,128)S(1)} custom-call(s32[2,16]{1,0:T(2,128)S(1)} %select_xor_fusion.refs_0_.order_ref, f32[4,4,8,2560]{3,2,1,0:T(8,128)S(1)} %pad_maximum_fusion.refs_1_.refs_4_, f32[4,4,8,2560]{3,2,1,0:T(8,128)} %collective-permute-done.2.refs_2_.refs_5_, f32[4,4,8,2560]{3,2,1,0:T(8,128)} %collective-permute-done.3.refs_3_.refs_6_), custom_call_target="tpu_custom_call" | custom-call | bytes 10485760 | tf_op jit(solution)/shard_map/collect/pallas_call | solution.py:82
  62.9 6.6 %collective-permute-done.9.refs_4_.refs_3_ = f32[4,4,8,2432]{3,2,1,0:T(8,128)} collective-permute-done((f32[4,4,8,2432]{3,2,1,0:T(8,128)}, f32[4,4,8,2432]{3,2,1,0:T(8,128)}, u32[]{:S(2)}, u32[]{:S(2)}) %collective-permute-start.9) | collective-permute-done | bytes 1245216 | tf_op jit(solution)/shard_map/ppermute | solution.py:297
  69.5 0.0 copy-done
  69.5 4.6 %inner_sums.2 = (f32[768,128]{1,0:T(8,128)S(1)}, f32[4,128,128]{2,1,0:T(8,128)S(1)}) custom-call(s32[2,16]{1,0:T(2,128)S(1)} %select_xor_fusion.refs_0_.order_ref, s32[2]{0:T(128)S(1)} %pad_add_fusion.refs_1_.info_ref, f32[96,4864]{1,0:T(8,128)S(1)} %copy-done, f32[16,4,8,2432]{3,2,1,0:T(8,128)S(1)} %collect.3.refs_3_, ...), custom_call_target="tpu_custom_call" | custom-call | flops 1358954496 | bytes 5603328 | tf_op jit(solution)/shard_map/inner_sums/pallas_call | solution.py:184
  74.1 0.0 collective-permute-done.4.refs_4_.refs_7_
  74.1 5.1 %inner_sums.3 = (f32[384,128]{1,0:T(8,128)S(1)}, f32[384,128]{1,0:T(8,128)S(1)}) custom-call(s32[2,16]{1,0:T(2,128)S(1)} %select_xor_fusion.refs_0_.order_ref, s32[2]{0:T(128)S(1)} %pad_add_fusion.refs_1_.info_ref, f32[96,4864]{1,0:T(8,128)S(1)} %copy-done, f32[16,4,8,2560]{3,2,1,0:T(8,128)S(1)} %collect.2.refs_3_, ...), custom_call_target="tpu_custom_call" | custom-call | flops 1509949440 | bytes 6225920 | tf_op jit(solution)/shard_map/inner_sums/pallas_call | solution.py:184
  79.2 6.3 %collective-permute-start.10 = (f32[384,128]{1,0:T(8,128)S(1)}, f32[384,128]{1,0:T(8,128)S(1)}, u32[]{:S(2)}, u32[]{:S(2)}) collective-permute-start(f32[384,128]{1,0:T(8,128)S(1)} %get-tuple-element.17), channel_id=1, source_target_pairs={{0,16},{16,0},{32,48},{48,32},{64,80},{80,64},{96,112},{112,96},{1... | collective-permute-start | bytes 589832 | tf_op jit(solution)/shard_map/ppermute | solution.py:313
  85.6 1.0 collective-permute-done.10
  86.6 30.6 %all_to_all.10 = f32[16,24,128]{2,1,0:T(8,128)} all-to-all(f32[16,24,128]{2,1,0:T(8,128)S(1)} %bitcast.10), channel_id=1, replica_groups={{0,32,64,96,128,160,192,224,256,288,320,352,384,416,448,480},{16,48,80,..., dimensions={0} | all-to-all | bytes 393216 | tf_op jit(solution)/shard_map/all_to_all | solution.py:309
  117.3 0.9 reduce_sum.9
  118.2 0.0 copy-start.2
  118.3 21.1 %all_to_all.11 = f32[16,24,128]{2,1,0:T(8,128)S(1)} all-to-all(f32[16,24,128]{2,1,0:T(8,128)S(1)} %broadcast_in_dim.11), channel_id=1, replica_groups={{0,32,64,96,128,160,192,224,256,288,320,352,384,416,448,480},{16,48,80,..., dimensions={0} | all-to-all | bytes 393216 | tf_op jit(solution)/shard_map/all_to_all | solution.py:309
  139.3 1.9 %collective-permute-start.11 = (f32[384,128]{1,0:T(8,128)S(1)}, f32[384,128]{1,0:T(8,128)S(1)}, u32[]{:S(2)}, u32[]{:S(2)}) collective-permute-start(f32[384,128]{1,0:T(8,128)S(1)} %bitcast.8), channel_id=1, source_target_pairs={{16,28},{17,29},{18,30},{19,31},{20,24},{21,25},{22,26},{23,27},{2... | collective-permute-start | bytes 589832 | tf_op jit(solution)/shard_map/ppermute | solution.py:321
  141.3 2.1 %all_gather.6.sum_ref = f32[768,128]{1,0:T(8,128)S(1)} all-gather(f32[384,128]{1,0:T(8,128)S(1)} %bitcast.9), channel_id=1, replica_groups={{0,16},{32,48},{64,80},{96,112},{128,144},{160,176},{192,208},{224,240}..., dimensions={0}, use_global_device_ids=true | all-gather | bytes 589824 | tf_op jit(solution)/shard_map/all_gather | solution.py:322
  143.3 3.6 %collective-permute-done.11 = f32[384,128]{1,0:T(8,128)S(1)} collective-permute-done((f32[384,128]{1,0:T(8,128)S(1)}, f32[384,128]{1,0:T(8,128)S(1)}, u32[]{:S(2)}, u32[]{:S(2)}) %collective-permute-start.11) | collective-permute-done | bytes 196640 | tf_op jit(solution)/shard_map/ppermute | solution.py:321
  147.0 2.3 %all_gather.7 = f32[768,128]{1,0:T(8,128)S(1)} all-gather(f32[384,128]{1,0:T(8,128)S(1)} %collective-permute-done.11), channel_id=1, replica_groups={{0,16},{32,48},{64,80},{96,112},{128,144},{160,176},{192,208},{224,240}..., dimensions={0}, use_global_device_ids=true | all-gather | bytes 589824 | tf_op jit(solution)/shard_map/all_gather | solution.py:324
  149.2 6.6 %update.1 = f32[96,4864]{1,0:T(8,128)} custom-call(s32[2,16]{1,0:T(2,128)S(1)} %select_xor_fusion.refs_0_.order_ref, s32[2]{0:T(128)S(1)} %pad_add_fusion.refs_1_.info_ref, f32[768,128]{1,0:T(8,128)S(1)} %all_gather.6.sum_ref, f32[384,128]{1,0:T(8,128)S(1)} %slice.12.rest_ref, f32[4,128,128]{2,1,0:T(8,128)S(1)} %get-tuple-element.20.fac_ref, ...), custom_call_target="tpu_custom_call" | custom-call | flops 1434451968 | bytes 13697024 | tf_op jit(solution)/shard_map/update/pallas_call | solution.py:261
  (9 shorter events, 0.1 us)
Async XLA Ops:
  0.0 4.3 %slice-start = ((f32[4,8,4864]{2,1,0:T(8,128)}), f32[4,8,2304]{2,1,0:T(8,128)S(1)}, s32[]{:S(2)}) async-start(f32[4,8,4864]{2,1,0:T(8,128)} %param.6), calls=%async_computation.2 | async-start | bytes 589824 | tf_op jit(solution)/shard_map/slice | solution.py:336
  1.0 8.1 %collective-permute-start = (f32[1,4,8,2560]{3,2,1,0:T(8,128)S(1)}, f32[1,4,8,2560]{3,2,1,0:T(8,128)S(1)}, u32[]{:S(2)}, u32[]{:S(2)}) collective-permute-start(f32[1,4,8,2560]{3,2,1,0:T(8,128)S(1)} %slice_bitcast_fusion), channel_id=1, source_target_pairs={{0,12},{1,13},{2,14},{3,15},{4,8},{5,9},{6,10},{7,11},{8,4},{9,5},... | collective-permute-start | bytes 983048 | tf_op jit(solution)/shard_map/ppermute | solution.py:297
  5.0 8.1 %collective-permute-start.5 = (f32[1,4,8,2432]{3,2,1,0:T(8,128)S(1)}, f32[1,4,8,2432]{3,2,1,0:T(8,128)S(1)}, u32[]{:S(2)}, u32[]{:S(2)}) collective-permute-start(f32[1,4,8,2432]{3,2,1,0:T(8,128)S(1)} %maximum_bitcast_fusion), channel_id=1, source_target_pairs={{0,4},{1,5},{2,6},{3,7},{4,0},{5,1},{6,2},{7,3},{8,12},{9,13},{10,... | collective-permute-start | bytes 933896 | tf_op jit(solution)/shard_map/ppermute | solution.py:297
  9.2 11.6 %collective-permute-start.1 = (f32[2,4,8,2560]{3,2,1,0:T(8,128)S(1)}, f32[2,4,8,2560]{3,2,1,0:T(8,128)S(1)}, u32[]{:S(2)}, u32[]{:S(2)}) collective-permute-start(f32[2,4,8,2560]{3,2,1,0:T(8,128)S(1)} %pad_maximum_fusion.2), channel_id=1, source_target_pairs={{0,4},{1,5},{2,6},{3,7},{4,0},{5,1},{6,2},{7,3},{8,12},{9,13},{10,... | collective-permute-start | bytes 1966088 | tf_op jit(solution)/shard_map/ppermute | solution.py:297
  13.1 12.2 %collective-permute-start.6 = (f32[2,4,8,2432]{3,2,1,0:T(8,128)S(1)}, f32[2,4,8,2432]{3,2,1,0:T(8,128)S(1)}, u32[]{:S(2)}, u32[]{:S(2)}) collective-permute-start(f32[2,4,8,2432]{3,2,1,0:T(8,128)S(1)} %pad_maximum_fusion.3), channel_id=1, source_target_pairs={{0,12},{1,13},{2,14},{3,15},{4,8},{5,9},{6,10},{7,11},{8,4},{9,5},... | collective-permute-start | bytes 1867784 | tf_op jit(solution)/shard_map/ppermute | solution.py:297
  20.9 28.2 %copy-start.3 = (s32[2,16]{1,0:T(2,128)S(1)}, s32[2,16]{1,0:T(2,128)}, u32[]{:S(2)}) copy-start(s32[2,16]{1,0:T(2,128)} %constant.24.clone) | copy-start | bytes 388
  20.9 28.1 %copy-start.4 = (s32[2,16]{1,0:T(2,128)S(1)}, s32[2,16]{1,0:T(2,128)}, u32[]{:S(2)}) copy-start(s32[2,16]{1,0:T(2,128)} %constant.25.clone) | copy-start | bytes 388
  21.0 26.1 %collective-permute-start.2 = (f32[4,4,8,2560]{3,2,1,0:T(8,128)S(1)}, f32[4,4,8,2560]{3,2,1,0:T(8,128)}, u32[]{:S(2)}, u32[]{:S(2)}) collective-permute-start(f32[4,4,8,2560]{3,2,1,0:T(8,128)S(1)} %pad_maximum_fusion.refs_1_.refs_4_), channel_id=1, source_target_pairs={{0,3},{1,2},{2,1},{3,0},{4,7},{5,6},{6,5},{7,4},{8,11},{9,10},{10,... | collective-permute-start | bytes 3932168 | tf_op jit(solution)/shard_map/ppermute | solution.py:297
  25.5 18.1 %collective-permute-start.7 = (f32[4,4,8,2432]{3,2,1,0:T(8,128)S(1)}, f32[4,4,8,2432]{3,2,1,0:T(8,128)}, u32[]{:S(2)}, u32[]{:S(2)}) collective-permute-start(f32[4,4,8,2432]{3,2,1,0:T(8,128)S(1)} %pad_maximum_fusion.1.refs_1_.refs_0_), channel_id=1, source_target_pairs={{0,1},{1,0},{2,3},{3,2},{4,5},{5,4},{6,7},{7,6},{8,9},{9,8},{10,11... | collective-permute-start | bytes 3735560 | tf_op jit(solution)/shard_map/ppermute | solution.py:297
  27.7 32.3 %collective-permute-start.3 = (f32[4,4,8,2560]{3,2,1,0:T(8,128)S(1)}, f32[4,4,8,2560]{3,2,1,0:T(8,128)}, u32[]{:S(2)}, u32[]{:S(2)}) collective-permute-start(f32[4,4,8,2560]{3,2,1,0:T(8,128)S(1)} %pad_maximum_fusion.refs_1_.refs_4_), channel_id=1, source_target_pairs={{0,1},{1,0},{2,3},{3,2},{4,5},{5,4},{6,7},{7,6},{8,9},{9,8},{10,11... | collective-permute-start | bytes 3932168 | tf_op jit(solution)/shard_map/ppermute | solution.py:297
  30.8 25.4 %collective-permute-start.8 = (f32[4,4,8,2432]{3,2,1,0:T(8,128)S(1)}, f32[4,4,8,2432]{3,2,1,0:T(8,128)}, u32[]{:S(2)}, u32[]{:S(2)}) collective-permute-start(f32[4,4,8,2432]{3,2,1,0:T(8,128)S(1)} %pad_maximum_fusion.1.refs_1_.refs_0_), channel_id=1, source_target_pairs={{0,3},{1,2},{2,1},{3,0},{4,7},{5,6},{6,5},{7,4},{8,11},{9,10},{10,... | collective-permute-start | bytes 3735560 | tf_op jit(solution)/shard_map/ppermute | solution.py:297
  43.5 26.0 %collective-permute-start.9 = (f32[4,4,8,2432]{3,2,1,0:T(8,128)}, f32[4,4,8,2432]{3,2,1,0:T(8,128)}, u32[]{:S(2)}, u32[]{:S(2)}) collective-permute-start(f32[4,4,8,2432]{3,2,1,0:T(8,128)} %collective-permute-done.7.refs_2_.refs_1_), channel_id=1, source_target_pairs={{0,3},{1,2},{2,1},{3,0},{4,7},{5,6},{6,5},{7,4},{8,11},{9,10},{10,... | collective-permute-start | bytes 3735560 | tf_op jit(solution)/shard_map/ppermute | solution.py:297
  47.1 27.0 %collective-permute-start.4 = (f32[4,4,8,2560]{3,2,1,0:T(8,128)}, f32[4,4,8,2560]{3,2,1,0:T(8,128)}, u32[]{:S(2)}, u32[]{:S(2)}) collective-permute-start(f32[4,4,8,2560]{3,2,1,0:T(8,128)} %collective-permute-done.2.refs_2_.refs_5_), channel_id=1, source_target_pairs={{0,1},{1,0},{2,3},{3,2},{4,5},{5,4},{6,7},{7,6},{8,9},{9,8},{10,11... | collective-permute-start | bytes 3932168 | tf_op jit(solution)/shard_map/ppermute | solution.py:297
  58.9 1.0 copy-start.1
  60.0 9.5 %copy-start = (f32[96,4864]{1,0:T(8,128)S(1)}, f32[96,4864]{1,0:T(8,128)}, u32[]{:S(2)}) copy-start(f32[96,4864]{1,0:T(8,128)} %eig_ref.1) | copy-start | bytes 5603332
  79.2 7.4 %collective-permute-start.10 = (f32[384,128]{1,0:T(8,128)S(1)}, f32[384,128]{1,0:T(8,128)S(1)}, u32[]{:S(2)}, u32[]{:S(2)}) collective-permute-start(f32[384,128]{1,0:T(8,128)S(1)} %get-tuple-element.17), channel_id=1, source_target_pairs={{0,16},{16,0},{32,48},{48,32},{64,80},{80,64},{96,112},{112,96},{1... | collective-permute-start | bytes 589832 | tf_op jit(solution)/shard_map/ppermute | solution.py:313
  118.2 31.0 %copy-start.2 = (f32[4,4,8,2432]{3,2,1,0:T(8,128)S(1)}, f32[4,4,8,2432]{3,2,1,0:T(8,128)}, u32[]{:S(2)}) copy-start(f32[4,4,8,2432]{3,2,1,0:T(8,128)} %copy-done.1) | copy-start | bytes 3735556
  139.3 7.6 %collective-permute-start.11 = (f32[384,128]{1,0:T(8,128)S(1)}, f32[384,128]{1,0:T(8,128)S(1)}, u32[]{:S(2)}, u32[]{:S(2)}) collective-permute-start(f32[384,128]{1,0:T(8,128)S(1)} %bitcast.8), channel_id=1, source_target_pairs={{16,28},{17,29},{18,30},{19,31},{20,24},{21,25},{22,26},{23,27},{2... | collective-permute-start | bytes 589832 | tf_op jit(solution)/shard_map/ppermute | solution.py:321

commit v8 on v7

--- a/solution.py
+++ b/solution.py
@@ -106,8 +106,10 @@
     kb = owners * share
     start = 0 if first else cols - data
 
-    vecs[...] = early_ref[...]
     count = late_ref.shape[0]
+    for i in range(owners - count):
+        owner = order_ref[part, i]
+        vecs[owner] = early_ref[owner]
     for i in range(count):
         vecs[order_ref[part, owners - count + i]] = late_ref[i]
 

time: 157 us -> 157 us (level)
  no operation moved by 1% of the time
where the time goes in v8:
time: 157 us; the launch traced here: 156 us
  blocking collectives  56.1 us (36%)
  starting transfers between devices  40.5 us (26%)
  waiting for transfers between devices  32.9 us (21%)
  Pallas kernels  21.9 us (14%)
  local copies, waits for them, and re-layouts  2.12 us (1%)
  other arithmetic  2.07 us (1%)
    all_to_all x2, blocking collectives, along_z(): return lax.all_to_all(x, 'prow', 0, 0, axis_index_groups=groups)  51.7 us
    ppermute x10, starting transfers between devices, send(): return lax.ppermute(x, ('prow', 'pcol'), pairs)  32.2 us
    ppermute x10, waiting for transfers between devices, send(): return lax.ppermute(x, ('prow', 'pcol'), pairs)  28.2 us
    pallas_call x2, Pallas kernels, inner_sums(): pl.pallas_call(lambda *refs: inner_kernel(part, data, *refs), out_shape=o...  9.58 us
    pallas_call x1, Pallas kernels, update(): pl.pallas_call(update_kernel, out_shape=jax.ShapeDtypeStruct(eig.shape, F...  6.64 us
    ppermute x1, starting transfers between devices, sum_over_rows(): mine = keep + lax.ppermute(give, 'prow', [(i, i ^ 1) for i in range(nprow)])  6.39 us
    pallas_call x2, Pallas kernels, collect(): pl.pallas_call(lambda *refs: collect_kernel(part, *refs), out_shape=jax.S...  5.7 us
    ppermute x1, waiting for transfers between devices, sum_over_rows(): other = lax.ppermute(whole, ('prow', 'pcol'), pairs)  3.61 us
  transfers between devices with their start and end apart: 12, of which 8 were waited for; matrix products, arithmetic and copies ran while one was open for 1% of the time, Pallas kernels for 7%

profile of v8, /device:TPU:41, one launch (start us, length us, event | category | flops | bytes accessed | tf_op | source)
XLA Modules:
  0.0 156.0 jit_solution(2185695614332367866)
XLA Ops:
  0.0 1.0 slice_bitcast_fusion
  1.0 3.2 %collective-permute-start = (f32[1,4,8,2560]{3,2,1,0:T(8,128)S(1)}, f32[1,4,8,2560]{3,2,1,0:T(8,128)S(1)}, u32[]{:S(2)}, u32[]{:S(2)}) collective-permute-start(f32[1,4,8,2560]{3,2,1,0:T(8,128)S(1)} %slice_bitcast_fusion), channel_id=1, source_target_pairs={{0,12},{1,13},{2,14},{3,15},{4,8},{5,9},{6,10},{7,11},{8,4},{9,5},... | collective-permute-start | bytes 983048 | tf_op jit(solution)/shard_map/ppermute | solution.py:299
  4.3 0.0 slice-done
  4.3 0.7 maximum_bitcast_fusion
  5.0 3.5 %collective-permute-start.5 = (f32[1,4,8,2432]{3,2,1,0:T(8,128)S(1)}, f32[1,4,8,2432]{3,2,1,0:T(8,128)S(1)}, u32[]{:S(2)}, u32[]{:S(2)}) collective-permute-start(f32[1,4,8,2432]{3,2,1,0:T(8,128)S(1)} %maximum_bitcast_fusion), channel_id=1, source_target_pairs={{0,4},{1,5},{2,6},{3,7},{4,0},{5,1},{6,2},{7,3},{8,12},{9,13},{10,... | collective-permute-start | bytes 933896 | tf_op jit(solution)/shard_map/ppermute | solution.py:299
  8.5 0.6 collective-permute-done
  9.2 3.4 %collective-permute-start.1 = (f32[2,4,8,2560]{3,2,1,0:T(8,128)S(1)}, f32[2,4,8,2560]{3,2,1,0:T(8,128)S(1)}, u32[]{:S(2)}, u32[]{:S(2)}) collective-permute-start(f32[2,4,8,2560]{3,2,1,0:T(8,128)S(1)} %pad_maximum_fusion.2), channel_id=1, source_target_pairs={{0,4},{1,5},{2,6},{3,7},{4,0},{5,1},{6,2},{7,3},{8,12},{9,13},{10,... | collective-permute-start | bytes 1966088 | tf_op jit(solution)/shard_map/ppermute | solution.py:299
  12.6 0.5 collective-permute-done.5
  13.1 3.5 %collective-permute-start.6 = (f32[2,4,8,2432]{3,2,1,0:T(8,128)S(1)}, f32[2,4,8,2432]{3,2,1,0:T(8,128)S(1)}, u32[]{:S(2)}, u32[]{:S(2)}) collective-permute-start(f32[2,4,8,2432]{3,2,1,0:T(8,128)S(1)} %pad_maximum_fusion.3), channel_id=1, source_target_pairs={{0,12},{1,13},{2,14},{3,15},{4,8},{5,9},{6,10},{7,11},{8,4},{9,5},... | collective-permute-start | bytes 1867784 | tf_op jit(solution)/shard_map/ppermute | solution.py:299
  16.6 4.2 %collective-permute-done.1 = f32[2,4,8,2560]{3,2,1,0:T(8,128)S(1)} collective-permute-done((f32[2,4,8,2560]{3,2,1,0:T(8,128)S(1)}, f32[2,4,8,2560]{3,2,1,0:T(8,128)S(1)}, u32[]{:S(2)}, u32[]{:S(2)}) %collective-permute-start.1) | collective-permute-done | bytes 655392 | tf_op jit(solution)/shard_map/ppermute | solution.py:299
  20.8 0.1 pad_maximum_fusion.refs_1_.refs_4_
  20.9 0.0 copy-start.3
  20.9 0.0 copy-start.4
  21.0 4.4 %collective-permute-start.2 = (f32[4,4,8,2560]{3,2,1,0:T(8,128)S(1)}, f32[4,4,8,2560]{3,2,1,0:T(8,128)}, u32[]{:S(2)}, u32[]{:S(2)}) collective-permute-start(f32[4,4,8,2560]{3,2,1,0:T(8,128)S(1)} %pad_maximum_fusion.refs_1_.refs_4_), channel_id=1, source_target_pairs={{0,3},{1,2},{2,1},{3,0},{4,7},{5,6},{6,5},{7,4},{8,11},{9,10},{10,... | collective-permute-start | bytes 3932168 | tf_op jit(solution)/shard_map/ppermute | solution.py:299
  25.3 0.0 collective-permute-done.6
  25.4 0.1 pad_maximum_fusion.1.refs_1_.refs_0_
  25.5 2.2 %collective-permute-start.7 = (f32[4,4,8,2432]{3,2,1,0:T(8,128)S(1)}, f32[4,4,8,2432]{3,2,1,0:T(8,128)}, u32[]{:S(2)}, u32[]{:S(2)}) collective-permute-start(f32[4,4,8,2432]{3,2,1,0:T(8,128)S(1)} %pad_maximum_fusion.1.refs_1_.refs_0_), channel_id=1, source_target_pairs={{0,1},{1,0},{2,3},{3,2},{4,5},{5,4},{6,7},{7,6},{8,9},{9,8},{10,11... | collective-permute-start | bytes 3735560 | tf_op jit(solution)/shard_map/ppermute | solution.py:299
  27.7 3.1 %collective-permute-start.3 = (f32[4,4,8,2560]{3,2,1,0:T(8,128)S(1)}, f32[4,4,8,2560]{3,2,1,0:T(8,128)}, u32[]{:S(2)}, u32[]{:S(2)}) collective-permute-start(f32[4,4,8,2560]{3,2,1,0:T(8,128)S(1)} %pad_maximum_fusion.refs_1_.refs_4_), channel_id=1, source_target_pairs={{0,1},{1,0},{2,3},{3,2},{4,5},{5,4},{6,7},{7,6},{8,9},{9,8},{10,11... | collective-permute-start | bytes 3932168 | tf_op jit(solution)/shard_map/ppermute | solution.py:299
  30.8 3.5 %collective-permute-start.8 = (f32[4,4,8,2432]{3,2,1,0:T(8,128)S(1)}, f32[4,4,8,2432]{3,2,1,0:T(8,128)}, u32[]{:S(2)}, u32[]{:S(2)}) collective-permute-start(f32[4,4,8,2432]{3,2,1,0:T(8,128)S(1)} %pad_maximum_fusion.1.refs_1_.refs_0_), channel_id=1, source_target_pairs={{0,3},{1,2},{2,1},{3,0},{4,7},{5,6},{6,5},{7,4},{8,11},{9,10},{10,... | collective-permute-start | bytes 3735560 | tf_op jit(solution)/shard_map/ppermute | solution.py:299
  34.3 9.2 %collective-permute-done.7.refs_2_.refs_1_ = f32[4,4,8,2432]{3,2,1,0:T(8,128)} collective-permute-done((f32[4,4,8,2432]{3,2,1,0:T(8,128)S(1)}, f32[4,4,8,2432]{3,2,1,0:T(8,128)}, u32[]{:S(2)}, u32[]{:S(2)}) %collective-permute-start.7) | collective-permute-done | bytes 1245216 | tf_op jit(solution)/shard_map/ppermute | solution.py:299
  43.5 3.5 %collective-permute-start.9 = (f32[4,4,8,2432]{3,2,1,0:T(8,128)}, f32[4,4,8,2432]{3,2,1,0:T(8,128)}, u32[]{:S(2)}, u32[]{:S(2)}) collective-permute-start(f32[4,4,8,2432]{3,2,1,0:T(8,128)} %collective-permute-done.7.refs_2_.refs_1_), channel_id=1, source_target_pairs={{0,3},{1,2},{2,1},{3,0},{4,7},{5,6},{6,5},{7,4},{8,11},{9,10},{10,... | collective-permute-start | bytes 3735560 | tf_op jit(solution)/shard_map/ppermute | solution.py:299
  47.1 0.0 collective-permute-done.2.refs_2_.refs_5_
  47.1 1.9 %collective-permute-start.4 = (f32[4,4,8,2560]{3,2,1,0:T(8,128)}, f32[4,4,8,2560]{3,2,1,0:T(8,128)}, u32[]{:S(2)}, u32[]{:S(2)}) collective-permute-start(f32[4,4,8,2560]{3,2,1,0:T(8,128)} %collective-permute-done.2.refs_2_.refs_5_), channel_id=1, source_target_pairs={{0,1},{1,0},{2,3},{3,2},{4,5},{5,4},{6,7},{7,6},{8,9},{9,8},{10,11... | collective-permute-start | bytes 3932168 | tf_op jit(solution)/shard_map/ppermute | solution.py:299
  49.0 0.1 pad_add_fusion.refs_1_.info_ref
  49.1 0.0 copy-done.3
  49.1 0.0 copy-done.4
  49.1 7.0 %collective-permute-done.8.refs_3_.refs_2_ = f32[4,4,8,2432]{3,2,1,0:T(8,128)} collective-permute-done((f32[4,4,8,2432]{3,2,1,0:T(8,128)S(1)}, f32[4,4,8,2432]{3,2,1,0:T(8,128)}, u32[]{:S(2)}, u32[]{:S(2)}) %collective-permute-start.8) | collective-permute-done | bytes 1245216 | tf_op jit(solution)/shard_map/ppermute | solution.py:299
  56.1 2.8 %collect.3.refs_3_ = f32[16,4,8,2432]{3,2,1,0:T(8,128)S(1)} custom-call(s32[2,16]{1,0:T(2,128)S(1)} %select_xor_fusion.refs_0_.order_ref, f32[4,4,8,2432]{3,2,1,0:T(8,128)S(1)} %pad_maximum_fusion.1.refs_1_.refs_0_, f32[4,4,8,2432]{3,2,1,0:T(8,128)} %collective-permute-done.7.refs_2_.refs_1_, f32[4,4,8,2432]{3,2,1,0:T(8,128)} %collective-permute-done.8.refs_3_.refs_2_), custom_call_target="tpu_custom_call" | custom-call | bytes 9961472 | tf_op jit(solution)/shard_map/collect/pallas_call | solution.py:82
  58.9 0.0 copy-start.1
  58.9 1.0 copy-done.1
  60.0 0.0 collective-permute-done.3.refs_3_.refs_6_
  60.0 2.9 %collect.2.refs_3_ = f32[16,4,8,2560]{3,2,1,0:T(8,128)S(1)} custom-call(s32[2,16]{1,0:T(2,128)S(1)} %select_xor_fusion.refs_0_.order_ref, f32[4,4,8,2560]{3,2,1,0:T(8,128)S(1)} %pad_maximum_fusion.refs_1_.refs_4_, f32[4,4,8,2560]{3,2,1,0:T(8,128)} %collective-permute-done.2.refs_2_.refs_5_, f32[4,4,8,2560]{3,2,1,0:T(8,128)} %collective-permute-done.3.refs_3_.refs_6_), custom_call_target="tpu_custom_call" | custom-call | bytes 10485760 | tf_op jit(solution)/shard_map/collect/pallas_call | solution.py:82
  62.9 6.6 %collective-permute-done.9.refs_4_.refs_3_ = f32[4,4,8,2432]{3,2,1,0:T(8,128)} collective-permute-done((f32[4,4,8,2432]{3,2,1,0:T(8,128)}, f32[4,4,8,2432]{3,2,1,0:T(8,128)}, u32[]{:S(2)}, u32[]{:S(2)}) %collective-permute-start.9) | collective-permute-done | bytes 1245216 | tf_op jit(solution)/shard_map/ppermute | solution.py:299
  69.5 0.0 copy-done
  69.5 4.5 %inner_sums.2 = (f32[768,128]{1,0:T(8,128)S(1)}, f32[4,128,128]{2,1,0:T(8,128)S(1)}) custom-call(s32[2,16]{1,0:T(2,128)S(1)} %select_xor_fusion.refs_0_.order_ref, s32[2]{0:T(128)S(1)} %pad_add_fusion.refs_1_.info_ref, f32[96,4864]{1,0:T(8,128)S(1)} %copy-done, f32[16,4,8,2432]{3,2,1,0:T(8,128)S(1)} %collect.3.refs_3_, ...), custom_call_target="tpu_custom_call" | custom-call | flops 1358954496 | bytes 5603328 | tf_op jit(solution)/shard_map/inner_sums/pallas_call | solution.py:186
  74.0 0.0 collective-permute-done.4.refs_4_.refs_7_
  74.0 5.0 %inner_sums.3 = (f32[384,128]{1,0:T(8,128)S(1)}, f32[384,128]{1,0:T(8,128)S(1)}) custom-call(s32[2,16]{1,0:T(2,128)S(1)} %select_xor_fusion.refs_0_.order_ref, s32[2]{0:T(128)S(1)} %pad_add_fusion.refs_1_.info_ref, f32[96,4864]{1,0:T(8,128)S(1)} %copy-done, f32[16,4,8,2560]{3,2,1,0:T(8,128)S(1)} %collect.2.refs_3_, ...), custom_call_target="tpu_custom_call" | custom-call | flops 1509949440 | bytes 6225920 | tf_op jit(solution)/shard_map/inner_sums/pallas_call | solution.py:186
  79.1 6.4 %collective-permute-start.10 = (f32[384,128]{1,0:T(8,128)S(1)}, f32[384,128]{1,0:T(8,128)S(1)}, u32[]{:S(2)}, u32[]{:S(2)}) collective-permute-start(f32[384,128]{1,0:T(8,128)S(1)} %get-tuple-element.17), channel_id=1, source_target_pairs={{0,16},{16,0},{32,48},{48,32},{64,80},{80,64},{96,112},{112,96},{1... | collective-permute-start | bytes 589832 | tf_op jit(solution)/shard_map/ppermute | solution.py:315
  85.5 1.0 collective-permute-done.10
  86.6 30.6 %all_to_all.10 = f32[16,24,128]{2,1,0:T(8,128)} all-to-all(f32[16,24,128]{2,1,0:T(8,128)S(1)} %bitcast.10), channel_id=1, replica_groups={{0,32,64,96,128,160,192,224,256,288,320,352,384,416,448,480},{16,48,80,..., dimensions={0} | all-to-all | bytes 393216 | tf_op jit(solution)/shard_map/all_to_all | solution.py:311
  117.2 0.9 reduce_sum.9
  118.1 0.0 copy-start.2
  118.2 21.1 %all_to_all.11 = f32[16,24,128]{2,1,0:T(8,128)S(1)} all-to-all(f32[16,24,128]{2,1,0:T(8,128)S(1)} %broadcast_in_dim.11), channel_id=1, replica_groups={{0,32,64,96,128,160,192,224,256,288,320,352,384,416,448,480},{16,48,80,..., dimensions={0} | all-to-all | bytes 393216 | tf_op jit(solution)/shard_map/all_to_all | solution.py:311
  139.3 1.9 %collective-permute-start.11 = (f32[384,128]{1,0:T(8,128)S(1)}, f32[384,128]{1,0:T(8,128)S(1)}, u32[]{:S(2)}, u32[]{:S(2)}) collective-permute-start(f32[384,128]{1,0:T(8,128)S(1)} %bitcast.8), channel_id=1, source_target_pairs={{16,28},{17,29},{18,30},{19,31},{20,24},{21,25},{22,26},{23,27},{2... | collective-permute-start | bytes 589832 | tf_op jit(solution)/shard_map/ppermute | solution.py:323
  141.2 2.1 %all_gather.6.sum_ref = f32[768,128]{1,0:T(8,128)S(1)} all-gather(f32[384,128]{1,0:T(8,128)S(1)} %bitcast.9), channel_id=1, replica_groups={{0,16},{32,48},{64,80},{96,112},{128,144},{160,176},{192,208},{224,240}..., dimensions={0}, use_global_device_ids=true | all-gather | bytes 589824 | tf_op jit(solution)/shard_map/all_gather | solution.py:324
  143.3 3.6 %collective-permute-done.11 = f32[384,128]{1,0:T(8,128)S(1)} collective-permute-done((f32[384,128]{1,0:T(8,128)S(1)}, f32[384,128]{1,0:T(8,128)S(1)}, u32[]{:S(2)}, u32[]{:S(2)}) %collective-permute-start.11) | collective-permute-done | bytes 196640 | tf_op jit(solution)/shard_map/ppermute | solution.py:323
  146.9 2.3 %all_gather.7 = f32[768,128]{1,0:T(8,128)S(1)} all-gather(f32[384,128]{1,0:T(8,128)S(1)} %collective-permute-done.11), channel_id=1, replica_groups={{0,16},{32,48},{64,80},{96,112},{128,144},{160,176},{192,208},{224,240}..., dimensions={0}, use_global_device_ids=true | all-gather | bytes 589824 | tf_op jit(solution)/shard_map/all_gather | solution.py:326
  149.2 6.6 %update.1 = f32[96,4864]{1,0:T(8,128)} custom-call(s32[2,16]{1,0:T(2,128)S(1)} %select_xor_fusion.refs_0_.order_ref, s32[2]{0:T(128)S(1)} %pad_add_fusion.refs_1_.info_ref, f32[768,128]{1,0:T(8,128)S(1)} %all_gather.6.sum_ref, f32[384,128]{1,0:T(8,128)S(1)} %slice.12.rest_ref, f32[4,128,128]{2,1,0:T(8,128)S(1)} %get-tuple-element.20.fac_ref, ...), custom_call_target="tpu_custom_call" | custom-call | flops 1434451968 | bytes 13697024 | tf_op jit(solution)/shard_map/update/pallas_call | solution.py:263
  (9 shorter events, 0.1 us)
Async XLA Ops:
  0.0 4.3 %slice-start = ((f32[4,8,4864]{2,1,0:T(8,128)}), f32[4,8,2304]{2,1,0:T(8,128)S(1)}, s32[]{:S(2)}) async-start(f32[4,8,4864]{2,1,0:T(8,128)} %param.6), calls=%async_computation.2 | async-start | bytes 589824 | tf_op jit(solution)/shard_map/slice | solution.py:338
  1.0 8.1 %collective-permute-start = (f32[1,4,8,2560]{3,2,1,0:T(8,128)S(1)}, f32[1,4,8,2560]{3,2,1,0:T(8,128)S(1)}, u32[]{:S(2)}, u32[]{:S(2)}) collective-permute-start(f32[1,4,8,2560]{3,2,1,0:T(8,128)S(1)} %slice_bitcast_fusion), channel_id=1, source_target_pairs={{0,12},{1,13},{2,14},{3,15},{4,8},{5,9},{6,10},{7,11},{8,4},{9,5},... | collective-permute-start | bytes 983048 | tf_op jit(solution)/shard_map/ppermute | solution.py:299
  5.0 8.1 %collective-permute-start.5 = (f32[1,4,8,2432]{3,2,1,0:T(8,128)S(1)}, f32[1,4,8,2432]{3,2,1,0:T(8,128)S(1)}, u32[]{:S(2)}, u32[]{:S(2)}) collective-permute-start(f32[1,4,8,2432]{3,2,1,0:T(8,128)S(1)} %maximum_bitcast_fusion), channel_id=1, source_target_pairs={{0,4},{1,5},{2,6},{3,7},{4,0},{5,1},{6,2},{7,3},{8,12},{9,13},{10,... | collective-permute-start | bytes 933896 | tf_op jit(solution)/shard_map/ppermute | solution.py:299
  9.2 11.6 %collective-permute-start.1 = (f32[2,4,8,2560]{3,2,1,0:T(8,128)S(1)}, f32[2,4,8,2560]{3,2,1,0:T(8,128)S(1)}, u32[]{:S(2)}, u32[]{:S(2)}) collective-permute-start(f32[2,4,8,2560]{3,2,1,0:T(8,128)S(1)} %pad_maximum_fusion.2), channel_id=1, source_target_pairs={{0,4},{1,5},{2,6},{3,7},{4,0},{5,1},{6,2},{7,3},{8,12},{9,13},{10,... | collective-permute-start | bytes 1966088 | tf_op jit(solution)/shard_map/ppermute | solution.py:299
  13.1 12.2 %collective-permute-start.6 = (f32[2,4,8,2432]{3,2,1,0:T(8,128)S(1)}, f32[2,4,8,2432]{3,2,1,0:T(8,128)S(1)}, u32[]{:S(2)}, u32[]{:S(2)}) collective-permute-start(f32[2,4,8,2432]{3,2,1,0:T(8,128)S(1)} %pad_maximum_fusion.3), channel_id=1, source_target_pairs={{0,12},{1,13},{2,14},{3,15},{4,8},{5,9},{6,10},{7,11},{8,4},{9,5},... | collective-permute-start | bytes 1867784 | tf_op jit(solution)/shard_map/ppermute | solution.py:299
  20.9 28.2 %copy-start.3 = (s32[2,16]{1,0:T(2,128)S(1)}, s32[2,16]{1,0:T(2,128)}, u32[]{:S(2)}) copy-start(s32[2,16]{1,0:T(2,128)} %constant.24.clone) | copy-start | bytes 388
  20.9 28.1 %copy-start.4 = (s32[2,16]{1,0:T(2,128)S(1)}, s32[2,16]{1,0:T(2,128)}, u32[]{:S(2)}) copy-start(s32[2,16]{1,0:T(2,128)} %constant.25.clone) | copy-start | bytes 388
  21.0 26.1 %collective-permute-start.2 = (f32[4,4,8,2560]{3,2,1,0:T(8,128)S(1)}, f32[4,4,8,2560]{3,2,1,0:T(8,128)}, u32[]{:S(2)}, u32[]{:S(2)}) collective-permute-start(f32[4,4,8,2560]{3,2,1,0:T(8,128)S(1)} %pad_maximum_fusion.refs_1_.refs_4_), channel_id=1, source_target_pairs={{0,3},{1,2},{2,1},{3,0},{4,7},{5,6},{6,5},{7,4},{8,11},{9,10},{10,... | collective-permute-start | bytes 3932168 | tf_op jit(solution)/shard_map/ppermute | solution.py:299
  25.5 18.1 %collective-permute-start.7 = (f32[4,4,8,2432]{3,2,1,0:T(8,128)S(1)}, f32[4,4,8,2432]{3,2,1,0:T(8,128)}, u32[]{:S(2)}, u32[]{:S(2)}) collective-permute-start(f32[4,4,8,2432]{3,2,1,0:T(8,128)S(1)} %pad_maximum_fusion.1.refs_1_.refs_0_), channel_id=1, source_target_pairs={{0,1},{1,0},{2,3},{3,2},{4,5},{5,4},{6,7},{7,6},{8,9},{9,8},{10,11... | collective-permute-start | bytes 3735560 | tf_op jit(solution)/shard_map/ppermute | solution.py:299
  27.7 32.3 %collective-permute-start.3 = (f32[4,4,8,2560]{3,2,1,0:T(8,128)S(1)}, f32[4,4,8,2560]{3,2,1,0:T(8,128)}, u32[]{:S(2)}, u32[]{:S(2)}) collective-permute-start(f32[4,4,8,2560]{3,2,1,0:T(8,128)S(1)} %pad_maximum_fusion.refs_1_.refs_4_), channel_id=1, source_target_pairs={{0,1},{1,0},{2,3},{3,2},{4,5},{5,4},{6,7},{7,6},{8,9},{9,8},{10,11... | collective-permute-start | bytes 3932168 | tf_op jit(solution)/shard_map/ppermute | solution.py:299
  30.8 25.4 %collective-permute-start.8 = (f32[4,4,8,2432]{3,2,1,0:T(8,128)S(1)}, f32[4,4,8,2432]{3,2,1,0:T(8,128)}, u32[]{:S(2)}, u32[]{:S(2)}) collective-permute-start(f32[4,4,8,2432]{3,2,1,0:T(8,128)S(1)} %pad_maximum_fusion.1.refs_1_.refs_0_), channel_id=1, source_target_pairs={{0,3},{1,2},{2,1},{3,0},{4,7},{5,6},{6,5},{7,4},{8,11},{9,10},{10,... | collective-permute-start | bytes 3735560 | tf_op jit(solution)/shard_map/ppermute | solution.py:299
  43.5 26.0 %collective-permute-start.9 = (f32[4,4,8,2432]{3,2,1,0:T(8,128)}, f32[4,4,8,2432]{3,2,1,0:T(8,128)}, u32[]{:S(2)}, u32[]{:S(2)}) collective-permute-start(f32[4,4,8,2432]{3,2,1,0:T(8,128)} %collective-permute-done.7.refs_2_.refs_1_), channel_id=1, source_target_pairs={{0,3},{1,2},{2,1},{3,0},{4,7},{5,6},{6,5},{7,4},{8,11},{9,10},{10,... | collective-permute-start | bytes 3735560 | tf_op jit(solution)/shard_map/ppermute | solution.py:299
  47.1 27.0 %collective-permute-start.4 = (f32[4,4,8,2560]{3,2,1,0:T(8,128)}, f32[4,4,8,2560]{3,2,1,0:T(8,128)}, u32[]{:S(2)}, u32[]{:S(2)}) collective-permute-start(f32[4,4,8,2560]{3,2,1,0:T(8,128)} %collective-permute-done.2.refs_2_.refs_5_), channel_id=1, source_target_pairs={{0,1},{1,0},{2,3},{3,2},{4,5},{5,4},{6,7},{7,6},{8,9},{9,8},{10,11... | collective-permute-start | bytes 3932168 | tf_op jit(solution)/shard_map/ppermute | solution.py:299
  58.9 1.0 copy-start.1
  60.0 9.5 %copy-start = (f32[96,4864]{1,0:T(8,128)S(1)}, f32[96,4864]{1,0:T(8,128)}, u32[]{:S(2)}) copy-start(f32[96,4864]{1,0:T(8,128)} %eig_ref.1) | copy-start | bytes 5603332
  79.1 7.4 %collective-permute-start.10 = (f32[384,128]{1,0:T(8,128)S(1)}, f32[384,128]{1,0:T(8,128)S(1)}, u32[]{:S(2)}, u32[]{:S(2)}) collective-permute-start(f32[384,128]{1,0:T(8,128)S(1)} %get-tuple-element.17), channel_id=1, source_target_pairs={{0,16},{16,0},{32,48},{48,32},{64,80},{80,64},{96,112},{112,96},{1... | collective-permute-start | bytes 589832 | tf_op jit(solution)/shard_map/ppermute | solution.py:315
  118.1 31.0 %copy-start.2 = (f32[4,4,8,2432]{3,2,1,0:T(8,128)S(1)}, f32[4,4,8,2432]{3,2,1,0:T(8,128)}, u32[]{:S(2)}) copy-start(f32[4,4,8,2432]{3,2,1,0:T(8,128)} %copy-done.1) | copy-start | bytes 3735556
  139.3 7.6 %collective-permute-start.11 = (f32[384,128]{1,0:T(8,128)S(1)}, f32[384,128]{1,0:T(8,128)S(1)}, u32[]{:S(2)}, u32[]{:S(2)}) collective-permute-start(f32[384,128]{1,0:T(8,128)S(1)} %bitcast.8), channel_id=1, source_target_pairs={{16,28},{17,29},{18,30},{19,31},{20,24},{21,25},{22,26},{23,27},{2... | collective-permute-start | bytes 589832 | tf_op jit(solution)/shard_map/ppermute | solution.py:323
